TPU v7x, 256 devices: a whole 4x4x8 slice. The times are simulated.
256 devices in a mesh: lat: 8 (over x, y_lo), lon: 32 (over y_hi, z, core).
Axes of the slice: x: 4, y: 4 (y_hi: 2, y_lo: 2; y = y_hi * 2 + y_lo), z: 8, core: 2. Of those that a mesh axis runs over, the one named last changes fastest.
Arguments:
- fields: float32 [32, 1024, 1024], P('lat', 'lon'), as said below
- row_points: int32 [32], replicated, may hold values from 32 to 1024, as said below
- band_mask: int32 [8, 4], replicated, may hold values 0 or 1
- norm_gain: float32 [1024], replicated, may hold values from 0.1 to 1.9
- w_query: bfloat16 [1024, 1024], replicated, as said below
- w_key: bfloat16 [1024, 1024], replicated
- w_value: bfloat16 [1024, 1024], replicated, may hold values from -0.1875 to 0.1875
- w_out: bfloat16 [1024, 1024], replicated, may hold values from -0.1875 to 0.1875
Outputs:
- block_out: float32 [32, 1024, 1024], P('lat', 'lon')
Inputs may be any that keep to these rules, and one draw needn't show every extreme that they name: fields: entries of order one to ten in magnitude, within -24 and 24. `row_points`: row r holds between half of its bound and its bound, where the bound is max(32, 1024 * (r + 1) // 32), and never fewer than 32; the last row holds 1024. `w_query`: entries of order 3 * 1024 ** -0.5.
All inputs are finite; a program needn't handle non-finite values.
Results may differ from a plain program's by a relative error of at most 0.0052.
Values may be sent and summed in bfloat16 or wider, within the bound.
No kernel may reach another device: no remote copies, remote signals or barrier semaphores. Data moves between devices by JAX's collectives and lax.ppermute only.
A program may use at most 128 MiB of HBM per device.

v0:
```python
import jax
import jax.numpy as jnp
from jax import lax
from jax.sharding import PartitionSpec as P

HEADS = 16
HEAD_DIM = 64
AXIAL_HEADS = 8
REACH = 2


EPS = 1e-05
NEG_FILL = -1e30


def passed_along(value, axis, steps):
    count = lax.axis_size(axis)
    first, last = (max(0, -steps), min(count, count - steps))
    return lax.ppermute(value, axis, [(source, source + steps) for source in range(first, last)])


def query_blocks(length):
    blocks = 1
    while length // blocks > 1024 and length % (blocks * 2) == 0:
        blocks = blocks * 2
    return blocks


def band_counts(row_points, lat_band, tile_rows):
    return lax.dynamic_slice_in_dim(row_points, lat_band * tile_rows, tile_rows)


def on_device(fields, row_points, band_mask, norm_gain, w_query, w_key, w_value, w_out):
    tile_rows, tile_points, model_width = fields.shape
    lat_count = lax.axis_size("lat")
    lon_count = lax.axis_size("lon")
    lat_index = lax.axis_index("lat")
    lon_index = lax.axis_index("lon")
    axial_width = AXIAL_HEADS * HEAD_DIM
    band_heads = HEADS - AXIAL_HEADS
    score_scale = HEAD_DIM ** (-0.5)
    token_count = tile_rows * tile_points
    slot_iota = jnp.arange(tile_points, dtype=jnp.int32)
    own_counts = band_counts(row_points, lat_index, tile_rows)
    own_lives = own_counts // lon_count + (lon_index < own_counts % lon_count).astype(jnp.int32)
    own_live = slot_iota[None, :] < own_lives[:, None]
    row_mean = jnp.mean(fields, axis=-1, keepdims=True)
    centred = fields - row_mean
    row_var = jnp.mean(centred * centred, axis=-1, keepdims=True)
    normed = (
        (centred * lax.rsqrt(row_var + EPS) * norm_gain)
        .astype(jnp.bfloat16)
        .reshape(token_count, model_width)
    )
    queries = jnp.dot(normed, w_query, preferred_element_type=jnp.float32).astype(jnp.bfloat16)
    key_heads = jnp.dot(normed, w_key, preferred_element_type=jnp.float32).astype(jnp.bfloat16)
    value_heads = jnp.dot(normed, w_value, preferred_element_type=jnp.float32).astype(jnp.bfloat16)
    axial_key = key_heads[:, :axial_width].reshape(tile_rows, tile_points, axial_width)
    axial_value = value_heads[:, :axial_width].reshape(tile_rows, tile_points, axial_width)
    axial_query = queries[:, :axial_width].reshape(tile_rows, tile_points, AXIAL_HEADS, HEAD_DIM)
    start_max = jnp.full((tile_rows, tile_points, AXIAL_HEADS), NEG_FILL, jnp.float32)
    weight_sum = jnp.zeros_like(start_max)
    part_key = lax.all_gather(axial_key, "lon", axis=1, tiled=True)
    part_value = lax.all_gather(axial_value, "lon", axis=1, tiled=True)
    slot_count = part_key.shape[1]
    slot_ids = jnp.arange(slot_count, dtype=jnp.int32)
    owner_ids = slot_ids // tile_points
    within = slot_ids % tile_points
    live_counts = own_counts[:, None] // lon_count + (
        owner_ids[None, :] < own_counts[:, None] % lon_count
    ).astype(jnp.int32)
    mask_wide = (within[None, :] < live_counts)[:, None, None, :]
    part_key = part_key.reshape(tile_rows, slot_count, AXIAL_HEADS, HEAD_DIM)
    part_value = part_value.reshape(tile_rows, slot_count, AXIAL_HEADS, HEAD_DIM)
    scores = (
        jnp.einsum("rphd,rkhd->rphk", axial_query, part_key, preferred_element_type=jnp.float32)
        * score_scale
    )
    new_max = jnp.maximum(start_max, jnp.max(jnp.where(mask_wide, scores, NEG_FILL), axis=-1))
    weights = jnp.where(mask_wide, jnp.exp(scores - new_max[..., None]), 0.0)
    weight_sum = jnp.sum(weights, axis=-1)
    accumulated = jnp.einsum(
        "rphk,rkhd->rphd",
        weights.astype(jnp.bfloat16),
        part_value,
        preferred_element_type=jnp.float32,
    )
    axial_out = (
        (accumulated / weight_sum[..., None]).astype(jnp.bfloat16).reshape(token_count, axial_width)
    )
    band_query = queries[:, axial_width:].reshape(token_count, band_heads, HEAD_DIM)
    band_key = key_heads[:, axial_width:]
    band_value = value_heads[:, axial_width:]
    key_list = [band_key]
    value_list = [band_value]
    live_list = [own_live.reshape(token_count)]
    for offset in [shift_by for shift_by in range(-REACH, REACH + 1) if shift_by != 0]:
        moved_tiles = passed_along((band_key, band_value), "lat", -offset)
        key_list.append(moved_tiles[0])
        value_list.append(moved_tiles[1])
        source = lat_index + offset
        inside = (source >= 0) & (source < lat_count)
        column = offset + REACH if offset < 0 else offset + REACH - 1
        allowed = inside & (band_mask[lat_index, column] == 1)
        counts = band_counts(row_points, jnp.clip(source, 0, lat_count - 1), tile_rows)
        neighbour_live_counts = counts // lon_count + (lon_index < counts % lon_count).astype(
            jnp.int32
        )
        live_list.append(
            ((slot_iota[None, :] < neighbour_live_counts[:, None]) & allowed).reshape(token_count)
        )
    all_keys = jnp.concatenate(key_list, axis=0).reshape(-1, band_heads, HEAD_DIM)
    all_values = jnp.concatenate(value_list, axis=0).reshape(-1, band_heads, HEAD_DIM)
    all_live = jnp.concatenate(live_list, axis=0)[None, None, :]
    blocks = query_blocks(token_count)
    block_len = token_count // blocks
    query_split = band_query.reshape(blocks, block_len, band_heads, HEAD_DIM)

    def band_block(block_query):
        scores = (
            jnp.einsum("qhd,khd->hqk", block_query, all_keys, preferred_element_type=jnp.float32)
            * score_scale
        )
        scores = jnp.where(all_live, scores, -jnp.inf)
        block_max = jnp.max(scores, axis=-1, keepdims=True)
        weights = jnp.exp(scores - block_max)
        weight_sum = jnp.sum(weights, axis=-1)
        summed = jnp.einsum(
            "hqk,khd->qhd",
            weights.astype(jnp.bfloat16),
            all_values,
            preferred_element_type=jnp.float32,
        )
        return summed / jnp.transpose(weight_sum)[:, :, None]

    band_out = (
        lax.map(band_block, query_split)
        .reshape(token_count, band_heads * HEAD_DIM)
        .astype(jnp.bfloat16)
    )
    mixed_heads = jnp.concatenate([axial_out, band_out], axis=1)
    projected = jnp.dot(mixed_heads, w_out, preferred_element_type=jnp.float32).reshape(
        tile_rows, tile_points, model_width
    )
    return jnp.where(own_live[:, :, None], fields + projected, 0.0)


def solution(mesh):
    in_specs = (P("lat", "lon", None), P(), P(), P(), P(), P(), P(), P())
    out_specs = P("lat", "lon", None)
    return jax.shard_map(
        on_device, mesh=mesh, in_specs=in_specs, out_specs=out_specs, check_vma=False
    )
```

profile of v0, /device:TPU:1, one launch (start us, length us, event | category | flops | bytes accessed | tf_op | source)
XLA Modules:
  0.0 210.2 jit_solution(13144438233445052328)
XLA Ops:
  6.5 1.3 reduce_sum.37
  7.8 1.2 multiply_reduce_fusion
  9.1 1.2 multiply_convert_fusion
  10.3 0.4 convolution_convert_fusion.1
  10.8 0.7 fusion.61
  11.5 0.0 all-gather.5.cloned.1.call-update
  11.6 0.0 all-gather.3.cloned.1.call-start
  11.6 2.0 convolution_convert_fusion.2
  13.6 0.7 fusion.62
  14.4 4.6 %collective-permute-start = (bf16[128,512]{1,0:T(8,128)(2,1)S(1)}, bf16[128,512]{1,0:T(8,128)(2,1)}, u32[]{:S(2)}, u32[]{:S(2)}) collective-permute-start(bf16[128,512]{1,0:T(8,128)(2,1)S(1)} %get-tuple-element.34), channel_id=1, source_target_pairs={{0,64},{32,96},{64,128},{96,160},{128,192},{160,224},{1,65},{33,97... | collective-permute-start | bytes 393224 | tf_op jit(solution)/shard_map/ppermute | solution.py:19
  19.0 3.2 %collective-permute-start.1 = (bf16[128,512]{1,0:T(8,128)(2,1)S(1)}, bf16[128,512]{1,0:T(8,128)(2,1)S(1)}, u32[]{:S(2)}, u32[]{:S(2)}) collective-permute-start(bf16[128,512]{1,0:T(8,128)(2,1)S(1)} %get-tuple-element.34), channel_id=1, source_target_pairs={{0,32},{32,64},{64,96},{96,128},{128,160},{160,192},{192,224},{1,3... | collective-permute-start | bytes 393224 | tf_op jit(solution)/shard_map/ppermute | solution.py:19
  22.2 1.3 collective-permute-start.2
  23.5 1.3 collective-permute-start.3
  24.8 4.8 %collective-permute-start.4 = (bf16[128,512]{1,0:T(8,128)(2,1)S(1)}, bf16[128,512]{1,0:T(8,128)(2,1)S(1)}, u32[]{:S(2)}, u32[]{:S(2)}) collective-permute-start(bf16[128,512]{1,0:T(8,128)(2,1)S(1)} %get-tuple-element.31), channel_id=1, source_target_pairs={{0,64},{32,96},{64,128},{96,160},{128,192},{160,224},{1,65},{33,97... | collective-permute-start | bytes 393224 | tf_op jit(solution)/shard_map/ppermute | solution.py:19
  29.7 0.6 constant_dynamic-slice_fusion
  32.7 0.1 and_select_fusion.8
  32.8 0.1 fusion.50
  32.9 0.1 fusion.46
  32.9 0.1 fusion.48
  33.0 0.1 add_compare_fusion
  33.1 2.0 convolution_convert_fusion
  35.2 0.1 iota_compare_fusion.4
  35.3 0.6 lt.211
  35.9 0.6 and.151
  36.5 0.6 and.158
  37.0 0.6 and.165
  37.6 0.1 and.172
  37.7 0.1 copy.20
  37.9 0.2 reshape.214
  38.1 0.8 dynamic-update-slice.5
  38.9 0.8 dynamic-update-slice.6
  39.7 0.7 dynamic-update-slice.7
  40.4 0.8 dynamic-update-slice.8
  41.2 0.2 dynamic-update-slice.9
  41.4 3.2 %collective-permute-start.5 = (bf16[128,512]{1,0:T(8,128)(2,1)S(1)}, bf16[128,512]{1,0:T(8,128)(2,1)S(1)}, u32[]{:S(2)}, u32[]{:S(2)}) collective-permute-start(bf16[128,512]{1,0:T(8,128)(2,1)S(1)} %get-tuple-element.31), channel_id=1, source_target_pairs={{0,32},{32,64},{64,96},{96,128},{128,160},{160,192},{192,224},{1,3... | collective-permute-start | bytes 393224 | tf_op jit(solution)/shard_map/ppermute | solution.py:19
  44.6 1.6 constant_dynamic-update-slice_fusion.3
  46.1 1.3 collective-permute-start.6
  47.4 0.7 constant_dynamic-update-slice_fusion.2
  48.1 1.3 collective-permute-start.7
  49.4 0.7 constant_dynamic-update-slice_fusion.1
  50.0 0.7 constant_dynamic-update-slice_fusion
  50.7 0.7 constant_dynamic-update-slice_fusion.8
  51.4 0.7 constant_dynamic-update-slice_fusion.7
  52.0 2.1 %copy.19 = bf16[640,512]{0,1:T(8,128)(2,1)} copy(bf16[640,512]{1,0:T(8,128)(2,1)} %constant_dynamic-update-slice_fusion) | data formatting | bytes 1310720 | tf_op jit(solution)/shard_map/concatenate | solution.py:113
  54.2 0.7 constant_dynamic-update-slice_fusion.6
  54.8 2.2 %collective-permute-done.7 = bf16[128,512]{1,0:T(8,128)(2,1)S(1)} collective-permute-done((bf16[128,512]{1,0:T(8,128)(2,1)S(1)}, bf16[128,512]{1,0:T(8,128)(2,1)S(1)}, u32[]{:S(2)}, u32[]{:S(2)}) %collective-permute-start.7) | collective-permute-done | bytes 131104 | tf_op jit(solution)/shard_map/ppermute | solution.py:19
  57.0 0.7 constant_dynamic-update-slice_fusion.5
  57.7 1.4 copy.21
  59.1 0.6 fusion.5
  59.8 0.7 fusion.12
  60.5 0.8 fusion.26
  61.3 0.1 copy.22
  61.4 41.3 %all-gather.5.cloned.1.call-done = bf16[4,1024,512]{2,1,0:T(8,128)(2,1)} async-done(((bf16[4,32,512]{2,1,0:T(8,128)(2,1)}), bf16[4,1024,512]{2,1,0:T(8,128)(2,1)}) %all-gather.5.cloned.1.call-update) | async-done | bytes 4194320 | tf_op jit(solution)/shard_map/all_gather | solution.py:63
  102.6 6.3 %copy.16 = bf16[4,1024,512]{1,2,0:T(8,128)(2,1)} copy(bf16[4,1024,512]{2,1,0:T(8,128)(2,1)} %all-gather.5.cloned.1.call-done) | data formatting | bytes 8388608 | tf_op jit(solution)/shard_map/all_gather | solution.py:63
  109.0 3.2 %fusion = (f32[4,32,8]{1,2,0:T(8,128)S(1)}, f32[4,8,1024,32]{2,3,1,0:T(8,128)S(1)}) fusion(pred[4,1024]{1,0:T(4,128)(4,1)S(1)} %add_compare_fusion, bf16[4,1024,8,64]{1,3,2,0:T(8,128)(2,1)} %bitcast.61, bf16[4,32,8,64]{3,2,1,0:T(8,128)(2,1)S(1)} %reshape.214), kind=kOutput, calls=%fused_computation.2 | convolution fusion | flops 137362432 | bytes 8527872 | tf_op jit(solution)/shard_map/rphd,rkhd->rphk/dot_general | solution.py:76
  112.2 2.0 copy-done.1
  114.1 1.1 fusion.3
  115.2 73.8 %all-gather.3.cloned.1.call-done = bf16[4,1024,512]{2,1,0:T(8,128)(2,1)} async-done(((bf16[4,32,512]{2,1,0:T(8,128)(2,1)}), bf16[4,1024,512]{2,1,0:T(8,128)(2,1)}) %all-gather.3.cloned.1.call-update) | async-done | bytes 4194320 | tf_op jit(solution)/shard_map/all_gather | solution.py:64
  189.0 6.3 %copy.15 = bf16[4,1024,512]{1,2,0:T(8,128)(2,1)} copy(bf16[4,1024,512]{2,1,0:T(8,128)(2,1)} %all-gather.3.cloned.1.call-done) | data formatting | bytes 8388608 | tf_op jit(solution)/shard_map/all_gather | solution.py:64
  195.3 4.8 %fusion.32 = bf16[4,32,8,64]{3,1,2,0:T(8,128)(2,1)S(1)} fusion(bf16[4,1024,8,64]{1,3,2,0:T(8,128)(2,1)} %bitcast.65, f32[4,8,1024,32]{2,3,1,0:T(8,128)} %copy-done.1, f32[4,32,8]{1,2,0:T(8,128)S(1)} %broadcast_maximum_fusion, pred[4,1024]{1,0:T(4,128)(4,1)S(1)} %add_compare_fusion, f32[4,32,8]{1,2,0:T(8,128)S(1)} %fusion.3), kind=kOutput, calls=%fused_computation.27 | convolution fusion | flops 138543104 | bytes 8531968 | tf_op jit(solution)/shard_map/rphk,rkhd->rphd/dot_general | solution.py:82
  200.1 0.1 copy.18
  200.2 0.2 reshape.215
  200.4 2.0 fusion.35
  202.5 0.9 add_select_fusion
  (26 shorter events, 0.1 us)
Async XLA Ops:
  6.5 3.8 %copy-start = (bf16[1024,1024]{1,0:T(8,128)(2,1)S(1)}, bf16[1024,1024]{1,0:T(8,128)(2,1)}, u32[]{:S(2)}) copy-start(bf16[1024,1024]{1,0:T(8,128)(2,1)} %param.13) | copy-start | bytes 6291460
  6.5 96.1 %all-gather.5.cloned.1.call-start = ((), (), s32[]{:S(2)}) async-start(), calls=%async_computation.1 | async-start | bytes 4325376 | tf_op jit(solution)/shard_map/all_gather | solution.py:63
  10.8 18.9 %copy-start.5 = (s32[8,4]{0,1:T(4,128)S(1)}, s32[8,4]{0,1:T(4,128)}, u32[]{:S(2)}) copy-start(s32[8,4]{0,1:T(4,128)} %param.10) | copy-start | bytes 388
  10.8 21.9 %copy-start.4 = (s32[32]{0:T(128)S(1)}, s32[32]{0:T(128)}, u32[]{:S(2)}) copy-start(s32[32]{0:T(128)} %param.9) | copy-start | bytes 388
  11.6 177.4 %all-gather.3.cloned.1.call-start = ((), (), s32[]{:S(2)}) async-start(), calls=%async_computation | async-start | bytes 4325376 | tf_op jit(solution)/shard_map/all_gather | solution.py:64
  14.4 27.0 %collective-permute-start = (bf16[128,512]{1,0:T(8,128)(2,1)S(1)}, bf16[128,512]{1,0:T(8,128)(2,1)}, u32[]{:S(2)}, u32[]{:S(2)}) collective-permute-start(bf16[128,512]{1,0:T(8,128)(2,1)S(1)} %get-tuple-element.34), channel_id=1, source_target_pairs={{0,64},{32,96},{64,128},{96,160},{128,192},{160,224},{1,65},{33,97... | collective-permute-start | bytes 393224 | tf_op jit(solution)/shard_map/ppermute | solution.py:19
  19.0 27.1 %collective-permute-start.1 = (bf16[128,512]{1,0:T(8,128)(2,1)S(1)}, bf16[128,512]{1,0:T(8,128)(2,1)S(1)}, u32[]{:S(2)}, u32[]{:S(2)}) collective-permute-start(bf16[128,512]{1,0:T(8,128)(2,1)S(1)} %get-tuple-element.34), channel_id=1, source_target_pairs={{0,32},{32,64},{64,96},{96,128},{128,160},{160,192},{192,224},{1,3... | collective-permute-start | bytes 393224 | tf_op jit(solution)/shard_map/ppermute | solution.py:19
  22.2 25.9 %collective-permute-start.2 = (bf16[128,512]{1,0:T(8,128)(2,1)S(1)}, bf16[128,512]{1,0:T(8,128)(2,1)S(1)}, u32[]{:S(2)}, u32[]{:S(2)}) collective-permute-start(bf16[128,512]{1,0:T(8,128)(2,1)S(1)} %get-tuple-element.34), channel_id=1, source_target_pairs={{32,0},{64,32},{96,64},{128,96},{160,128},{192,160},{224,192},{33,... | collective-permute-start | bytes 393224 | tf_op jit(solution)/shard_map/ppermute | solution.py:19
  23.5 26.5 %collective-permute-start.3 = (bf16[128,512]{1,0:T(8,128)(2,1)S(1)}, bf16[128,512]{1,0:T(8,128)(2,1)S(1)}, u32[]{:S(2)}, u32[]{:S(2)}) collective-permute-start(bf16[128,512]{1,0:T(8,128)(2,1)S(1)} %get-tuple-element.34), channel_id=1, source_target_pairs={{64,0},{96,32},{128,64},{160,96},{192,128},{224,160},{65,1},{97,33... | collective-permute-start | bytes 393224 | tf_op jit(solution)/shard_map/ppermute | solution.py:19
  24.8 25.9 %collective-permute-start.4 = (bf16[128,512]{1,0:T(8,128)(2,1)S(1)}, bf16[128,512]{1,0:T(8,128)(2,1)S(1)}, u32[]{:S(2)}, u32[]{:S(2)}) collective-permute-start(bf16[128,512]{1,0:T(8,128)(2,1)S(1)} %get-tuple-element.31), channel_id=1, source_target_pairs={{0,64},{32,96},{64,128},{96,160},{128,192},{160,224},{1,65},{33,97... | collective-permute-start | bytes 393224 | tf_op jit(solution)/shard_map/ppermute | solution.py:19
  41.4 10.0 %collective-permute-start.5 = (bf16[128,512]{1,0:T(8,128)(2,1)S(1)}, bf16[128,512]{1,0:T(8,128)(2,1)S(1)}, u32[]{:S(2)}, u32[]{:S(2)}) collective-permute-start(bf16[128,512]{1,0:T(8,128)(2,1)S(1)} %get-tuple-element.31), channel_id=1, source_target_pairs={{0,32},{32,64},{64,96},{96,128},{128,160},{160,192},{192,224},{1,3... | collective-permute-start | bytes 393224 | tf_op jit(solution)/shard_map/ppermute | solution.py:19
  46.1 8.0 %collective-permute-start.6 = (bf16[128,512]{1,0:T(8,128)(2,1)S(1)}, bf16[128,512]{1,0:T(8,128)(2,1)S(1)}, u32[]{:S(2)}, u32[]{:S(2)}) collective-permute-start(bf16[128,512]{1,0:T(8,128)(2,1)S(1)} %get-tuple-element.31), channel_id=1, source_target_pairs={{32,0},{64,32},{96,64},{128,96},{160,128},{192,160},{224,192},{33,... | collective-permute-start | bytes 393224 | tf_op jit(solution)/shard_map/ppermute | solution.py:19
  48.1 9.0 %collective-permute-start.7 = (bf16[128,512]{1,0:T(8,128)(2,1)S(1)}, bf16[128,512]{1,0:T(8,128)(2,1)S(1)}, u32[]{:S(2)}, u32[]{:S(2)}) collective-permute-start(bf16[128,512]{1,0:T(8,128)(2,1)S(1)} %get-tuple-element.31), channel_id=1, source_target_pairs={{64,0},{96,32},{128,64},{160,96},{192,128},{224,160},{65,1},{97,33... | collective-permute-start | bytes 393224 | tf_op jit(solution)/shard_map/ppermute | solution.py:19
  59.1 1.4 copy-start.3
  112.1 2.0 copy-start.1
  200.1 2.4 %copy-start.2 = (f32[4,32,1024]{2,1,0:T(8,128)S(1)}, f32[4,32,1024]{2,1,0:T(8,128)}, u32[]{:S(2)}) copy-start(f32[4,32,1024]{2,1,0:T(8,128)} %param.8) | copy-start | bytes 1572868
Sparse Core Ops, SparseCore 0:
  11.7 90.9 all-gather.4
  105.5 83.4 all-gather.2
where the time goes:
time: 211 us; the launch traced here: 210 us
  waiting for transfers between devices  117 us (55%)
  local copies, waits for them, and re-layouts  33 us (16%)
  starting transfers between devices  21 us (10%)
  between operations  16.1 us (8%)
  matrix products  15.9 us (8%)
  other arithmetic  6.88 us (3%)
    all_gather x1, waiting for transfers between devices, on_device(): part_value = lax.all_gather(axial_value, 'lon', axis=1, tiled=True)  73.8 us
    all_gather x1, waiting for transfers between devices, on_device(): part_key = lax.all_gather(axial_key, 'lon', axis=1, tiled=True)  41.3 us
    ppermute x8, starting transfers between devices, passed_along(): lax.ppermute(value, axis, [(source, source + steps) for source in range(f...  20.9 us
    unnamed x22, local copies, waits for them, and re-layouts  9.98 us
    all_gather x1, local copies, waits for them, and re-layouts, on_device(): part_key = lax.all_gather(axial_key, 'lon', axis=1, tiled=True)  6.33 us
    all_gather x1, local copies, waits for them, and re-layouts, on_device(): part_value = lax.all_gather(axial_value, 'lon', axis=1, tiled=True)  6.32 us
    dot_general x1, matrix products, on_device(): jnp.einsum('rphk,rkhd->rphd', weights.astype(jnp.bfloat16), part_value, p...  4.78 us
  transfers between devices with their start and end apart: 10, of which 3 were waited for; matrix products, arithmetic and copies ran while one was open for 16% of the time, Pallas kernels for 0%

commit v1 on v0

v1 whole, which is shorter than its diff:
```python
import functools

import jax
import jax.numpy as jnp
from jax import lax
from jax.experimental import pallas as pl
from jax.experimental.pallas import tpu as pltpu
from jax.sharding import PartitionSpec as P

HEADS = 16
HEAD_DIM = 64
AXIAL_HEADS = 8
REACH = 2
EPS = 1e-05
DEAD = -1e30
PAIR = 2 * HEAD_DIM
SCALE = HEAD_DIM**-0.5
OFFSETS = (-2, -1, 1, 2)

VMEM = pl.BlockSpec(memory_space=pltpu.VMEM)
SMEM = pl.BlockSpec(memory_space=pltpu.SMEM)
PARAMS = pltpu.CompilerParams(vmem_limit_bytes=48 * 1024 * 1024)


def dot(a, b):
    return jnp.dot(a, b, preferred_element_type=jnp.float32)


def dot_t(a, b):
    return lax.dot_general(a, b, (((1,), (1,)), ((), ())), preferred_element_type=jnp.float32)


def half_roll(value):
    return pltpu.roll(value, HEAD_DIM, 1)


def low_half(shape):
    return lax.broadcasted_iota(jnp.int32, shape, 1) < HEAD_DIM


def live_count(points, tile, tiles):
    return points // tiles + (tile < points % tiles).astype(jnp.int32)


def norm_kernel(fields_ref, gain_ref, out_ref):
    rows, slots, width = fields_ref.shape
    values = fields_ref[...].reshape(rows * slots, width)
    mean = jnp.mean(values, axis=-1, keepdims=True)
    centred = values - mean
    var = jnp.mean(centred * centred, axis=-1, keepdims=True)
    out_ref[...] = (centred * lax.rsqrt(var + EPS) * gain_ref[...]).astype(jnp.bfloat16)


def axial_project_kernel(lon_count, own_ref, peer_ref, wq_ref, wk_ref, wv_ref, out_ref):
    core = lax.rem(lax.axis_index("lon"), 2)
    tokens = own_ref.shape[0]
    slots = out_ref.shape[1] // 3
    rows = tokens // slots
    heads = AXIAL_HEADS // 2
    width = heads * HEAD_DIM
    columns = pl.ds(pl.multiple_of(core * width, width), width)
    both = jnp.concatenate([own_ref[...], peer_ref[...]], axis=0)
    query = dot(both, wq_ref[:, columns])
    key = dot(both, wk_ref[:, columns])
    value = dot(both, wv_ref[:, columns])
    low = low_half((2 * tokens, PAIR))
    low_v = low_half((tokens, PAIR))
    for pair in range(heads // 2):
        span = slice(pair * PAIR, (pair + 1) * PAIR)
        q, k = query[:, span], key[:, span]
        v_own, v_peer = value[:tokens, span], value[tokens:, span]
        qk = (jnp.where(low, q, half_roll(k)), jnp.where(low, half_roll(q), k))
        v = (jnp.where(low_v, v_own, half_roll(v_peer)), jnp.where(low_v, half_roll(v_own), v_peer))
        for side in range(2):
            qk_side = qk[side].astype(jnp.bfloat16)
            v_side = v[side].astype(jnp.bfloat16)
            for row in range(rows):
                item = row * heads + pair * 2 + side
                part = slice(row * slots, (row + 1) * slots)
                part_peer = slice(tokens + row * slots, tokens + (row + 1) * slots)
                out_ref[item, 0:slots, :] = qk_side[part]
                out_ref[item, slots : 2 * slots, :] = qk_side[part_peer]
                out_ref[item, 2 * slots : 3 * slots, :] = v_side[part]


def axial_kernel(lon_count, points_ref, in_ref, out_ref):
    lon = lax.axis_index("lon")
    core = lax.rem(lon, 2)
    chip = lon // 2
    chips, third, _ = in_ref.shape
    slots = third // 3
    rows = chips // (AXIAL_HEADS // 2)
    points = points_ref[lax.axis_index("lat") * rows + chip // (AXIAL_HEADS // 2)]
    keys = chips * 2 * slots
    query_key = in_ref[:, : 2 * slots, :].astype(jnp.float32).reshape(keys, PAIR)
    lane = lax.broadcasted_iota(jnp.int32, (keys, PAIR), 1)
    index = lax.broadcasted_iota(jnp.int32, (keys, PAIR), 0)
    half = lax.rem(index // slots, 2)
    tile = 2 * (index // (2 * slots)) + jnp.where(half == 0, core, 1 - core)
    live = lax.rem(index, slots) < points // lon_count + (tile < points % lon_count).astype(jnp.int32)
    bias = jnp.where(live, 0.0, DEAD)
    one_hot = (lane == HEAD_DIM).astype(jnp.float32)
    low = lane < HEAD_DIM
    query = jnp.where(low, query_key * SCALE, one_hot).astype(jnp.bfloat16)
    key = jnp.where(low, half_roll(query_key), one_hot * bias).astype(jnp.bfloat16)
    key = key.reshape(chips, 2, slots, PAIR)
    key_own = key[:, 0].reshape(chips * slots, PAIR)
    key_peer = key[:, 1].reshape(chips * slots, PAIR)
    value = in_ref[:, 2 * slots :, :].reshape(chips * slots, PAIR)
    block = 4 * 2 * slots
    low_block = low_half((block, PAIR))
    low_out = low_half((slots, PAIR))
    for step in range(keys // block):
        q = query[step * block : (step + 1) * block]
        s_own = dot_t(q, key_own)
        s_peer = dot_t(q, key_peer)
        peak = jnp.maximum(
            jnp.max(s_own, axis=-1, keepdims=True), jnp.max(s_peer, axis=-1, keepdims=True)
        )
        e_own = jnp.exp(s_own - peak)
        e_peer = jnp.exp(s_peer - peak)
        total = jnp.sum(e_own, axis=-1, keepdims=True) + jnp.sum(e_peer, axis=-1, keepdims=True)
        mixed = dot(e_own.astype(jnp.bfloat16), value)
        mixed_peer = half_roll(dot(e_peer.astype(jnp.bfloat16), value))
        mixed = jnp.where(low_block, mixed + mixed_peer, 0.0) / total
        for chip_of in range(4):
            first = mixed[chip_of * 2 * slots : chip_of * 2 * slots + slots]
            second = mixed[chip_of * 2 * slots + slots : (chip_of + 1) * 2 * slots]
            out_ref[step * 4 + chip_of] = jnp.where(low_out, first, half_roll(second)).astype(
                jnp.bfloat16
            )


def band_kernel(
    lat_count, lon_count, points_ref, mask_ref, own_ref, m2_ref, m1_ref, p1_ref, p2_ref,
    wq_ref, wk_ref, wv_ref, out_ref,
):
    lat = lax.axis_index("lat")
    lon = lax.axis_index("lon")
    tokens = own_ref.shape[0]
    slots = 32
    rows = tokens // slots
    first = AXIAL_HEADS * HEAD_DIM
    bands = (0,) + OFFSETS
    everything = jnp.concatenate(
        [own_ref[...], m2_ref[...], m1_ref[...], p1_ref[...], p2_ref[...]], axis=0
    )
    keys = everything.shape[0]
    key = dot(everything, wk_ref[:, first:]).astype(jnp.bfloat16)
    value = dot(everything, wv_ref[:, first:]).astype(jnp.bfloat16)
    query = dot(own_ref[...], wq_ref[:, first:]).astype(jnp.bfloat16)
    slot = lax.broadcasted_iota(jnp.int32, (slots, PAIR), 0)
    blocks = []
    for offset in bands:
        source = lat + offset
        held = jnp.clip(source, 0, lat_count - 1)
        if offset == 0:
            allowed = jnp.int32(1)
        else:
            column = offset + REACH if offset < 0 else offset + REACH - 1
            inside = (source >= 0) & (source < lat_count)
            allowed = jnp.where(inside & (mask_ref[lat, column] == 1), 1, 0)
        for row in range(rows):
            count = live_count(points_ref[held * rows + row], lon, lon_count) * allowed
            blocks.append(jnp.where(slot < count, 0.0, DEAD))
    bias = jnp.concatenate(blocks, axis=0).astype(jnp.bfloat16)
    lane_k = lax.broadcasted_iota(jnp.int32, (keys, PAIR), 1)
    lane_q = lax.broadcasted_iota(jnp.int32, (tokens, PAIR), 1)
    zero_k = jnp.zeros((keys, PAIR), jnp.bfloat16)
    low_o = lane_q < HEAD_DIM
    for pair in range((HEADS - AXIAL_HEADS) // 2):
        span = slice(pair * PAIR, (pair + 1) * PAIR)
        q, k, v = query[:, span] * jnp.bfloat16(SCALE), key[:, span], value[:, span]
        outs = []
        for side in range(2):
            spare = HEAD_DIM if side == 0 else 0
            mine_q = (lane_q < HEAD_DIM) if side == 0 else (lane_q >= HEAD_DIM)
            mine_k = (lane_k < HEAD_DIM) if side == 0 else (lane_k >= HEAD_DIM)
            q_side = jnp.where(mine_q, q, (lane_q == spare).astype(jnp.bfloat16))
            k_side = jnp.where(mine_k, k, jnp.where(lane_k == spare, bias, zero_k))
            scores = dot_t(q_side, k_side)
            peak = jnp.max(scores, axis=-1, keepdims=True)
            weights = jnp.exp(scores - peak)
            total = jnp.sum(weights, axis=-1, keepdims=True)
            outs.append(dot(weights.astype(jnp.bfloat16), v) / total)
        out_ref[:, span] = jnp.where(low_o, outs[0], outs[1]).astype(jnp.bfloat16)


def band_out_kernel(fields_ref, band_ref, w_ref, out_ref):
    rows, slots, width = fields_ref.shape
    first = AXIAL_HEADS * HEAD_DIM
    out_ref[...] = fields_ref[...].reshape(rows * slots, width) + dot(band_ref[...], w_ref[first:, :])


def finish_kernel(lon_count, points_ref, sum_ref, mine_ref, other_ref, w_ref, out_ref):
    lon = lax.axis_index("lon")
    core = lax.rem(lon, 2)
    rows, slots, width = out_ref.shape
    heads = AXIAL_HEADS // 2
    low = low_half((slots, PAIR))
    mine_rows, other_rows = [], []
    for row in range(rows):
        mine, other = [], []
        for pair in range(heads // 2):
            item = row * heads + pair * 2
            a = mine_ref[item].astype(jnp.float32)
            b = mine_ref[item + 1].astype(jnp.float32)
            mine.append(jnp.where(low, a, half_roll(b)))
            a = other_ref[item].astype(jnp.float32)
            b = other_ref[item + 1].astype(jnp.float32)
            other.append(jnp.where(low, half_roll(a), b))
        mine_rows.append(jnp.concatenate(mine, axis=1))
        other_rows.append(jnp.concatenate(other, axis=1))
    mine = jnp.concatenate(mine_rows, axis=0).astype(jnp.bfloat16)
    other = jnp.concatenate(other_rows, axis=0).astype(jnp.bfloat16)
    depth = heads * HEAD_DIM
    mine_w = w_ref[pl.ds(pl.multiple_of(core * depth, depth), depth), :]
    other_w = w_ref[pl.ds(pl.multiple_of((1 - core) * depth, depth), depth), :]
    result = sum_ref[...] + dot(mine, mine_w) + dot(other, other_w)
    slot = lax.broadcasted_iota(jnp.int32, (slots, width), 0)
    for row in range(rows):
        count = live_count(points_ref[lax.axis_index("lat") * rows + row], lon, lon_count)
        part = result[row * slots : (row + 1) * slots]
        out_ref[row] = jnp.where(slot < count, part, 0.0)


def call(kernel, shape, dtype, specs):
    return pl.pallas_call(
        kernel,
        out_shape=jax.ShapeDtypeStruct(shape, dtype),
        in_specs=specs,
        out_specs=VMEM,
        compiler_params=PARAMS,
    )


def on_device(fields, row_points, band_mask, norm_gain, w_query, w_key, w_value, w_out):
    rows, slots, width = fields.shape
    lat_count = lax.axis_size("lat")
    lon_count = lax.axis_size("lon")
    tokens = rows * slots
    chips = lon_count // 2
    bf16 = jnp.bfloat16
    groups = [[2 * chip + core for chip in range(chips)] for core in range(2)]
    swap = [(place, place + 1 - 2 * (place % 2)) for place in range(lon_count)]

    normed = call(norm_kernel, (tokens, width), bf16, [VMEM, VMEM])(
        fields, norm_gain.reshape(1, width)
    )
    peer = lax.ppermute(normed, "lon", swap)
    near = [
        lax.ppermute(
            normed, "lat", [(place, (place - offset) % lat_count) for place in range(lat_count)]
        )
        for offset in OFFSETS
    ]
    packed = call(
        functools.partial(axial_project_kernel, lon_count), (chips, 3 * slots, PAIR), bf16, [VMEM] * 5
    )(normed, peer, w_query, w_key, w_value)
    row_head = lax.all_to_all(packed, "lon", 0, 0, axis_index_groups=groups, tiled=True)
    axial = call(
        functools.partial(axial_kernel, lon_count), (chips, slots, PAIR), bf16, [SMEM, VMEM]
    )(row_points, row_head)
    mine = lax.all_to_all(axial, "lon", 0, 0, axis_index_groups=groups, tiled=True)
    other = lax.ppermute(mine, "lon", swap)
    band = call(
        functools.partial(band_kernel, lat_count, lon_count),
        (tokens, (HEADS - AXIAL_HEADS) * HEAD_DIM),
        bf16,
        [SMEM, SMEM] + [VMEM] * 8,
    )(row_points, band_mask, normed, *near, w_query, w_key, w_value)
    summed = call(band_out_kernel, (tokens, width), jnp.float32, [VMEM] * 3)(fields, band, w_out)
    return call(
        functools.partial(finish_kernel, lon_count), (rows, slots, width), jnp.float32, [SMEM] + [VMEM] * 4
    )(row_points, summed, mine, other, w_out)


def solution(mesh):
    in_specs = (P("lat", "lon", None), P(), P(), P(), P(), P(), P(), P())
    out_specs = P("lat", "lon", None)
    return jax.shard_map(
        on_device, mesh=mesh, in_specs=in_specs, out_specs=out_specs, check_vma=False
    )
```

time: 211 us -> 70.3 us (0.33)
  waiting for transfers between devices: 117 us -> 9.26 us
  local copies, waits for them, and re-layouts: 33 us -> 6.6 us
  blocking collectives: 0 us -> 21.6 us
  between operations: 16.1 us -> 0.08 us
  matrix products: 15.9 us -> 0 us
  Pallas kernels: 0 us -> 14.6 us
  other arithmetic: 6.88 us -> 0 us
  starting transfers between devices: 21 us -> 16.9 us
    all_gather x2 -> x0, waiting for transfers between devices: 115 us -> none  [the longest x1 73.8 us: on_device(): part_value = lax.all_gather(axial_value, 'lon', axis=1, tiled=True)]
    all_to_all x0 -> x1, blocking collectives: none -> 21.6 us  [on_device(): lax.all_to_all(packed, 'lon', 0, 0, axis_index_groups=groups, tiled=True)]
    dot_general x8 -> x0, matrix products: 15.9 us -> none  [the longest x1 4.78 us: on_device(): jnp.einsum('rphk,rkhd->rphd', weights.astype(jnp.bfloat16), part_value, p...]
    pallas_call x0 -> x6, Pallas kernels: none -> 14.6 us  [the longest x1 5.93 us: on_device(): call(functools.partial(band_kernel, lat_count, lon_count), (tokens, (HEAD...]
    all_gather x2 -> x0, local copies, waits for them, and re-layouts: 12.6 us -> none  [the longest x1 6.33 us: on_device(): part_key = lax.all_gather(axial_key, 'lon', axis=1, tiled=True)]
    ppermute x8 -> x6, starting transfers between devices: 20.9 us -> 10.9 us  [the longest x4 5.12 us: on_device(): lax.ppermute(normed, 'lat', [(place, (place - offset) % lat_count) for pl...]
    all_to_all x0 -> x1, starting transfers between devices: none -> 6.06 us  [on_device(): lax.all_to_all(axial, 'lon', 0, 0, axis_index_groups=groups, tiled=True)]
    concatenate x5 -> x0, local copies, waits for them, and re-layouts: 5.04 us -> none  [the longest x2 2.8 us: on_device(): jnp.concatenate(value_list, axis=0).reshape(-1, band_heads, HEAD_DIM)]
  transfers between devices with their start and end apart: 10 -> 7, of which waited for: 3 -> 4; matrix products, arithmetic and copies ran while one was open for 16% -> 0% of each run, Pallas kernels for 0% -> 9%
where the time goes in v1:
time: 70.3 us; the launch traced here: 69 us
  blocking collectives  21.6 us (31%)
  starting transfers between devices  16.9 us (24%)
  Pallas kernels  14.6 us (21%)
  waiting for transfers between devices  9.26 us (13%)
  local copies, waits for them, and re-layouts  6.6 us (9%)
    all_to_all x1, blocking collectives, on_device(): lax.all_to_all(packed, 'lon', 0, 0, axis_index_groups=groups, tiled=True)  21.6 us
    unnamed x21, local copies, waits for them, and re-layouts  6.6 us
    all_to_all x1, starting transfers between devices, on_device(): lax.all_to_all(axial, 'lon', 0, 0, axis_index_groups=groups, tiled=True)  6.06 us
    pallas_call x1, Pallas kernels, on_device(): call(functools.partial(band_kernel, lat_count, lon_count), (tokens, (HEAD...  5.93 us
    ppermute x4, starting transfers between devices, on_device(): lax.ppermute(normed, 'lat', [(place, (place - offset) % lat_count) for pl...  5.12 us
    all_to_all x1, waiting for transfers between devices, on_device(): lax.all_to_all(axial, 'lon', 0, 0, axis_index_groups=groups, tiled=True)  4.07 us
    ppermute x4, waiting for transfers between devices, on_device(): lax.ppermute(normed, 'lat', [(place, (place - offset) % lat_count) for pl...  4.02 us
    pallas_call x1, Pallas kernels, on_device(): call(functools.partial(axial_kernel, lon_count), (chips, slots, PAIR), bf...  3.6 us
  transfers between devices with their start and end apart: 7, of which 4 were waited for; matrix products, arithmetic and copies ran while one was open for 0% of the time, Pallas kernels for 9%

profile of v1, /device:TPU:1, one launch (start us, length us, event | category | flops | bytes accessed | tf_op | source)
XLA Modules:
  0.0 69.0 jit_solution(10870279122207839698)
XLA Ops:
  0.0 0.0 copy-start.5
  0.0 1.0 %copy-done.5 = f32[4,32,1024]{2,1,0:T(8,128)S(1)} copy-done((f32[4,32,1024]{2,1,0:T(8,128)S(1)}, f32[4,32,1024]{2,1,0:T(8,128)}, u32[]{:S(2)}) %copy-start.5) | copy-done | bytes 524312
  1.0 0.0 copy-start.8
  1.0 0.7 copy-done.8
  1.7 0.0 copy-start.7
  1.7 0.0 copy-start.9
  1.7 0.2 shard_map.82.own_ref
  2.0 3.3 %collective-permute-start.4 = (bf16[128,1024]{1,0:T(8,128)(2,1)S(1)}, bf16[128,1024]{1,0:T(8,128)(2,1)S(1)}, u32[]{:S(2)}, u32[]{:S(2)}) collective-permute-start(bf16[128,1024]{1,0:T(8,128)(2,1)S(1)} %shard_map.82.own_ref), channel_id=1, source_target_pairs={{0,1},{1,0},{2,3},{3,2},{4,5},{5,4},{6,7},{7,6},{8,9},{9,8},{10,11... | collective-permute-start | bytes 786440 | tf_op jit(solution)/shard_map/ppermute | solution.py:250
  5.3 1.2 %collective-permute-done.4.peer_ref = bf16[128,1024]{1,0:T(8,128)(2,1)S(1)} collective-permute-done((bf16[128,1024]{1,0:T(8,128)(2,1)S(1)}, bf16[128,1024]{1,0:T(8,128)(2,1)S(1)}, u32[]{:S(2)}, u32[]{:S(2)}) %collective-permute-start.4) | collective-permute-done | bytes 262176 | tf_op jit(solution)/shard_map/ppermute | solution.py:250
  6.5 0.0 copy-start
  6.5 1.6 %copy-done = bf16[1024,1024]{1,0:T(8,128)(2,1)S(1)} copy-done((bf16[1024,1024]{1,0:T(8,128)(2,1)S(1)}, bf16[1024,1024]{1,0:T(8,128)(2,1)}, u32[]{:S(2)}) %copy-start) | copy-done | bytes 2097176
  8.1 0.0 copy-start.2
  8.1 1.6 %copy-done.2 = bf16[1024,1024]{1,0:T(8,128)(2,1)S(1)} copy-done((bf16[1024,1024]{1,0:T(8,128)(2,1)S(1)}, bf16[1024,1024]{1,0:T(8,128)(2,1)}, u32[]{:S(2)}) %copy-start.2) | copy-done | bytes 2097176
  9.7 0.0 copy-start.1
  9.7 2.4 %shard_map.85 = bf16[16,96,128]{2,1,0:T(8,128)(2,1)S(1)} custom-call(bf16[128,1024]{1,0:T(8,128)(2,1)S(1)} %shard_map.82.own_ref, bf16[128,1024]{1,0:T(8,128)(2,1)S(1)} %collective-permute-done.4.peer_ref, bf16[1024,1024]{1,0:T(8,128)(2,1)S(1)} %copy-done, bf16[1024,1024]{1,0:T(8,128)(2,1)S(1)} %copy-done.2, bf16[1024,1024]{1,0:T(8,128)(2,1)} %wv_ref.3), custom_call_target="tpu_custom_call" | custom-call | tf_op jit(solution)/shard_map/pallas_call | solution.py:257
  12.1 21.6 %all_to_all.10.in_ref = bf16[16,96,128]{2,1,0:T(8,128)(2,1)S(1)} all-to-all(bf16[16,96,128]{2,1,0:T(8,128)(2,1)S(1)} %shard_map.85), channel_id=1, replica_groups={{0,2,4,6,8,10,12,14,16,18,20,22,24,26,28,30},{1,3,5,7,9,11,13,15,17,19,..., dimensions={0} | all-to-all | bytes 786432 | tf_op jit(solution)/shard_map/all_to_all | solution.py:260
  33.7 0.0 copy-done.7
  33.7 3.6 %shard_map.86 = bf16[16,32,128]{2,1,0:T(8,128)(2,1)} custom-call(s32[32]{0:T(128)S(1)} %copy-done.7, bf16[16,96,128]{2,1,0:T(8,128)(2,1)S(1)} %all_to_all.10.in_ref), custom_call_target="tpu_custom_call" | custom-call | tf_op jit(solution)/shard_map/pallas_call | solution.py:261
  37.3 6.1 %all-to-all-start.1 = ((bf16[16,32,128]{2,1,0:T(8,128)(2,1)}), bf16[16,32,128]{2,1,0:T(8,128)(2,1)S(1)}, u32[]{:S(2)}, u32[]{:S(2)}) async-start(bf16[16,32,128]{2,1,0:T(8,128)(2,1)} %shard_map.86), calls=%async_computation.1 | async-start | bytes 262144 | tf_op jit(solution)/shard_map/all_to_all | solution.py:264
  43.3 1.3 %collective-permute-start = (bf16[128,1024]{1,0:T(8,128)(2,1)S(1)}, bf16[128,1024]{1,0:T(8,128)(2,1)S(1)}, u32[]{:S(2)}, u32[]{:S(2)}) collective-permute-start(bf16[128,1024]{1,0:T(8,128)(2,1)S(1)} %shard_map.82.own_ref), channel_id=1, source_target_pairs={{0,64},{32,96},{64,128},{96,160},{128,192},{160,224},{192,0},{224,... | collective-permute-start | bytes 786440 | tf_op jit(solution)/shard_map/ppermute | solution.py:252
  44.6 0.4 collective-permute-start.1
  45.0 3.2 %collective-permute-start.2 = (bf16[128,1024]{1,0:T(8,128)(2,1)S(1)}, bf16[128,1024]{1,0:T(8,128)(2,1)S(1)}, u32[]{:S(2)}, u32[]{:S(2)}) collective-permute-start(bf16[128,1024]{1,0:T(8,128)(2,1)S(1)} %shard_map.82.own_ref), channel_id=1, source_target_pairs={{0,224},{32,0},{64,32},{96,64},{128,96},{160,128},{192,160},{224,1... | collective-permute-start | bytes 786440 | tf_op jit(solution)/shard_map/ppermute | solution.py:252
  48.2 0.3 collective-permute-start.3
  48.5 4.1 %all-to-all-done.1.mine_ref = bf16[16,32,128]{2,1,0:T(8,128)(2,1)S(1)} async-done(((bf16[16,32,128]{2,1,0:T(8,128)(2,1)}), bf16[16,32,128]{2,1,0:T(8,128)(2,1)S(1)}, u32[]{:S(2)}, u32[]{:S(2)}) %all-to-all-start.1) | async-done | bytes 131104 | tf_op jit(solution)/shard_map/all_to_all | solution.py:264
  52.5 2.4 %collective-permute-start.5 = (bf16[16,32,128]{2,1,0:T(8,128)(2,1)S(1)}, bf16[16,32,128]{2,1,0:T(8,128)(2,1)}, u32[]{:S(2)}, u32[]{:S(2)}) collective-permute-start(bf16[16,32,128]{2,1,0:T(8,128)(2,1)S(1)} %all-to-all-done.1.mine_ref), channel_id=1, source_target_pairs={{0,1},{1,0},{2,3},{3,2},{4,5},{5,4},{6,7},{7,6},{8,9},{9,8},{10,11... | collective-permute-start | bytes 393224 | tf_op jit(solution)/shard_map/ppermute | solution.py:265
  55.0 0.0 copy-done.9
  55.0 0.1 copy.9.mask_ref
  55.0 0.0 collective-permute-done.m2_ref
  55.0 1.9 %collective-permute-done.1.m1_ref = bf16[128,1024]{1,0:T(8,128)(2,1)S(1)} collective-permute-done((bf16[128,1024]{1,0:T(8,128)(2,1)S(1)}, bf16[128,1024]{1,0:T(8,128)(2,1)S(1)}, u32[]{:S(2)}, u32[]{:S(2)}) %collective-permute-start.1) | collective-permute-done | bytes 262176 | tf_op jit(solution)/shard_map/ppermute | solution.py:252
  56.9 2.1 %collective-permute-done.2.p1_ref = bf16[128,1024]{1,0:T(8,128)(2,1)S(1)} collective-permute-done((bf16[128,1024]{1,0:T(8,128)(2,1)S(1)}, bf16[128,1024]{1,0:T(8,128)(2,1)S(1)}, u32[]{:S(2)}, u32[]{:S(2)}) %collective-permute-start.2) | collective-permute-done | bytes 262176 | tf_op jit(solution)/shard_map/ppermute | solution.py:252
  59.1 0.0 collective-permute-done.3.p2_ref
  59.1 0.0 copy-done.1
  59.1 0.0 copy-start.3
  59.1 1.6 %copy-done.3 = bf16[1024,1024]{1,0:T(8,128)(2,1)S(1)} copy-done((bf16[1024,1024]{1,0:T(8,128)(2,1)S(1)}, bf16[1024,1024]{1,0:T(8,128)(2,1)}, u32[]{:S(2)}) %copy-start.3) | copy-done | bytes 2097176
  60.7 0.0 copy-start.4
  60.7 0.0 copy-start.6
  60.7 5.9 %shard_map.83.band_ref = bf16[128,512]{1,0:T(8,128)(2,1)S(1)} custom-call(s32[32]{0:T(128)S(1)} %copy-done.7, s32[8,4]{1,0:T(8,128)S(1)} %copy.9.mask_ref, bf16[128,1024]{1,0:T(8,128)(2,1)S(1)} %shard_map.82.own_ref, bf16[128,1024]{1,0:T(8,128)(2,1)S(1)} %collective-permute-done.m2_ref, bf16[128,1024]{1,0:T(8,128)(2,1)S(1)} %collective-permute-done.1.m1_ref, ...), custom_call_target="tpu_custom_call" | custom-call | tf_op jit(solution)/shard_map/pallas_call | solution.py:266
  66.6 0.0 copy-done.4
  66.6 0.0 copy-done.6
  66.6 0.3 shard_map.84.sum_ref
  66.9 0.0 collective-permute-done.5.other_ref
  67.0 2.1 %shard_map.87 = f32[4,32,1024]{2,1,0:T(8,128)} custom-call(s32[32]{0:T(128)S(1)} %copy-done.7, f32[128,1024]{1,0:T(8,128)S(1)} %shard_map.84.sum_ref, bf16[16,32,128]{2,1,0:T(8,128)(2,1)S(1)} %all-to-all-done.1.mine_ref, bf16[16,32,128]{2,1,0:T(8,128)(2,1)} %collective-permute-done.5.other_ref, bf16[1024,1024]{1,0:T(8,128)(2,1)S(1)} %copy-done.4), custom_call_target="tpu_custom_call" | custom-call | tf_op jit(solution)/shard_map/pallas_call | solution.py:273
Async XLA Ops:
  0.0 1.0 %copy-start.5 = (f32[4,32,1024]{2,1,0:T(8,128)S(1)}, f32[4,32,1024]{2,1,0:T(8,128)}, u32[]{:S(2)}) copy-start(f32[4,32,1024]{2,1,0:T(8,128)} %fields_ref.3) | copy-start | bytes 1572868
  1.0 0.7 copy-start.8
  1.7 32.0 %copy-start.7 = (s32[32]{0:T(128)S(1)}, s32[32]{0:T(128)}, u32[]{:S(2)}) copy-start(s32[32]{0:T(128)} %points_ref.5) | copy-start | bytes 388
  1.7 53.2 %copy-start.9 = (s32[8,4]{0,1:T(4,128)S(1)}, s32[8,4]{0,1:T(4,128)}, u32[]{:S(2)}) copy-start(s32[8,4]{0,1:T(4,128)} %param.10) | copy-start | bytes 388
  2.0 4.5 %collective-permute-start.4 = (bf16[128,1024]{1,0:T(8,128)(2,1)S(1)}, bf16[128,1024]{1,0:T(8,128)(2,1)S(1)}, u32[]{:S(2)}, u32[]{:S(2)}) collective-permute-start(bf16[128,1024]{1,0:T(8,128)(2,1)S(1)} %shard_map.82.own_ref), channel_id=1, source_target_pairs={{0,1},{1,0},{2,3},{3,2},{4,5},{5,4},{6,7},{7,6},{8,9},{9,8},{10,11... | collective-permute-start | bytes 786440 | tf_op jit(solution)/shard_map/ppermute | solution.py:250
  6.5 1.6 %copy-start = (bf16[1024,1024]{1,0:T(8,128)(2,1)S(1)}, bf16[1024,1024]{1,0:T(8,128)(2,1)}, u32[]{:S(2)}) copy-start(bf16[1024,1024]{1,0:T(8,128)(2,1)} %wq_ref.3) | copy-start | bytes 6291460
  8.1 1.6 %copy-start.2 = (bf16[1024,1024]{1,0:T(8,128)(2,1)S(1)}, bf16[1024,1024]{1,0:T(8,128)(2,1)}, u32[]{:S(2)}) copy-start(bf16[1024,1024]{1,0:T(8,128)(2,1)} %wk_ref.3) | copy-start | bytes 6291460
  9.7 49.4 %copy-start.1 = (bf16[1024,1024]{1,0:T(8,128)(2,1)S(1)}, bf16[1024,1024]{1,0:T(8,128)(2,1)}, u32[]{:S(2)}) copy-start(bf16[1024,1024]{1,0:T(8,128)(2,1)} %wq_ref.3) | copy-start | bytes 6291460
  37.3 15.3 %all-to-all-start.1 = ((bf16[16,32,128]{2,1,0:T(8,128)(2,1)}), bf16[16,32,128]{2,1,0:T(8,128)(2,1)S(1)}, u32[]{:S(2)}, u32[]{:S(2)}) async-start(bf16[16,32,128]{2,1,0:T(8,128)(2,1)} %shard_map.86), calls=%async_computation.1 | async-start | bytes 262144 | tf_op jit(solution)/shard_map/all_to_all | solution.py:264
  43.3 11.7 %collective-permute-start = (bf16[128,1024]{1,0:T(8,128)(2,1)S(1)}, bf16[128,1024]{1,0:T(8,128)(2,1)S(1)}, u32[]{:S(2)}, u32[]{:S(2)}) collective-permute-start(bf16[128,1024]{1,0:T(8,128)(2,1)S(1)} %shard_map.82.own_ref), channel_id=1, source_target_pairs={{0,64},{32,96},{64,128},{96,160},{128,192},{160,224},{192,0},{224,... | collective-permute-start | bytes 786440 | tf_op jit(solution)/shard_map/ppermute | solution.py:252
  44.6 12.3 %collective-permute-start.1 = (bf16[128,1024]{1,0:T(8,128)(2,1)S(1)}, bf16[128,1024]{1,0:T(8,128)(2,1)S(1)}, u32[]{:S(2)}, u32[]{:S(2)}) collective-permute-start(bf16[128,1024]{1,0:T(8,128)(2,1)S(1)} %shard_map.82.own_ref), channel_id=1, source_target_pairs={{0,32},{32,64},{64,96},{96,128},{128,160},{160,192},{192,224},{224... | collective-permute-start | bytes 786440 | tf_op jit(solution)/shard_map/ppermute | solution.py:252
  45.0 14.0 %collective-permute-start.2 = (bf16[128,1024]{1,0:T(8,128)(2,1)S(1)}, bf16[128,1024]{1,0:T(8,128)(2,1)S(1)}, u32[]{:S(2)}, u32[]{:S(2)}) collective-permute-start(bf16[128,1024]{1,0:T(8,128)(2,1)S(1)} %shard_map.82.own_ref), channel_id=1, source_target_pairs={{0,224},{32,0},{64,32},{96,64},{128,96},{160,128},{192,160},{224,1... | collective-permute-start | bytes 786440 | tf_op jit(solution)/shard_map/ppermute | solution.py:252
  48.2 10.9 %collective-permute-start.3 = (bf16[128,1024]{1,0:T(8,128)(2,1)S(1)}, bf16[128,1024]{1,0:T(8,128)(2,1)S(1)}, u32[]{:S(2)}, u32[]{:S(2)}) collective-permute-start(bf16[128,1024]{1,0:T(8,128)(2,1)S(1)} %shard_map.82.own_ref), channel_id=1, source_target_pairs={{0,192},{32,224},{64,0},{96,32},{128,64},{160,96},{192,128},{224,1... | collective-permute-start | bytes 786440 | tf_op jit(solution)/shard_map/ppermute | solution.py:252
  52.5 14.4 %collective-permute-start.5 = (bf16[16,32,128]{2,1,0:T(8,128)(2,1)S(1)}, bf16[16,32,128]{2,1,0:T(8,128)(2,1)}, u32[]{:S(2)}, u32[]{:S(2)}) collective-permute-start(bf16[16,32,128]{2,1,0:T(8,128)(2,1)S(1)} %all-to-all-done.1.mine_ref), channel_id=1, source_target_pairs={{0,1},{1,0},{2,3},{3,2},{4,5},{5,4},{6,7},{7,6},{8,9},{9,8},{10,11... | collective-permute-start | bytes 393224 | tf_op jit(solution)/shard_map/ppermute | solution.py:265
  59.1 1.6 %copy-start.3 = (bf16[1024,1024]{1,0:T(8,128)(2,1)S(1)}, bf16[1024,1024]{1,0:T(8,128)(2,1)}, u32[]{:S(2)}) copy-start(bf16[1024,1024]{1,0:T(8,128)(2,1)} %wk_ref.3) | copy-start | bytes 6291460
  60.7 5.9 %copy-start.4 = (bf16[1024,1024]{1,0:T(8,128)(2,1)S(1)}, bf16[1024,1024]{1,0:T(8,128)(2,1)}, u32[]{:S(2)}) copy-start(bf16[1024,1024]{1,0:T(8,128)(2,1)} %w_ref.3) | copy-start | bytes 6291460
  60.7 6.0 %copy-start.6 = (f32[4,32,1024]{2,1,0:T(8,128)S(1)}, f32[4,32,1024]{2,1,0:T(8,128)}, u32[]{:S(2)}) copy-start(f32[4,32,1024]{2,1,0:T(8,128)} %fields_ref.3) | copy-start | bytes 1572868

commit v2 on v1

--- a/solution.py
+++ b/solution.py
@@ -16,10 +16,13 @@
 PAIR = 2 * HEAD_DIM
 SCALE = HEAD_DIM**-0.5
 OFFSETS = (-2, -1, 1, 2)
+BAND_FLOPS = 20_000_000_000
+BAND_OUT_FLOPS = 20_000_000_000
 
 VMEM = pl.BlockSpec(memory_space=pltpu.VMEM)
 SMEM = pl.BlockSpec(memory_space=pltpu.SMEM)
-PARAMS = pltpu.CompilerParams(vmem_limit_bytes=48 * 1024 * 1024)
+HBM = pl.BlockSpec(memory_space=pltpu.HBM)
+ANY = pl.BlockSpec(memory_space=pl.ANY)
 
 
 def dot(a, b):
@@ -42,27 +45,43 @@
     return points // tiles + (tile < points % tiles).astype(jnp.int32)
 
 
-def norm_kernel(fields_ref, gain_ref, out_ref):
+def norm_kernel(
+    fields_hbm, gain_hbm, wq_hbm, wk_hbm, wv_hbm, out_ref, weights_ref, fields_ref, gain_ref, sems
+):
+    core = lax.rem(lax.axis_index("lon"), 2)
+    width = weights_ref.shape[2]
+    columns = pl.ds(pl.multiple_of(core * width, width), width)
+    first = [
+        pltpu.make_async_copy(fields_hbm, fields_ref, sems.at[0]),
+        pltpu.make_async_copy(gain_hbm, gain_ref, sems.at[1]),
+    ]
+    rest = [
+        pltpu.make_async_copy(hbm.at[:, columns], weights_ref.at[place], sems.at[2 + place])
+        for place, hbm in enumerate((wq_hbm, wk_hbm, wv_hbm))
+    ]
+    for copy in first + rest:
+        copy.start()
+    for copy in first:
+        copy.wait()
     rows, slots, width = fields_ref.shape
     values = fields_ref[...].reshape(rows * slots, width)
     mean = jnp.mean(values, axis=-1, keepdims=True)
     centred = values - mean
     var = jnp.mean(centred * centred, axis=-1, keepdims=True)
     out_ref[...] = (centred * lax.rsqrt(var + EPS) * gain_ref[...]).astype(jnp.bfloat16)
-
-
-def axial_project_kernel(lon_count, own_ref, peer_ref, wq_ref, wk_ref, wv_ref, out_ref):
-    core = lax.rem(lax.axis_index("lon"), 2)
+    for copy in rest:
+        copy.wait()
+
+
+def axial_project_kernel(own_ref, peer_ref, weights_ref, out_ref):
     tokens = own_ref.shape[0]
     slots = out_ref.shape[1] // 3
     rows = tokens // slots
     heads = AXIAL_HEADS // 2
-    width = heads * HEAD_DIM
-    columns = pl.ds(pl.multiple_of(core * width, width), width)
     both = jnp.concatenate([own_ref[...], peer_ref[...]], axis=0)
-    query = dot(both, wq_ref[:, columns])
-    key = dot(both, wk_ref[:, columns])
-    value = dot(both, wv_ref[:, columns])
+    query = dot(both, weights_ref[0])
+    key = dot(both, weights_ref[1])
+    value = dot(both, weights_ref[2])
     low = low_half((2 * tokens, PAIR))
     low_v = low_half((tokens, PAIR))
     for pair in range(heads // 2):
@@ -83,7 +102,7 @@
                 out_ref[item, 2 * slots : 3 * slots, :] = v_side[part]
 
 
-def axial_kernel(lon_count, points_ref, in_ref, out_ref):
+def axial_kernel(lon_count, points_ref, in_ref, band_ref, out_ref):
     lon = lax.axis_index("lon")
     core = lax.rem(lon, 2)
     chip = lon // 2
@@ -133,22 +152,32 @@
 
 def band_kernel(
     lat_count, lon_count, points_ref, mask_ref, own_ref, m2_ref, m1_ref, p1_ref, p2_ref,
-    wq_ref, wk_ref, wv_ref, out_ref,
+    wq_hbm, wk_hbm, wv_hbm, out_ref, wq_ref, wkv_ref, sems,
 ):
+    pairs = (HEADS - AXIAL_HEADS) // 2
+    first = AXIAL_HEADS * HEAD_DIM
+    copies = []
+    for pair in range(pairs):
+        columns = pl.ds(first + pair * PAIR, PAIR)
+        copies.append(
+            [
+                pltpu.make_async_copy(wk_hbm.at[:, columns], wkv_ref.at[pair, :, pl.ds(0, PAIR)], sems.at[pair, 0]),
+                pltpu.make_async_copy(wv_hbm.at[:, columns], wkv_ref.at[pair, :, pl.ds(PAIR, PAIR)], sems.at[pair, 1]),
+                pltpu.make_async_copy(wq_hbm.at[:, columns], wq_ref.at[pair], sems.at[pair, 2]),
+            ]
+        )
+    for group in copies:
+        for copy in group:
+            copy.start()
     lat = lax.axis_index("lat")
     lon = lax.axis_index("lon")
     tokens = own_ref.shape[0]
     slots = 32
     rows = tokens // slots
-    first = AXIAL_HEADS * HEAD_DIM
     bands = (0,) + OFFSETS
-    everything = jnp.concatenate(
-        [own_ref[...], m2_ref[...], m1_ref[...], p1_ref[...], p2_ref[...]], axis=0
-    )
+    own = own_ref[...]
+    everything = jnp.concatenate([own, m2_ref[...], m1_ref[...], p1_ref[...], p2_ref[...]], axis=0)
     keys = everything.shape[0]
-    key = dot(everything, wk_ref[:, first:]).astype(jnp.bfloat16)
-    value = dot(everything, wv_ref[:, first:]).astype(jnp.bfloat16)
-    query = dot(own_ref[...], wq_ref[:, first:]).astype(jnp.bfloat16)
     slot = lax.broadcasted_iota(jnp.int32, (slots, PAIR), 0)
     blocks = []
     for offset in bands:
@@ -159,7 +188,7 @@
         else:
             column = offset + REACH if offset < 0 else offset + REACH - 1
             inside = (source >= 0) & (source < lat_count)
-            allowed = jnp.where(inside & (mask_ref[lat, column] == 1), 1, 0)
+            allowed = jnp.where(inside & (mask_ref[column, lat] == 1), 1, 0)
         for row in range(rows):
             count = live_count(points_ref[held * rows + row], lon, lon_count) * allowed
             blocks.append(jnp.where(slot < count, 0.0, DEAD))
@@ -168,9 +197,12 @@
     lane_q = lax.broadcasted_iota(jnp.int32, (tokens, PAIR), 1)
     zero_k = jnp.zeros((keys, PAIR), jnp.bfloat16)
     low_o = lane_q < HEAD_DIM
-    for pair in range((HEADS - AXIAL_HEADS) // 2):
-        span = slice(pair * PAIR, (pair + 1) * PAIR)
-        q, k, v = query[:, span] * jnp.bfloat16(SCALE), key[:, span], value[:, span]
+    for pair in range(pairs):
+        for copy in copies[pair]:
+            copy.wait()
+        kv = dot(everything, wkv_ref[pair]).astype(jnp.bfloat16)
+        k, v = kv[:, :PAIR], kv[:, PAIR:]
+        q = dot(own, wq_ref[pair]).astype(jnp.bfloat16) * jnp.bfloat16(SCALE)
         outs = []
         for side in range(2):
             spare = HEAD_DIM if side == 0 else 0
@@ -183,13 +215,25 @@
             weights = jnp.exp(scores - peak)
             total = jnp.sum(weights, axis=-1, keepdims=True)
             outs.append(dot(weights.astype(jnp.bfloat16), v) / total)
-        out_ref[:, span] = jnp.where(low_o, outs[0], outs[1]).astype(jnp.bfloat16)
-
-
-def band_out_kernel(fields_ref, band_ref, w_ref, out_ref):
+        out_ref[:, pair * PAIR : (pair + 1) * PAIR] = jnp.where(low_o, outs[0], outs[1]).astype(
+            jnp.bfloat16
+        )
+
+
+def band_out_kernel(fields_hbm, band_ref, w_hbm, out_ref, axial_w_ref, fields_ref, w_ref, sems):
     rows, slots, width = fields_ref.shape
-    first = AXIAL_HEADS * HEAD_DIM
-    out_ref[...] = fields_ref[...].reshape(rows * slots, width) + dot(band_ref[...], w_ref[first:, :])
+    depth = w_ref.shape[0]
+    copies = [
+        pltpu.make_async_copy(w_hbm.at[pl.ds(depth, depth)], w_ref, sems.at[0]),
+        pltpu.make_async_copy(fields_hbm, fields_ref, sems.at[1]),
+        pltpu.make_async_copy(w_hbm.at[pl.ds(0, depth)], axial_w_ref, sems.at[2]),
+    ]
+    for copy in copies:
+        copy.start()
+    for copy in copies[:2]:
+        copy.wait()
+    out_ref[...] = fields_ref[...].reshape(rows * slots, width) + dot(band_ref[...], w_ref[...])
+    copies[2].wait()
 
 
 def finish_kernel(lon_count, points_ref, sum_ref, mine_ref, other_ref, w_ref, out_ref):
@@ -224,13 +268,15 @@
         out_ref[row] = jnp.where(slot < count, part, 0.0)
 
 
-def call(kernel, shape, dtype, specs):
+def call(kernel, shapes, specs, scratch=(), flops=0):
     return pl.pallas_call(
         kernel,
-        out_shape=jax.ShapeDtypeStruct(shape, dtype),
+        out_shape=[jax.ShapeDtypeStruct(shape, dtype) for shape, dtype in shapes],
         in_specs=specs,
-        out_specs=VMEM,
-        compiler_params=PARAMS,
+        out_specs=[VMEM] * len(shapes),
+        scratch_shapes=scratch,
+        compiler_params=pltpu.CompilerParams(vmem_limit_bytes=24 * 1024 * 1024),
+        cost_estimate=pl.CostEstimate(flops=flops, transcendentals=0, bytes_accessed=0) if flops else None,
     )
 
 
@@ -240,13 +286,26 @@
     lon_count = lax.axis_size("lon")
     tokens = rows * slots
     chips = lon_count // 2
-    bf16 = jnp.bfloat16
+    axial_width = AXIAL_HEADS * HEAD_DIM
+    band_width = (HEADS - AXIAL_HEADS) * HEAD_DIM
+    pairs = band_width // PAIR
+    bf16, f32 = jnp.bfloat16, jnp.float32
     groups = [[2 * chip + core for chip in range(chips)] for core in range(2)]
     swap = [(place, place + 1 - 2 * (place % 2)) for place in range(lon_count)]
 
-    normed = call(norm_kernel, (tokens, width), bf16, [VMEM, VMEM])(
-        fields, norm_gain.reshape(1, width)
-    )
+    def in_hbm(*arrays):
+        return [pltpu.with_memory_space_constraint(array, pltpu.HBM) for array in arrays]
+
+    normed, weights = call(
+        norm_kernel,
+        [((tokens, width), bf16), ((3, width, axial_width // 2), bf16)],
+        [HBM] * 5,
+        [
+            pltpu.VMEM((rows, slots, width), f32),
+            pltpu.VMEM((1, width), f32),
+            pltpu.SemaphoreType.DMA((5,)),
+        ],
+    )(*in_hbm(fields, norm_gain.reshape(1, width), w_query, w_key, w_value))
     peer = lax.ppermute(normed, "lon", swap)
     near = [
         lax.ppermute(
@@ -254,25 +313,45 @@
         )
         for offset in OFFSETS
     ]
-    packed = call(
-        functools.partial(axial_project_kernel, lon_count), (chips, 3 * slots, PAIR), bf16, [VMEM] * 5
-    )(normed, peer, w_query, w_key, w_value)
+    (packed,) = call(axial_project_kernel, [((chips, 3 * slots, PAIR), bf16)], [VMEM] * 3)(
+        normed, peer, weights
+    )
     row_head = lax.all_to_all(packed, "lon", 0, 0, axis_index_groups=groups, tiled=True)
-    axial = call(
-        functools.partial(axial_kernel, lon_count), (chips, slots, PAIR), bf16, [SMEM, VMEM]
-    )(row_points, row_head)
+    (band,) = call(
+        functools.partial(band_kernel, lat_count, lon_count),
+        [((tokens, band_width), bf16)],
+        [SMEM, SMEM] + [VMEM] * 5 + [HBM] * 3,
+        [
+            pltpu.VMEM((pairs, width, PAIR), bf16),
+            pltpu.VMEM((pairs, width, 2 * PAIR), bf16),
+            pltpu.SemaphoreType.DMA((pairs, 3)),
+        ],
+        BAND_FLOPS,
+    )(row_points, band_mask.T, normed, *near, *in_hbm(w_query, w_key, w_value))
+    (axial,) = call(
+        functools.partial(axial_kernel, lon_count),
+        [((chips, slots, PAIR), bf16)],
+        [SMEM, VMEM, ANY],
+    )(row_points, row_head, band)
     mine = lax.all_to_all(axial, "lon", 0, 0, axis_index_groups=groups, tiled=True)
     other = lax.ppermute(mine, "lon", swap)
-    band = call(
-        functools.partial(band_kernel, lat_count, lon_count),
-        (tokens, (HEADS - AXIAL_HEADS) * HEAD_DIM),
-        bf16,
-        [SMEM, SMEM] + [VMEM] * 8,
-    )(row_points, band_mask, normed, *near, w_query, w_key, w_value)
-    summed = call(band_out_kernel, (tokens, width), jnp.float32, [VMEM] * 3)(fields, band, w_out)
-    return call(
-        functools.partial(finish_kernel, lon_count), (rows, slots, width), jnp.float32, [SMEM] + [VMEM] * 4
-    )(row_points, summed, mine, other, w_out)
+    summed, axial_w = call(
+        band_out_kernel,
+        [((tokens, width), f32), ((axial_width, width), bf16)],
+        [HBM, VMEM, HBM],
+        [
+            pltpu.VMEM((rows, slots, width), f32),
+            pltpu.VMEM((band_width, width), bf16),
+            pltpu.SemaphoreType.DMA((3,)),
+        ],
+        BAND_OUT_FLOPS,
+    )(*in_hbm(fields), band, *in_hbm(w_out))
+    (out,) = call(
+        functools.partial(finish_kernel, lon_count),
+        [((rows, slots, width), f32)],
+        [SMEM] + [VMEM] * 4,
+    )(row_points, summed, mine, other, axial_w)
+    return out
 
 
 def solution(mesh):

time: 70.3 us -> 57.1 us (0.81)
  blocking collectives: 21.6 us -> 14.5 us
  local copies, waits for them, and re-layouts: 6.6 us -> 0.01 us
  waiting for transfers between devices: 9.26 us -> 3.93 us
  starting transfers between devices: 16.9 us -> 20.1 us
  Pallas kernels: 14.6 us -> 17.7 us
    all_to_all x1, blocking collectives: 21.6 us -> 14.5 us  [on_device(): lax.all_to_all(axial, 'lon', 0, 0, axis_index_groups=groups, tiled=True)]
    unnamed x21 -> x4, local copies, waits for them, and re-layouts: 6.6 us -> 0.01 us
    all_to_all x1, starting transfers between devices: 6.06 us -> 10.6 us  [on_device(): lax.all_to_all(packed, 'lon', 0, 0, axis_index_groups=groups, tiled=True)]
    ppermute x4, waiting for transfers between devices: 4.02 us -> 0.01 us  [on_device(): lax.ppermute(normed, 'lat', [(place, (place - offset) % lat_count) for pl...]
    pallas_call x6, Pallas kernels: 14.6 us -> 17.7 us  [the longest x1 8.37 us: on_device(): call(functools.partial(band_kernel, lat_count, lon_count), [((tokens, ban...]
    ppermute x4, starting transfers between devices: 5.12 us -> 3.24 us  [on_device(): lax.ppermute(normed, 'lat', [(place, (place - offset) % lat_count) for pl...]
    ppermute x1, waiting for transfers between devices: 1.16 us -> 0.01 us  [on_device(): peer = lax.ppermute(normed, 'lon', swap)]
  transfers between devices with their start and end apart: 7 -> 7, of which waited for: 4 -> 1; matrix products, arithmetic and copies ran while one was open for 0% -> 0% of each run, Pallas kernels for 9% -> 20%
where the time goes in v2:
time: 57.1 us; the launch traced here: 56.4 us
  starting transfers between devices  20.1 us (35%)
  Pallas kernels  17.7 us (31%)
  blocking collectives  14.5 us (25%)
  waiting for transfers between devices  3.93 us (7%)
    all_to_all x1, blocking collectives, on_device(): lax.all_to_all(axial, 'lon', 0, 0, axis_index_groups=groups, tiled=True)  14.5 us
    all_to_all x1, starting transfers between devices, on_device(): lax.all_to_all(packed, 'lon', 0, 0, axis_index_groups=groups, tiled=True)  10.6 us
    pallas_call x1, Pallas kernels, on_device(): call(functools.partial(band_kernel, lat_count, lon_count), [((tokens, ban...  8.37 us
    all_to_all x1, waiting for transfers between devices, on_device(): lax.all_to_all(packed, 'lon', 0, 0, axis_index_groups=groups, tiled=True)  3.92 us
    ppermute x1, starting transfers between devices, on_device(): peer = lax.ppermute(normed, 'lon', swap)  3.33 us
    ppermute x4, starting transfers between devices, on_device(): lax.ppermute(normed, 'lat', [(place, (place - offset) % lat_count) for pl...  3.24 us
    pallas_call x1, Pallas kernels, on_device(): call(functools.partial(axial_kernel, lon_count), [((chips, slots, PAIR),...  2.93 us
    ppermute x1, starting transfers between devices, on_device(): other = lax.ppermute(mine, 'lon', swap)  2.87 us
  transfers between devices with their start and end apart: 7, of which 1 were waited for; matrix products, arithmetic and copies ran while one was open for 0% of the time, Pallas kernels for 20%

profile of v2, /device:TPU:1, one launch (start us, length us, event | category | flops | bytes accessed | tf_op | source)
XLA Modules:
  0.0 56.4 jit_solution(3705887625833157084)
XLA Ops:
  0.0 1.6 %shard_map.82 = (bf16[128,1024]{1,0:T(8,128)(2,1)S(1)}, bf16[3,1024,256]{2,1,0:T(8,128)(2,1)S(1)}) custom-call(f32[4,32,1024]{2,1,0:T(8,128)} %fields_hbm.3, f32[1,1024]{1,0:T(1,128)} %bitcast.3, bf16[1024,1024]{1,0:T(8,128)(2,1)} %wq_hbm.3, bf16[1024,1024]{1,0:T(8,128)(2,1)} %wk_hbm.3, bf16[1024,1024]{1,0:T(8,128)(2,1)} %wv_hbm.3), custom_call_target="tpu_custom_call" | custom-call | tf_op jit(solution)/shard_map/pallas_call | solution.py:299
  1.6 0.0 copy-start
  1.6 0.0 copy-start.1
  1.6 3.3 %collective-permute-start.4 = (bf16[128,1024]{1,0:T(8,128)(2,1)S(1)}, bf16[128,1024]{1,0:T(8,128)(2,1)S(1)}, u32[]{:S(2)}, u32[]{:S(2)}) collective-permute-start(bf16[128,1024]{1,0:T(8,128)(2,1)S(1)} %get-tuple-element.9.own_ref), channel_id=1, source_target_pairs={{0,1},{1,0},{2,3},{3,2},{4,5},{5,4},{6,7},{7,6},{8,9},{9,8},{10,11... | collective-permute-start | bytes 786440 | tf_op jit(solution)/shard_map/ppermute | solution.py:309
  5.0 0.8 %collective-permute-start.3 = (bf16[128,1024]{1,0:T(8,128)(2,1)S(1)}, bf16[128,1024]{1,0:T(8,128)(2,1)S(1)}, u32[]{:S(2)}, u32[]{:S(2)}) collective-permute-start(bf16[128,1024]{1,0:T(8,128)(2,1)S(1)} %get-tuple-element.9.own_ref), channel_id=1, source_target_pairs={{0,192},{32,224},{64,0},{96,32},{128,64},{160,96},{192,128},{224,1... | collective-permute-start | bytes 786440 | tf_op jit(solution)/shard_map/ppermute | solution.py:311
  5.7 1.6 %collective-permute-start.2 = (bf16[128,1024]{1,0:T(8,128)(2,1)S(1)}, bf16[128,1024]{1,0:T(8,128)(2,1)S(1)}, u32[]{:S(2)}, u32[]{:S(2)}) collective-permute-start(bf16[128,1024]{1,0:T(8,128)(2,1)S(1)} %get-tuple-element.9.own_ref), channel_id=1, source_target_pairs={{0,224},{32,0},{64,32},{96,64},{128,96},{160,128},{192,160},{224,1... | collective-permute-start | bytes 786440 | tf_op jit(solution)/shard_map/ppermute | solution.py:311
  7.3 0.0 collective-permute-start.1
  7.3 0.9 %collective-permute-start = (bf16[128,1024]{1,0:T(8,128)(2,1)S(1)}, bf16[128,1024]{1,0:T(8,128)(2,1)S(1)}, u32[]{:S(2)}, u32[]{:S(2)}) collective-permute-start(bf16[128,1024]{1,0:T(8,128)(2,1)S(1)} %get-tuple-element.9.own_ref), channel_id=1, source_target_pairs={{0,64},{32,96},{64,128},{96,160},{128,192},{160,224},{192,0},{224,... | collective-permute-start | bytes 786440 | tf_op jit(solution)/shard_map/ppermute | solution.py:311
  8.2 0.0 collective-permute-done.4.peer_ref
  8.2 1.4 %shard_map.85 = bf16[16,96,128]{2,1,0:T(8,128)(2,1)} custom-call(bf16[128,1024]{1,0:T(8,128)(2,1)S(1)} %get-tuple-element.9.own_ref, bf16[128,1024]{1,0:T(8,128)(2,1)S(1)} %collective-permute-done.4.peer_ref, bf16[3,1024,256]{2,1,0:T(8,128)(2,1)S(1)} %get-tuple-element.11.weights_ref), custom_call_target="tpu_custom_call" | custom-call | tf_op jit(solution)/shard_map/pallas_call | solution.py:316
  9.6 10.6 %all-to-all-start = ((bf16[16,96,128]{2,1,0:T(8,128)(2,1)}), bf16[16,96,128]{2,1,0:T(8,128)(2,1)S(1)}, u32[]{:S(2)}, u32[]{:S(2)}) async-start(bf16[16,96,128]{2,1,0:T(8,128)(2,1)} %shard_map.85), calls=%async_computation | async-start | bytes 786432 | tf_op jit(solution)/shard_map/all_to_all | solution.py:319
  20.2 0.0 collective-permute-done.3.p2_ref
  20.2 0.0 collective-permute-done.2.p1_ref
  20.2 0.0 collective-permute-done.1.m1_ref
  20.3 0.0 collective-permute-done.m2_ref
  20.3 0.0 copy-done
  20.3 0.0 copy-done.1
  20.3 8.4 %shard_map.83.band_ref = bf16[128,512]{1,0:T(8,128)(2,1)S(1)} custom-call(s32[32]{0:T(128)S(1)} %copy-done, s32[4,8]{1,0:T(4,128)S(1)} %bitcast.2, bf16[128,1024]{1,0:T(8,128)(2,1)S(1)} %get-tuple-element.9.own_ref, bf16[128,1024]{1,0:T(8,128)(2,1)S(1)} %collective-permute-done.m2_ref, bf16[128,1024]{1,0:T(8,128)(2,1)S(1)} %collective-permute-done.1.m1_ref, ...), custom_call_target="tpu_custom_call" | custom-call | flops 20000000000 | tf_op jit(solution)/shard_map/pallas_call | solution.py:320
  28.7 3.9 %all-to-all-done.in_ref = bf16[16,96,128]{2,1,0:T(8,128)(2,1)S(1)} async-done(((bf16[16,96,128]{2,1,0:T(8,128)(2,1)}), bf16[16,96,128]{2,1,0:T(8,128)(2,1)S(1)}, u32[]{:S(2)}, u32[]{:S(2)}) %all-to-all-start) | async-done | bytes 393248 | tf_op jit(solution)/shard_map/all_to_all | solution.py:319
  32.6 2.9 %shard_map.86 = bf16[16,32,128]{2,1,0:T(8,128)(2,1)S(1)} custom-call(s32[32]{0:T(128)S(1)} %copy-done, bf16[16,96,128]{2,1,0:T(8,128)(2,1)S(1)} %all-to-all-done.in_ref, bf16[128,512]{1,0:T(8,128)(2,1)S(1)} %shard_map.83.band_ref), custom_call_target="tpu_custom_call" | custom-call | tf_op jit(solution)/shard_map/pallas_call | solution.py:331
  35.5 14.5 %all_to_all.10.mine_ref = bf16[16,32,128]{2,1,0:T(8,128)(2,1)S(1)} all-to-all(bf16[16,32,128]{2,1,0:T(8,128)(2,1)S(1)} %shard_map.86), channel_id=1, replica_groups={{0,2,4,6,8,10,12,14,16,18,20,22,24,26,28,30},{1,3,5,7,9,11,13,15,17,19,..., dimensions={0} | all-to-all | bytes 262144 | tf_op jit(solution)/shard_map/all_to_all | solution.py:336
  50.1 2.9 %collective-permute-start.5 = (bf16[16,32,128]{2,1,0:T(8,128)(2,1)S(1)}, bf16[16,32,128]{2,1,0:T(8,128)(2,1)S(1)}, u32[]{:S(2)}, u32[]{:S(2)}) collective-permute-start(bf16[16,32,128]{2,1,0:T(8,128)(2,1)S(1)} %all_to_all.10.mine_ref), channel_id=1, source_target_pairs={{0,1},{1,0},{2,3},{3,2},{4,5},{5,4},{6,7},{7,6},{8,9},{9,8},{10,11... | collective-permute-start | bytes 393224 | tf_op jit(solution)/shard_map/ppermute | solution.py:337
  52.9 1.7 %shard_map.84 = (f32[128,1024]{1,0:T(8,128)S(1)}, bf16[512,1024]{1,0:T(8,128)(2,1)S(1)}) custom-call(f32[4,32,1024]{2,1,0:T(8,128)} %fields_hbm.3, bf16[128,512]{1,0:T(8,128)(2,1)S(1)} %shard_map.83.band_ref, bf16[1024,1024]{1,0:T(8,128)(2,1)} %w_hbm.1), custom_call_target="tpu_custom_call" | custom-call | flops 20000000000 | tf_op jit(solution)/shard_map/pallas_call | solution.py:338
  54.7 0.0 collective-permute-done.5.other_ref
  54.7 1.7 %shard_map.87 = f32[4,32,1024]{2,1,0:T(8,128)} custom-call(s32[32]{0:T(128)S(1)} %copy-done, f32[128,1024]{1,0:T(8,128)S(1)} %get-tuple-element.10.sum_ref, bf16[16,32,128]{2,1,0:T(8,128)(2,1)S(1)} %all_to_all.10.mine_ref, bf16[16,32,128]{2,1,0:T(8,128)(2,1)S(1)} %collective-permute-done.5.other_ref, bf16[512,1024]{1,0:T(8,128)(2,1)S(1)} %get-tuple-element.12.w_ref), custom_call_target="tpu_custom_call" | custom-call | tf_op jit(solution)/shard_map/pallas_call | solution.py:349
Async XLA Ops:
  1.6 18.7 %copy-start = (s32[32]{0:T(128)S(1)}, s32[32]{0:T(128)}, u32[]{:S(2)}) copy-start(s32[32]{0:T(128)} %points_ref.5) | copy-start | bytes 388
  1.6 18.7 %copy-start.1 = (s32[8,4]{0,1:T(4,128)S(1)}, s32[8,4]{0,1:T(4,128)}, u32[]{:S(2)}) copy-start(s32[8,4]{0,1:T(4,128)} %param.10) | copy-start | bytes 388
  1.6 6.6 %collective-permute-start.4 = (bf16[128,1024]{1,0:T(8,128)(2,1)S(1)}, bf16[128,1024]{1,0:T(8,128)(2,1)S(1)}, u32[]{:S(2)}, u32[]{:S(2)}) collective-permute-start(bf16[128,1024]{1,0:T(8,128)(2,1)S(1)} %get-tuple-element.9.own_ref), channel_id=1, source_target_pairs={{0,1},{1,0},{2,3},{3,2},{4,5},{5,4},{6,7},{7,6},{8,9},{9,8},{10,11... | collective-permute-start | bytes 786440 | tf_op jit(solution)/shard_map/ppermute | solution.py:309
  5.0 15.3 %collective-permute-start.3 = (bf16[128,1024]{1,0:T(8,128)(2,1)S(1)}, bf16[128,1024]{1,0:T(8,128)(2,1)S(1)}, u32[]{:S(2)}, u32[]{:S(2)}) collective-permute-start(bf16[128,1024]{1,0:T(8,128)(2,1)S(1)} %get-tuple-element.9.own_ref), channel_id=1, source_target_pairs={{0,192},{32,224},{64,0},{96,32},{128,64},{160,96},{192,128},{224,1... | collective-permute-start | bytes 786440 | tf_op jit(solution)/shard_map/ppermute | solution.py:311
  5.7 14.5 %collective-permute-start.2 = (bf16[128,1024]{1,0:T(8,128)(2,1)S(1)}, bf16[128,1024]{1,0:T(8,128)(2,1)S(1)}, u32[]{:S(2)}, u32[]{:S(2)}) collective-permute-start(bf16[128,1024]{1,0:T(8,128)(2,1)S(1)} %get-tuple-element.9.own_ref), channel_id=1, source_target_pairs={{0,224},{32,0},{64,32},{96,64},{128,96},{160,128},{192,160},{224,1... | collective-permute-start | bytes 786440 | tf_op jit(solution)/shard_map/ppermute | solution.py:311
  7.3 13.0 %collective-permute-start.1 = (bf16[128,1024]{1,0:T(8,128)(2,1)S(1)}, bf16[128,1024]{1,0:T(8,128)(2,1)S(1)}, u32[]{:S(2)}, u32[]{:S(2)}) collective-permute-start(bf16[128,1024]{1,0:T(8,128)(2,1)S(1)} %get-tuple-element.9.own_ref), channel_id=1, source_target_pairs={{0,32},{32,64},{64,96},{96,128},{128,160},{160,192},{192,224},{224... | collective-permute-start | bytes 786440 | tf_op jit(solution)/shard_map/ppermute | solution.py:311
  7.3 13.0 %collective-permute-start = (bf16[128,1024]{1,0:T(8,128)(2,1)S(1)}, bf16[128,1024]{1,0:T(8,128)(2,1)S(1)}, u32[]{:S(2)}, u32[]{:S(2)}) collective-permute-start(bf16[128,1024]{1,0:T(8,128)(2,1)S(1)} %get-tuple-element.9.own_ref), channel_id=1, source_target_pairs={{0,64},{32,96},{64,128},{96,160},{128,192},{160,224},{192,0},{224,... | collective-permute-start | bytes 786440 | tf_op jit(solution)/shard_map/ppermute | solution.py:311
  9.6 23.0 %all-to-all-start = ((bf16[16,96,128]{2,1,0:T(8,128)(2,1)}), bf16[16,96,128]{2,1,0:T(8,128)(2,1)S(1)}, u32[]{:S(2)}, u32[]{:S(2)}) async-start(bf16[16,96,128]{2,1,0:T(8,128)(2,1)} %shard_map.85), calls=%async_computation | async-start | bytes 786432 | tf_op jit(solution)/shard_map/all_to_all | solution.py:319
  50.1 4.6 %collective-permute-start.5 = (bf16[16,32,128]{2,1,0:T(8,128)(2,1)S(1)}, bf16[16,32,128]{2,1,0:T(8,128)(2,1)S(1)}, u32[]{:S(2)}, u32[]{:S(2)}) collective-permute-start(bf16[16,32,128]{2,1,0:T(8,128)(2,1)S(1)} %all_to_all.10.mine_ref), channel_id=1, source_target_pairs={{0,1},{1,0},{2,3},{3,2},{4,5},{5,4},{6,7},{7,6},{8,9},{9,8},{10,11... | collective-permute-start | bytes 393224 | tf_op jit(solution)/shard_map/ppermute | solution.py:337

commit v3 on v2

v3 whole, which is shorter than its diff:
```python
import functools

import jax
import jax.numpy as jnp
from jax import lax
from jax.experimental import pallas as pl
from jax.experimental.pallas import tpu as pltpu
from jax.sharding import PartitionSpec as P

HEADS = 16
HEAD_DIM = 64
AXIAL_HEADS = 8
REACH = 2
EPS = 1e-05
DEAD = -1e30
PAIR = 2 * HEAD_DIM
SCALE = HEAD_DIM**-0.5
OFFSETS = (-2, -1, 1, 2)
BAND_FLOPS = 20_000_000_000
BAND_OUT_FLOPS = 20_000_000_000

VMEM = pl.BlockSpec(memory_space=pltpu.VMEM)
SMEM = pl.BlockSpec(memory_space=pltpu.SMEM)
HBM = pl.BlockSpec(memory_space=pltpu.HBM)
ANY = pl.BlockSpec(memory_space=pl.ANY)


def dot(a, b):
    return jnp.dot(a, b, preferred_element_type=jnp.float32)


def dot_t(a, b):
    return lax.dot_general(a, b, (((1,), (1,)), ((), ())), preferred_element_type=jnp.float32)


def half_roll(value):
    return pltpu.roll(value, HEAD_DIM, 1)


def low_half(shape):
    return lax.broadcasted_iota(jnp.int32, shape, 1) < HEAD_DIM


def live_count(points, tile, tiles):
    return points // tiles + (tile < points % tiles).astype(jnp.int32)


def norm_kernel(
    fields_hbm, gain_hbm, wq_hbm, wk_hbm, wv_hbm, out_ref, weights_ref, fields_ref, gain_ref, sems
):
    core = lax.rem(lax.axis_index("lon"), 2)
    width = weights_ref.shape[2]
    columns = pl.ds(pl.multiple_of(core * width, width), width)
    rows = fields_hbm.shape[0]
    slots = fields_hbm.shape[1]
    gain_copy = pltpu.make_async_copy(gain_hbm, gain_ref, sems.at[0])
    row_copies = [
        pltpu.make_async_copy(fields_hbm.at[row], fields_ref.at[row], sems.at[1 + row])
        for row in range(rows)
    ]
    rest = [
        pltpu.make_async_copy(hbm.at[:, columns], weights_ref.at[place], sems.at[1 + rows + place])
        for place, hbm in enumerate((wq_hbm, wk_hbm, wv_hbm))
    ]
    for copy in [gain_copy] + row_copies + rest:
        copy.start()
    gain_copy.wait()
    for row in range(rows):
        row_copies[row].wait()
        values = fields_ref[row]
        mean = jnp.mean(values, axis=-1, keepdims=True)
        centred = values - mean
        var = jnp.mean(centred * centred, axis=-1, keepdims=True)
        out_ref[row * slots : (row + 1) * slots, :] = (
            centred * lax.rsqrt(var + EPS) * gain_ref[...]
        ).astype(jnp.bfloat16)
    for copy in rest:
        copy.wait()


def axial_project_kernel(own_ref, peer_ref, weights_ref, out_hbm, out_ref, sems):
    tokens = own_ref.shape[0]
    items, third, _ = out_ref.shape
    slots = third // 3
    rows = tokens // slots
    heads = AXIAL_HEADS // 2
    both = jnp.concatenate([own_ref[...], peer_ref[...]], axis=0)
    low = low_half((tokens, PAIR))
    copies = []
    for part in range(3):
        result = dot(both, weights_ref[part])
        if part == 0:
            result = result.astype(jnp.bfloat16).astype(jnp.float32) * SCALE
        for pair in range(heads // 2):
            span = slice(pair * PAIR, (pair + 1) * PAIR)
            own, peer = result[:tokens, span], result[tokens:, span]
            sides = (
                jnp.where(low, own, half_roll(peer)),
                jnp.where(low, half_roll(own), peer),
            )
            for side in range(2):
                packed = sides[side].astype(jnp.bfloat16)
                for row in range(rows):
                    out_ref[row * heads + pair * 2 + side, part * slots : (part + 1) * slots, :] = (
                        packed[row * slots : (row + 1) * slots]
                    )
        block = pl.ds(part * slots, slots)
        copies.append(
            pltpu.make_async_copy(out_ref.at[:, block], out_hbm.at[:, block], sems.at[part])
        )
        copies[part].start()
    for copy in copies:
        copy.wait()


def axial_kernel(lon_count, points_ref, in_ref, after_ref, out_ref):
    lon = lax.axis_index("lon")
    core = lax.rem(lon, 2)
    chip = lon // 2
    chips, third, _ = in_ref.shape
    slots = third // 3
    heads = AXIAL_HEADS // 2
    tokens = chips * slots
    points = points_ref[lax.axis_index("lat") * (chips // heads) + chip // heads]
    slot = lax.broadcasted_iota(jnp.int32, (slots, PAIR), 0)

    def bias_of(which):
        return jnp.concatenate(
            [
                jnp.where(slot < live_count(points, 2 * place + which, lon_count), 0.0, DEAD)
                for place in range(chips)
            ],
            axis=0,
        )

    lane = lax.broadcasted_iota(jnp.int32, (tokens, PAIR), 1)
    low = lane < HEAD_DIM
    first_lane = (lane == 0).astype(jnp.float32)
    high_lane = (lane == HEAD_DIM).astype(jnp.float32)

    def part(index):
        return in_ref[:, index * slots : (index + 1) * slots, :].reshape(tokens, PAIR)

    bf16 = jnp.bfloat16
    query = part(0).astype(jnp.float32)
    key = part(1).astype(jnp.float32)
    value = part(2)
    key_own = jnp.where(low, key, high_lane * bias_of(core)).astype(bf16)
    key_peer = jnp.where(low, first_lane * bias_of(1 - core), key).astype(bf16)
    rolled = half_roll(query)
    value_rolled = half_roll(value.astype(jnp.float32)).astype(bf16)
    plain = jnp.concatenate([value, value_rolled], axis=0)
    crossed = jnp.concatenate([value_rolled, value], axis=0)
    blocks = (
        (jnp.where(low, query, high_lane), jnp.where(low, first_lane, rolled), plain),
        (jnp.where(low, rolled, high_lane), jnp.where(low, first_lane, query), crossed),
    )
    outs = []
    for for_own, for_peer, values in blocks:
        scores = jnp.concatenate(
            [dot_t(for_own.astype(bf16), key_own), dot_t(for_peer.astype(bf16), key_peer)], axis=1
        )
        weights = jnp.exp(scores - jnp.max(scores, axis=-1, keepdims=True))
        total = jnp.sum(weights, axis=-1, keepdims=True)
        outs.append(dot(weights.astype(bf16), values) / total)
    out_ref[...] = jnp.where(low, outs[0], outs[1]).astype(bf16).reshape(chips, slots, PAIR)


def band_kernel(
    lat_count, lon_count, points_ref, mask_ref, own_ref, m2_ref, m1_ref, p1_ref, p2_ref,
    wq_hbm, wk_hbm, wv_hbm, out_ref, wq_ref, wkv_ref, sems,
):
    pairs = (HEADS - AXIAL_HEADS) // 2
    first = AXIAL_HEADS * HEAD_DIM
    copies = []
    for pair in range(pairs):
        columns = pl.ds(first + pair * PAIR, PAIR)
        copies.append(
            [
                pltpu.make_async_copy(wk_hbm.at[:, columns], wkv_ref.at[pair, :, pl.ds(0, PAIR)], sems.at[pair, 0]),
                pltpu.make_async_copy(wv_hbm.at[:, columns], wkv_ref.at[pair, :, pl.ds(PAIR, PAIR)], sems.at[pair, 1]),
                pltpu.make_async_copy(wq_hbm.at[:, columns], wq_ref.at[pair], sems.at[pair, 2]),
            ]
        )
    for group in copies:
        for copy in group:
            copy.start()
    lat = lax.axis_index("lat")
    lon = lax.axis_index("lon")
    tokens = own_ref.shape[0]
    slots = 32
    rows = tokens // slots
    bands = (0,) + OFFSETS
    own = own_ref[...]
    everything = jnp.concatenate([own, m2_ref[...], m1_ref[...], p1_ref[...], p2_ref[...]], axis=0)
    keys = everything.shape[0]
    slot = lax.broadcasted_iota(jnp.int32, (slots, PAIR), 0)
    blocks = []
    for offset in bands:
        source = lat + offset
        held = jnp.clip(source, 0, lat_count - 1)
        if offset == 0:
            allowed = jnp.int32(1)
        else:
            column = offset + REACH if offset < 0 else offset + REACH - 1
            inside = (source >= 0) & (source < lat_count)
            allowed = jnp.where(inside & (mask_ref[column, lat] == 1), 1, 0)
        for row in range(rows):
            count = live_count(points_ref[held * rows + row], lon, lon_count) * allowed
            blocks.append(jnp.where(slot < count, 0.0, DEAD))
    bias = jnp.concatenate(blocks, axis=0).astype(jnp.bfloat16)
    lane_k = lax.broadcasted_iota(jnp.int32, (keys, PAIR), 1)
    lane_q = lax.broadcasted_iota(jnp.int32, (tokens, PAIR), 1)
    zero_k = jnp.zeros((keys, PAIR), jnp.bfloat16)
    low_o = lane_q < HEAD_DIM
    for pair in range(pairs):
        for copy in copies[pair]:
            copy.wait()
        kv = dot(everything, wkv_ref[pair]).astype(jnp.bfloat16)
        k, v = kv[:, :PAIR], kv[:, PAIR:]
        q = dot(own, wq_ref[pair]).astype(jnp.bfloat16) * jnp.bfloat16(SCALE)
        outs = []
        for side in range(2):
            spare = HEAD_DIM if side == 0 else 0
            mine_q = (lane_q < HEAD_DIM) if side == 0 else (lane_q >= HEAD_DIM)
            mine_k = (lane_k < HEAD_DIM) if side == 0 else (lane_k >= HEAD_DIM)
            q_side = jnp.where(mine_q, q, (lane_q == spare).astype(jnp.bfloat16))
            k_side = jnp.where(mine_k, k, jnp.where(lane_k == spare, bias, zero_k))
            scores = dot_t(q_side, k_side)
            peak = jnp.max(scores, axis=-1, keepdims=True)
            weights = jnp.exp(scores - peak)
            total = jnp.sum(weights, axis=-1, keepdims=True)
            outs.append(dot(weights.astype(jnp.bfloat16), v) / total)
        out_ref[:, pair * PAIR : (pair + 1) * PAIR] = jnp.where(low_o, outs[0], outs[1]).astype(
            jnp.bfloat16
        )


def band_out_kernel(fields_hbm, band_ref, w_hbm, out_ref, axial_w_ref, fields_ref, w_ref, sems):
    core = lax.rem(lax.axis_index("lon"), 2)
    rows, slots, width = fields_ref.shape
    depth = w_ref.shape[0]
    heads = AXIAL_HEADS // 2
    first = [
        pltpu.make_async_copy(w_hbm.at[pl.ds(depth, depth)], w_ref, sems.at[0]),
        pltpu.make_async_copy(fields_hbm, fields_ref, sems.at[1]),
    ]
    rest = []
    for head in range(heads):
        for side in range(2):
            source = (jnp.where(side == 0, core, 1 - core) * heads + head) * HEAD_DIM
            rest.append(
                pltpu.make_async_copy(
                    w_hbm.at[pl.ds(pl.multiple_of(source, HEAD_DIM), HEAD_DIM)],
                    axial_w_ref.at[pl.ds(head * PAIR + side * HEAD_DIM, HEAD_DIM)],
                    sems.at[2 + head * 2 + side],
                )
            )
    for copy in first + rest:
        copy.start()
    for copy in first:
        copy.wait()
    out_ref[...] = fields_ref[...].reshape(rows * slots, width) + dot(band_ref[...], w_ref[...])
    for copy in rest:
        copy.wait()


def finish_kernel(lon_count, points_ref, sum_ref, mine_ref, other_ref, w_ref, out_hbm, out_ref, sems):
    lon = lax.axis_index("lon")
    lat = lax.axis_index("lat")
    rows, slots, width = out_ref.shape
    heads = AXIAL_HEADS // 2
    low = low_half((slots, PAIR))
    mixed = jnp.concatenate(
        [
            jnp.concatenate(
                [
                    jnp.where(low, mine_ref[row * heads + head], other_ref[row * heads + head])
                    for head in range(heads)
                ],
                axis=1,
            )
            for row in range(rows)
        ],
        axis=0,
    )
    step = 256
    slot = lax.broadcasted_iota(jnp.int32, (slots, step), 0)
    counts = [live_count(points_ref[lat * rows + row], lon, lon_count) for row in range(rows)]
    copies = []
    for place in range(width // step):
        span = pl.ds(place * step, step)
        result = sum_ref[:, span] + dot(mixed, w_ref[:, span])
        for row in range(rows):
            out_ref[row, :, span] = jnp.where(
                slot < counts[row], result[row * slots : (row + 1) * slots], 0.0
            )
        copies.append(
            pltpu.make_async_copy(out_ref.at[:, :, span], out_hbm.at[:, :, span], sems.at[place])
        )
        copies[place].start()
    for copy in copies:
        copy.wait()


def call(kernel, shapes, specs, scratch=(), flops=0, out=VMEM):
    return pl.pallas_call(
        kernel,
        out_shape=[jax.ShapeDtypeStruct(shape, dtype) for shape, dtype in shapes],
        in_specs=specs,
        out_specs=[out] * len(shapes),
        scratch_shapes=scratch,
        compiler_params=pltpu.CompilerParams(vmem_limit_bytes=24 * 1024 * 1024),
        cost_estimate=pl.CostEstimate(flops=flops, transcendentals=0, bytes_accessed=0) if flops else None,
    )


def on_device(fields, row_points, band_mask, norm_gain, w_query, w_key, w_value, w_out):
    rows, slots, width = fields.shape
    lat_count = lax.axis_size("lat")
    lon_count = lax.axis_size("lon")
    tokens = rows * slots
    chips = lon_count // 2
    axial_width = AXIAL_HEADS * HEAD_DIM
    band_width = (HEADS - AXIAL_HEADS) * HEAD_DIM
    pairs = band_width // PAIR
    bf16, f32 = jnp.bfloat16, jnp.float32
    groups = [[2 * chip + core for chip in range(chips)] for core in range(2)]
    swap = [(place, place + 1 - 2 * (place % 2)) for place in range(lon_count)]

    def in_hbm(*arrays):
        return [pltpu.with_memory_space_constraint(array, pltpu.HBM) for array in arrays]

    normed, weights = call(
        norm_kernel,
        [((tokens, width), bf16), ((3, width, axial_width // 2), bf16)],
        [HBM] * 5,
        [
            pltpu.VMEM((rows, slots, width), f32),
            pltpu.VMEM((1, width), f32),
            pltpu.SemaphoreType.DMA((4 + rows,)),
        ],
    )(*in_hbm(fields, norm_gain.reshape(1, width), w_query, w_key, w_value))
    peer = lax.ppermute(normed, "lon", swap)
    near = [
        lax.ppermute(
            normed, "lat", [(place, (place - offset) % lat_count) for place in range(lat_count)]
        )
        for offset in OFFSETS
    ]
    (packed,) = call(
        axial_project_kernel,
        [((chips, 3 * slots, PAIR), bf16)],
        [VMEM] * 3,
        [pltpu.VMEM((chips, 3 * slots, PAIR), bf16), pltpu.SemaphoreType.DMA((3,))],
        out=ANY,
    )(normed, peer, weights)
    row_head = lax.all_to_all(packed, "lon", 0, 0, axis_index_groups=groups, tiled=True)
    (band,) = call(
        functools.partial(band_kernel, lat_count, lon_count),
        [((tokens, band_width), bf16)],
        [SMEM, SMEM] + [VMEM] * 5 + [HBM] * 3,
        [
            pltpu.VMEM((pairs, width, PAIR), bf16),
            pltpu.VMEM((pairs, width, 2 * PAIR), bf16),
            pltpu.SemaphoreType.DMA((pairs, 3)),
        ],
        BAND_FLOPS,
    )(row_points, band_mask.T, normed, *near, *in_hbm(w_query, w_key, w_value))
    summed, axial_w = call(
        band_out_kernel,
        [((tokens, width), f32), ((axial_width, width), bf16)],
        [HBM, VMEM, HBM],
        [
            pltpu.VMEM((rows, slots, width), f32),
            pltpu.VMEM((band_width, width), bf16),
            pltpu.SemaphoreType.DMA((2 + AXIAL_HEADS,)),
        ],
        BAND_OUT_FLOPS,
    )(*in_hbm(fields), band, *in_hbm(w_out))
    (axial,) = call(
        functools.partial(axial_kernel, lon_count),
        [((chips, slots, PAIR), bf16)],
        [SMEM, VMEM, ANY],
    )(row_points, row_head, summed)
    mine = lax.all_to_all(axial, "lon", 0, 0, axis_index_groups=groups, tiled=True)
    other = lax.ppermute(mine, "lon", swap)
    (out,) = call(
        functools.partial(finish_kernel, lon_count),
        [((rows, slots, width), f32)],
        [SMEM] + [VMEM] * 4,
        [pltpu.VMEM((rows, slots, width), f32), pltpu.SemaphoreType.DMA((4,))],
        out=ANY,
    )(row_points, summed, mine, other, axial_w)
    return out


def solution(mesh):
    in_specs = (P("lat", "lon", None), P(), P(), P(), P(), P(), P(), P())
    out_specs = P("lat", "lon", None)
    return jax.shard_map(
        on_device, mesh=mesh, in_specs=in_specs, out_specs=out_specs, check_vma=False
    )
```

time: 57.1 us -> 57.8 us (1.012)
  the two profiles are of different devices: /device:TPU:1 before, /device:TPU:9 now
where the time goes in v3:
time: 57.8 us; the launch traced here: 57.6 us
  starting transfers between devices  18.5 us (32%)
  blocking collectives  18.3 us (32%)
  Pallas kernels  17.4 us (30%)
  waiting for transfers between devices  3.24 us (6%)
    all_to_all x1, blocking collectives, on_device(): lax.all_to_all(axial, 'lon', 0, 0, axis_index_groups=groups, tiled=True)  18.3 us
    all_to_all x1, starting transfers between devices, on_device(): lax.all_to_all(packed, 'lon', 0, 0, axis_index_groups=groups, tiled=True)  10 us
    pallas_call x1, Pallas kernels, on_device(): call(functools.partial(band_kernel, lat_count, lon_count), [((tokens, ban...  8.37 us
    ppermute x4, starting transfers between devices, on_device(): lax.ppermute(normed, 'lat', [(place, (place - offset) % lat_count) for pl...  4.86 us
    ppermute x1, starting transfers between devices, on_device(): other = lax.ppermute(mine, 'lon', swap)  2.87 us
    pallas_call x1, Pallas kernels, on_device(): call(functools.partial(axial_kernel, lon_count), [((chips, slots, PAIR),...  2.51 us
    pallas_call x1, Pallas kernels, on_device(): call(band_out_kernel, [((tokens, width), f32), ((axial_width, width), bf1...  1.78 us
    pallas_call x1, Pallas kernels, on_device(): call(norm_kernel, [((tokens, width), bf16), ((3, width, axial_width // 2)...  1.77 us
  transfers between devices with their start and end apart: 7, of which 3 were waited for; matrix products, arithmetic and copies ran while one was open for 0% of the time, Pallas kernels for 20%

profile of v3, /device:TPU:9, one launch (start us, length us, event | category | flops | bytes accessed | tf_op | source)
XLA Modules:
  0.0 57.6 jit_solution(1538068649521559499)
XLA Ops:
  0.0 1.8 %shard_map.82 = (bf16[128,1024]{1,0:T(8,128)(2,1)S(1)}, bf16[3,1024,256]{2,1,0:T(8,128)(2,1)S(1)}) custom-call(f32[4,32,1024]{2,1,0:T(8,128)} %fields_hbm.3, f32[1,1024]{1,0:T(1,128)} %bitcast.3, bf16[1024,1024]{1,0:T(8,128)(2,1)} %wq_hbm.3, bf16[1024,1024]{1,0:T(8,128)(2,1)} %wk_hbm.3, bf16[1024,1024]{1,0:T(8,128)(2,1)} %wv_hbm.3), custom_call_target="tpu_custom_call" | custom-call | tf_op jit(solution)/shard_map/pallas_call | solution.py:334
  1.8 0.0 copy-start
  1.8 0.0 copy-start.1
  1.8 0.8 %collective-permute-start.4 = (bf16[128,1024]{1,0:T(8,128)(2,1)S(1)}, bf16[128,1024]{1,0:T(8,128)(2,1)S(1)}, u32[]{:S(2)}, u32[]{:S(2)}) collective-permute-start(bf16[128,1024]{1,0:T(8,128)(2,1)S(1)} %get-tuple-element.9.own_ref), channel_id=1, source_target_pairs={{0,1},{1,0},{2,3},{3,2},{4,5},{5,4},{6,7},{7,6},{8,9},{9,8},{10,11... | collective-permute-start | bytes 786440 | tf_op jit(solution)/shard_map/ppermute | solution.py:344
  2.6 2.5 %collective-permute-start.3 = (bf16[128,1024]{1,0:T(8,128)(2,1)S(1)}, bf16[128,1024]{1,0:T(8,128)(2,1)S(1)}, u32[]{:S(2)}, u32[]{:S(2)}) collective-permute-start(bf16[128,1024]{1,0:T(8,128)(2,1)S(1)} %get-tuple-element.9.own_ref), channel_id=1, source_target_pairs={{0,192},{32,224},{64,0},{96,32},{128,64},{160,96},{192,128},{224,1... | collective-permute-start | bytes 786440 | tf_op jit(solution)/shard_map/ppermute | solution.py:346
  5.1 0.2 collective-permute-start.2
  5.2 2.2 %collective-permute-start.1 = (bf16[128,1024]{1,0:T(8,128)(2,1)S(1)}, bf16[128,1024]{1,0:T(8,128)(2,1)S(1)}, u32[]{:S(2)}, u32[]{:S(2)}) collective-permute-start(bf16[128,1024]{1,0:T(8,128)(2,1)S(1)} %get-tuple-element.9.own_ref), channel_id=1, source_target_pairs={{0,32},{32,64},{64,96},{96,128},{128,160},{160,192},{192,224},{224... | collective-permute-start | bytes 786440 | tf_op jit(solution)/shard_map/ppermute | solution.py:346
  7.4 0.0 collective-permute-start
  7.4 0.0 collective-permute-done.4.peer_ref
  7.4 1.4 %shard_map.85 = bf16[16,96,128]{2,1,0:T(8,128)(2,1)} custom-call(bf16[128,1024]{1,0:T(8,128)(2,1)S(1)} %get-tuple-element.9.own_ref, bf16[128,1024]{1,0:T(8,128)(2,1)S(1)} %collective-permute-done.4.peer_ref, bf16[3,1024,256]{2,1,0:T(8,128)(2,1)S(1)} %get-tuple-element.11.weights_ref), custom_call_target="tpu_custom_call" | custom-call | tf_op jit(solution)/shard_map/pallas_call | solution.py:351
  8.8 10.0 %all-to-all-start = ((bf16[16,96,128]{2,1,0:T(8,128)(2,1)}), bf16[16,96,128]{2,1,0:T(8,128)(2,1)S(1)}, u32[]{:S(2)}, u32[]{:S(2)}) async-start(bf16[16,96,128]{2,1,0:T(8,128)(2,1)} %shard_map.85), calls=%async_computation | async-start | bytes 786432 | tf_op jit(solution)/shard_map/all_to_all | solution.py:358
  18.9 0.0 collective-permute-done.3.p2_ref
  18.9 0.0 collective-permute-done.2.p1_ref
  18.9 0.0 collective-permute-done.1.m1_ref
  18.9 1.7 %collective-permute-done.m2_ref = bf16[128,1024]{1,0:T(8,128)(2,1)S(1)} collective-permute-done((bf16[128,1024]{1,0:T(8,128)(2,1)S(1)}, bf16[128,1024]{1,0:T(8,128)(2,1)S(1)}, u32[]{:S(2)}, u32[]{:S(2)}) %collective-permute-start) | collective-permute-done | bytes 262176 | tf_op jit(solution)/shard_map/ppermute | solution.py:346
  20.6 0.0 copy-done
  20.6 0.0 copy-done.1
  20.6 8.4 %shard_map.83.band_ref = bf16[128,512]{1,0:T(8,128)(2,1)S(1)} custom-call(s32[32]{0:T(128)S(1)} %copy-done, s32[4,8]{1,0:T(4,128)S(1)} %bitcast.2, bf16[128,1024]{1,0:T(8,128)(2,1)S(1)} %get-tuple-element.9.own_ref, bf16[128,1024]{1,0:T(8,128)(2,1)S(1)} %collective-permute-done.m2_ref, bf16[128,1024]{1,0:T(8,128)(2,1)S(1)} %collective-permute-done.1.m1_ref, ...), custom_call_target="tpu_custom_call" | custom-call | flops 20000000000 | tf_op jit(solution)/shard_map/pallas_call | solution.py:359
  29.0 1.8 %shard_map.84 = (f32[128,1024]{1,0:T(8,128)S(1)}, bf16[512,1024]{1,0:T(8,128)(2,1)S(1)}) custom-call(f32[4,32,1024]{2,1,0:T(8,128)} %fields_hbm.3, bf16[128,512]{1,0:T(8,128)(2,1)S(1)} %shard_map.83.band_ref, bf16[1024,1024]{1,0:T(8,128)(2,1)} %w_hbm.1), custom_call_target="tpu_custom_call" | custom-call | flops 20000000000 | tf_op jit(solution)/shard_map/pallas_call | solution.py:370
  30.8 0.5 all-to-all-done.in_ref
  31.3 2.5 %shard_map.86 = bf16[16,32,128]{2,1,0:T(8,128)(2,1)S(1)} custom-call(s32[32]{0:T(128)S(1)} %copy-done, bf16[16,96,128]{2,1,0:T(8,128)(2,1)S(1)} %all-to-all-done.in_ref, f32[128,1024]{1,0:T(8,128)S(1)} %get-tuple-element.10.after_ref.sum_ref), custom_call_target="tpu_custom_call" | custom-call | tf_op jit(solution)/shard_map/pallas_call | solution.py:381
  33.8 18.3 %all_to_all.10.mine_ref = bf16[16,32,128]{2,1,0:T(8,128)(2,1)S(1)} all-to-all(bf16[16,32,128]{2,1,0:T(8,128)(2,1)S(1)} %shard_map.86), channel_id=1, replica_groups={{0,2,4,6,8,10,12,14,16,18,20,22,24,26,28,30},{1,3,5,7,9,11,13,15,17,19,..., dimensions={0} | all-to-all | bytes 262144 | tf_op jit(solution)/shard_map/all_to_all | solution.py:386
  52.1 2.9 %collective-permute-start.5 = (bf16[16,32,128]{2,1,0:T(8,128)(2,1)S(1)}, bf16[16,32,128]{2,1,0:T(8,128)(2,1)S(1)}, u32[]{:S(2)}, u32[]{:S(2)}) collective-permute-start(bf16[16,32,128]{2,1,0:T(8,128)(2,1)S(1)} %all_to_all.10.mine_ref), channel_id=1, source_target_pairs={{0,1},{1,0},{2,3},{3,2},{4,5},{5,4},{6,7},{7,6},{8,9},{9,8},{10,11... | collective-permute-start | bytes 393224 | tf_op jit(solution)/shard_map/ppermute | solution.py:387
  55.0 1.0 %collective-permute-done.5.other_ref = bf16[16,32,128]{2,1,0:T(8,128)(2,1)S(1)} collective-permute-done((bf16[16,32,128]{2,1,0:T(8,128)(2,1)S(1)}, bf16[16,32,128]{2,1,0:T(8,128)(2,1)S(1)}, u32[]{:S(2)}, u32[]{:S(2)}) %collective-permute-start.5) | collective-permute-done | bytes 131104 | tf_op jit(solution)/shard_map/ppermute | solution.py:387
  56.0 1.6 %shard_map.87 = f32[4,32,1024]{2,1,0:T(8,128)} custom-call(s32[32]{0:T(128)S(1)} %copy-done, f32[128,1024]{1,0:T(8,128)S(1)} %get-tuple-element.10.after_ref.sum_ref, bf16[16,32,128]{2,1,0:T(8,128)(2,1)S(1)} %all_to_all.10.mine_ref, bf16[16,32,128]{2,1,0:T(8,128)(2,1)S(1)} %collective-permute-done.5.other_ref, bf16[512,1024]{1,0:T(8,128)(2,1)S(1)} %get-tuple-element.12.w_ref), custom_call_target="tpu_custom_call" | custom-call | tf_op jit(solution)/shard_map/pallas_call | solution.py:388
Async XLA Ops:
  1.8 18.8 %copy-start = (s32[32]{0:T(128)S(1)}, s32[32]{0:T(128)}, u32[]{:S(2)}) copy-start(s32[32]{0:T(128)} %points_ref.5) | copy-start | bytes 388
  1.8 18.8 %copy-start.1 = (s32[8,4]{0,1:T(4,128)S(1)}, s32[8,4]{0,1:T(4,128)}, u32[]{:S(2)}) copy-start(s32[8,4]{0,1:T(4,128)} %param.10) | copy-start | bytes 388
  1.8 5.6 %collective-permute-start.4 = (bf16[128,1024]{1,0:T(8,128)(2,1)S(1)}, bf16[128,1024]{1,0:T(8,128)(2,1)S(1)}, u32[]{:S(2)}, u32[]{:S(2)}) collective-permute-start(bf16[128,1024]{1,0:T(8,128)(2,1)S(1)} %get-tuple-element.9.own_ref), channel_id=1, source_target_pairs={{0,1},{1,0},{2,3},{3,2},{4,5},{5,4},{6,7},{7,6},{8,9},{9,8},{10,11... | collective-permute-start | bytes 786440 | tf_op jit(solution)/shard_map/ppermute | solution.py:344
  2.6 16.3 %collective-permute-start.3 = (bf16[128,1024]{1,0:T(8,128)(2,1)S(1)}, bf16[128,1024]{1,0:T(8,128)(2,1)S(1)}, u32[]{:S(2)}, u32[]{:S(2)}) collective-permute-start(bf16[128,1024]{1,0:T(8,128)(2,1)S(1)} %get-tuple-element.9.own_ref), channel_id=1, source_target_pairs={{0,192},{32,224},{64,0},{96,32},{128,64},{160,96},{192,128},{224,1... | collective-permute-start | bytes 786440 | tf_op jit(solution)/shard_map/ppermute | solution.py:346
  5.1 13.8 %collective-permute-start.2 = (bf16[128,1024]{1,0:T(8,128)(2,1)S(1)}, bf16[128,1024]{1,0:T(8,128)(2,1)S(1)}, u32[]{:S(2)}, u32[]{:S(2)}) collective-permute-start(bf16[128,1024]{1,0:T(8,128)(2,1)S(1)} %get-tuple-element.9.own_ref), channel_id=1, source_target_pairs={{0,224},{32,0},{64,32},{96,64},{128,96},{160,128},{192,160},{224,1... | collective-permute-start | bytes 786440 | tf_op jit(solution)/shard_map/ppermute | solution.py:346
  5.2 13.6 %collective-permute-start.1 = (bf16[128,1024]{1,0:T(8,128)(2,1)S(1)}, bf16[128,1024]{1,0:T(8,128)(2,1)S(1)}, u32[]{:S(2)}, u32[]{:S(2)}) collective-permute-start(bf16[128,1024]{1,0:T(8,128)(2,1)S(1)} %get-tuple-element.9.own_ref), channel_id=1, source_target_pairs={{0,32},{32,64},{64,96},{96,128},{128,160},{160,192},{192,224},{224... | collective-permute-start | bytes 786440 | tf_op jit(solution)/shard_map/ppermute | solution.py:346
  7.4 13.2 %collective-permute-start = (bf16[128,1024]{1,0:T(8,128)(2,1)S(1)}, bf16[128,1024]{1,0:T(8,128)(2,1)S(1)}, u32[]{:S(2)}, u32[]{:S(2)}) collective-permute-start(bf16[128,1024]{1,0:T(8,128)(2,1)S(1)} %get-tuple-element.9.own_ref), channel_id=1, source_target_pairs={{0,64},{32,96},{64,128},{96,160},{128,192},{160,224},{192,0},{224,... | collective-permute-start | bytes 786440 | tf_op jit(solution)/shard_map/ppermute | solution.py:346
  8.8 22.5 %all-to-all-start = ((bf16[16,96,128]{2,1,0:T(8,128)(2,1)}), bf16[16,96,128]{2,1,0:T(8,128)(2,1)S(1)}, u32[]{:S(2)}, u32[]{:S(2)}) async-start(bf16[16,96,128]{2,1,0:T(8,128)(2,1)} %shard_map.85), calls=%async_computation | async-start | bytes 786432 | tf_op jit(solution)/shard_map/all_to_all | solution.py:358
  52.1 3.9 %collective-permute-start.5 = (bf16[16,32,128]{2,1,0:T(8,128)(2,1)S(1)}, bf16[16,32,128]{2,1,0:T(8,128)(2,1)S(1)}, u32[]{:S(2)}, u32[]{:S(2)}) collective-permute-start(bf16[16,32,128]{2,1,0:T(8,128)(2,1)S(1)} %all_to_all.10.mine_ref), channel_id=1, source_target_pairs={{0,1},{1,0},{2,3},{3,2},{4,5},{5,4},{6,7},{7,6},{8,9},{9,8},{10,11... | collective-permute-start | bytes 393224 | tf_op jit(solution)/shard_map/ppermute | solution.py:387

commit v4 on v3

--- a/solution.py
+++ b/solution.py
@@ -168,35 +168,28 @@
 
 def band_kernel(
     lat_count, lon_count, points_ref, mask_ref, own_ref, m2_ref, m1_ref, p1_ref, p2_ref,
-    wq_hbm, wk_hbm, wv_hbm, out_ref, wq_ref, wkv_ref, sems,
+    wq_hbm, wk_hbm, wv_hbm, out_ref, weights_ref, sems,
 ):
-    pairs = (HEADS - AXIAL_HEADS) // 2
     first = AXIAL_HEADS * HEAD_DIM
-    copies = []
-    for pair in range(pairs):
-        columns = pl.ds(first + pair * PAIR, PAIR)
-        copies.append(
-            [
-                pltpu.make_async_copy(wk_hbm.at[:, columns], wkv_ref.at[pair, :, pl.ds(0, PAIR)], sems.at[pair, 0]),
-                pltpu.make_async_copy(wv_hbm.at[:, columns], wkv_ref.at[pair, :, pl.ds(PAIR, PAIR)], sems.at[pair, 1]),
-                pltpu.make_async_copy(wq_hbm.at[:, columns], wq_ref.at[pair], sems.at[pair, 2]),
-            ]
-        )
-    for group in copies:
-        for copy in group:
-            copy.start()
+    columns = pl.ds(first, weights_ref.shape[2])
+    copies = [
+        pltpu.make_async_copy(hbm.at[:, columns], weights_ref.at[place], sems.at[place])
+        for place, hbm in enumerate((wk_hbm, wv_hbm, wq_hbm))
+    ]
+    for copy in copies:
+        copy.start()
     lat = lax.axis_index("lat")
     lon = lax.axis_index("lon")
     tokens = own_ref.shape[0]
     slots = 32
     rows = tokens // slots
-    bands = (0,) + OFFSETS
+    bf16 = jnp.bfloat16
     own = own_ref[...]
     everything = jnp.concatenate([own, m2_ref[...], m1_ref[...], p1_ref[...], p2_ref[...]], axis=0)
     keys = everything.shape[0]
     slot = lax.broadcasted_iota(jnp.int32, (slots, PAIR), 0)
     blocks = []
-    for offset in bands:
+    for offset in (0,) + OFFSETS:
         source = lat + offset
         held = jnp.clip(source, 0, lat_count - 1)
         if offset == 0:
@@ -208,32 +201,34 @@
         for row in range(rows):
             count = live_count(points_ref[held * rows + row], lon, lon_count) * allowed
             blocks.append(jnp.where(slot < count, 0.0, DEAD))
-    bias = jnp.concatenate(blocks, axis=0).astype(jnp.bfloat16)
+    bias = jnp.concatenate(blocks, axis=0)
     lane_k = lax.broadcasted_iota(jnp.int32, (keys, PAIR), 1)
     lane_q = lax.broadcasted_iota(jnp.int32, (tokens, PAIR), 1)
-    zero_k = jnp.zeros((keys, PAIR), jnp.bfloat16)
-    low_o = lane_q < HEAD_DIM
-    for pair in range(pairs):
-        for copy in copies[pair]:
-            copy.wait()
-        kv = dot(everything, wkv_ref[pair]).astype(jnp.bfloat16)
-        k, v = kv[:, :PAIR], kv[:, PAIR:]
-        q = dot(own, wq_ref[pair]).astype(jnp.bfloat16) * jnp.bfloat16(SCALE)
-        outs = []
-        for side in range(2):
-            spare = HEAD_DIM if side == 0 else 0
-            mine_q = (lane_q < HEAD_DIM) if side == 0 else (lane_q >= HEAD_DIM)
-            mine_k = (lane_k < HEAD_DIM) if side == 0 else (lane_k >= HEAD_DIM)
-            q_side = jnp.where(mine_q, q, (lane_q == spare).astype(jnp.bfloat16))
-            k_side = jnp.where(mine_k, k, jnp.where(lane_k == spare, bias, zero_k))
-            scores = dot_t(q_side, k_side)
-            peak = jnp.max(scores, axis=-1, keepdims=True)
-            weights = jnp.exp(scores - peak)
-            total = jnp.sum(weights, axis=-1, keepdims=True)
-            outs.append(dot(weights.astype(jnp.bfloat16), v) / total)
-        out_ref[:, pair * PAIR : (pair + 1) * PAIR] = jnp.where(low_o, outs[0], outs[1]).astype(
-            jnp.bfloat16
-        )
+    low_k, low_q = lane_k < HEAD_DIM, lane_q < HEAD_DIM
+    bias_high = jnp.where(lane_k == HEAD_DIM, bias, 0.0).astype(bf16)
+    bias_low = jnp.where(lane_k == 0, bias, 0.0).astype(bf16)
+    one_high = (lane_q == HEAD_DIM).astype(bf16)
+    one_low = (lane_q == 0).astype(bf16)
+    copies[0].wait()
+    key = dot(everything, weights_ref[0]).astype(bf16)
+    copies[1].wait()
+    value = dot(everything, weights_ref[1]).astype(bf16)
+    copies[2].wait()
+    query = dot(own, weights_ref[2]).astype(bf16) * bf16(SCALE)
+    for pair in range((HEADS - AXIAL_HEADS) // 2):
+        span = slice(pair * PAIR, (pair + 1) * PAIR)
+        q, k, v = query[:, span], key[:, span], value[:, span]
+        scores = jnp.concatenate(
+            [
+                dot_t(jnp.where(low_q, q, one_high), jnp.where(low_k, k, bias_high)),
+                dot_t(jnp.where(low_q, one_low, q), jnp.where(low_k, bias_low, k)),
+            ],
+            axis=0,
+        )
+        weights = jnp.exp(scores - jnp.max(scores, axis=-1, keepdims=True))
+        total = jnp.sum(weights, axis=-1, keepdims=True)
+        mixed = dot(weights.astype(bf16), v) / total
+        out_ref[:, span] = jnp.where(low_q, mixed[:tokens], mixed[tokens:]).astype(bf16)
 
 
 def band_out_kernel(fields_hbm, band_ref, w_hbm, out_ref, axial_w_ref, fields_ref, w_ref, sems):
@@ -323,7 +318,6 @@
     chips = lon_count // 2
     axial_width = AXIAL_HEADS * HEAD_DIM
     band_width = (HEADS - AXIAL_HEADS) * HEAD_DIM
-    pairs = band_width // PAIR
     bf16, f32 = jnp.bfloat16, jnp.float32
     groups = [[2 * chip + core for chip in range(chips)] for core in range(2)]
     swap = [(place, place + 1 - 2 * (place % 2)) for place in range(lon_count)]
@@ -361,9 +355,8 @@
         [((tokens, band_width), bf16)],
         [SMEM, SMEM] + [VMEM] * 5 + [HBM] * 3,
         [
-            pltpu.VMEM((pairs, width, PAIR), bf16),
-            pltpu.VMEM((pairs, width, 2 * PAIR), bf16),
-            pltpu.SemaphoreType.DMA((pairs, 3)),
+            pltpu.VMEM((3, width, band_width), bf16),
+            pltpu.SemaphoreType.DMA((3,)),
         ],
         BAND_FLOPS,
     )(row_points, band_mask.T, normed, *near, *in_hbm(w_query, w_key, w_value))

time: 57.8 us -> 55.5 us (0.960)
  the two profiles are of different devices: /device:TPU:9 before, /device:TPU:1 now
where the time goes in v4:
time: 55.5 us; the launch traced here: 55.3 us
  starting transfers between devices  20.1 us (36%)
  Pallas kernels  14.5 us (26%)
  blocking collectives  14.5 us (26%)
  waiting for transfers between devices  5.99 us (11%)
    all_to_all x1, blocking collectives, on_device(): lax.all_to_all(axial, 'lon', 0, 0, axis_index_groups=groups, tiled=True)  14.5 us
    all_to_all x1, starting transfers between devices, on_device(): lax.all_to_all(packed, 'lon', 0, 0, axis_index_groups=groups, tiled=True)  10.6 us
    pallas_call x1, Pallas kernels, on_device(): call(functools.partial(band_kernel, lat_count, lon_count), [((tokens, ban...  5.51 us
    all_to_all x1, waiting for transfers between devices, on_device(): lax.all_to_all(packed, 'lon', 0, 0, axis_index_groups=groups, tiled=True)  5 us
    ppermute x1, starting transfers between devices, on_device(): peer = lax.ppermute(normed, 'lon', swap)  3.33 us
    ppermute x4, starting transfers between devices, on_device(): lax.ppermute(normed, 'lat', [(place, (place - offset) % lat_count) for pl...  3.24 us
    ppermute x1, starting transfers between devices, on_device(): other = lax.ppermute(mine, 'lon', swap)  2.87 us
    pallas_call x1, Pallas kernels, on_device(): call(functools.partial(axial_kernel, lon_count), [((chips, slots, PAIR),...  2.51 us
  transfers between devices with their start and end apart: 7, of which 2 were waited for; matrix products, arithmetic and copies ran while one was open for 0% of the time, Pallas kernels for 16%

profile of v4, /device:TPU:1, one launch (start us, length us, event | category | flops | bytes accessed | tf_op | source)
XLA Modules:
  0.0 55.3 jit_solution(7006615149975127374)
XLA Ops:
  0.0 1.8 %shard_map.82 = (bf16[128,1024]{1,0:T(8,128)(2,1)S(1)}, bf16[3,1024,256]{2,1,0:T(8,128)(2,1)S(1)}) custom-call(f32[4,32,1024]{2,1,0:T(8,128)} %fields_hbm.3, f32[1,1024]{1,0:T(1,128)} %bitcast.3, bf16[1024,1024]{1,0:T(8,128)(2,1)} %wq_hbm.3, bf16[1024,1024]{1,0:T(8,128)(2,1)} %wk_hbm.3, bf16[1024,1024]{1,0:T(8,128)(2,1)} %wv_hbm.3), custom_call_target="tpu_custom_call" | custom-call | tf_op jit(solution)/shard_map/pallas_call | solution.py:328
  1.8 0.0 copy-start
  1.8 0.0 copy-start.1
  1.8 3.3 %collective-permute-start.4 = (bf16[128,1024]{1,0:T(8,128)(2,1)S(1)}, bf16[128,1024]{1,0:T(8,128)(2,1)S(1)}, u32[]{:S(2)}, u32[]{:S(2)}) collective-permute-start(bf16[128,1024]{1,0:T(8,128)(2,1)S(1)} %get-tuple-element.9.own_ref), channel_id=1, source_target_pairs={{0,1},{1,0},{2,3},{3,2},{4,5},{5,4},{6,7},{7,6},{8,9},{9,8},{10,11... | collective-permute-start | bytes 786440 | tf_op jit(solution)/shard_map/ppermute | solution.py:338
  5.1 0.8 %collective-permute-start.3 = (bf16[128,1024]{1,0:T(8,128)(2,1)S(1)}, bf16[128,1024]{1,0:T(8,128)(2,1)S(1)}, u32[]{:S(2)}, u32[]{:S(2)}) collective-permute-start(bf16[128,1024]{1,0:T(8,128)(2,1)S(1)} %get-tuple-element.9.own_ref), channel_id=1, source_target_pairs={{0,192},{32,224},{64,0},{96,32},{128,64},{160,96},{192,128},{224,1... | collective-permute-start | bytes 786440 | tf_op jit(solution)/shard_map/ppermute | solution.py:340
  5.9 1.6 %collective-permute-start.2 = (bf16[128,1024]{1,0:T(8,128)(2,1)S(1)}, bf16[128,1024]{1,0:T(8,128)(2,1)S(1)}, u32[]{:S(2)}, u32[]{:S(2)}) collective-permute-start(bf16[128,1024]{1,0:T(8,128)(2,1)S(1)} %get-tuple-element.9.own_ref), channel_id=1, source_target_pairs={{0,224},{32,0},{64,32},{96,64},{128,96},{160,128},{192,160},{224,1... | collective-permute-start | bytes 786440 | tf_op jit(solution)/shard_map/ppermute | solution.py:340
  7.5 0.0 collective-permute-start.1
  7.5 0.9 %collective-permute-start = (bf16[128,1024]{1,0:T(8,128)(2,1)S(1)}, bf16[128,1024]{1,0:T(8,128)(2,1)S(1)}, u32[]{:S(2)}, u32[]{:S(2)}) collective-permute-start(bf16[128,1024]{1,0:T(8,128)(2,1)S(1)} %get-tuple-element.9.own_ref), channel_id=1, source_target_pairs={{0,64},{32,96},{64,128},{96,160},{128,192},{160,224},{192,0},{224,... | collective-permute-start | bytes 786440 | tf_op jit(solution)/shard_map/ppermute | solution.py:340
  8.4 0.0 collective-permute-done.4.peer_ref
  8.4 1.4 %shard_map.85 = bf16[16,96,128]{2,1,0:T(8,128)(2,1)} custom-call(bf16[128,1024]{1,0:T(8,128)(2,1)S(1)} %get-tuple-element.9.own_ref, bf16[128,1024]{1,0:T(8,128)(2,1)S(1)} %collective-permute-done.4.peer_ref, bf16[3,1024,256]{2,1,0:T(8,128)(2,1)S(1)} %get-tuple-element.11.weights_ref), custom_call_target="tpu_custom_call" | custom-call | tf_op jit(solution)/shard_map/pallas_call | solution.py:345
  9.8 10.6 %all-to-all-start = ((bf16[16,96,128]{2,1,0:T(8,128)(2,1)}), bf16[16,96,128]{2,1,0:T(8,128)(2,1)S(1)}, u32[]{:S(2)}, u32[]{:S(2)}) async-start(bf16[16,96,128]{2,1,0:T(8,128)(2,1)} %shard_map.85), calls=%async_computation | async-start | bytes 786432 | tf_op jit(solution)/shard_map/all_to_all | solution.py:352
  20.4 0.0 collective-permute-done.3.p2_ref
  20.4 0.0 collective-permute-done.2.p1_ref
  20.4 0.0 collective-permute-done.1.m1_ref
  20.4 0.0 collective-permute-done.m2_ref
  20.4 0.0 copy-done
  20.5 0.0 copy-done.1
  20.5 5.5 %shard_map.83.band_ref = bf16[128,512]{1,0:T(8,128)(2,1)S(1)} custom-call(s32[32]{0:T(128)S(1)} %copy-done, s32[4,8]{1,0:T(4,128)S(1)} %bitcast.2, bf16[128,1024]{1,0:T(8,128)(2,1)S(1)} %get-tuple-element.9.own_ref, bf16[128,1024]{1,0:T(8,128)(2,1)S(1)} %collective-permute-done.m2_ref, bf16[128,1024]{1,0:T(8,128)(2,1)S(1)} %collective-permute-done.1.m1_ref, ...), custom_call_target="tpu_custom_call" | custom-call | flops 20000000000 | tf_op jit(solution)/shard_map/pallas_call | solution.py:353
  26.0 1.8 %shard_map.84 = (f32[128,1024]{1,0:T(8,128)S(1)}, bf16[512,1024]{1,0:T(8,128)(2,1)S(1)}) custom-call(f32[4,32,1024]{2,1,0:T(8,128)} %fields_hbm.3, bf16[128,512]{1,0:T(8,128)(2,1)S(1)} %shard_map.83.band_ref, bf16[1024,1024]{1,0:T(8,128)(2,1)} %w_hbm.1), custom_call_target="tpu_custom_call" | custom-call | flops 20000000000 | tf_op jit(solution)/shard_map/pallas_call | solution.py:363
  27.8 5.0 %all-to-all-done.in_ref = bf16[16,96,128]{2,1,0:T(8,128)(2,1)S(1)} async-done(((bf16[16,96,128]{2,1,0:T(8,128)(2,1)}), bf16[16,96,128]{2,1,0:T(8,128)(2,1)S(1)}, u32[]{:S(2)}, u32[]{:S(2)}) %all-to-all-start) | async-done | bytes 393248 | tf_op jit(solution)/shard_map/all_to_all | solution.py:352
  32.8 2.5 %shard_map.86 = bf16[16,32,128]{2,1,0:T(8,128)(2,1)S(1)} custom-call(s32[32]{0:T(128)S(1)} %copy-done, bf16[16,96,128]{2,1,0:T(8,128)(2,1)S(1)} %all-to-all-done.in_ref, f32[128,1024]{1,0:T(8,128)S(1)} %get-tuple-element.10.after_ref.sum_ref), custom_call_target="tpu_custom_call" | custom-call | tf_op jit(solution)/shard_map/pallas_call | solution.py:374
  35.3 14.5 %all_to_all.10.mine_ref = bf16[16,32,128]{2,1,0:T(8,128)(2,1)S(1)} all-to-all(bf16[16,32,128]{2,1,0:T(8,128)(2,1)S(1)} %shard_map.86), channel_id=1, replica_groups={{0,2,4,6,8,10,12,14,16,18,20,22,24,26,28,30},{1,3,5,7,9,11,13,15,17,19,..., dimensions={0} | all-to-all | bytes 262144 | tf_op jit(solution)/shard_map/all_to_all | solution.py:379
  49.8 2.9 %collective-permute-start.5 = (bf16[16,32,128]{2,1,0:T(8,128)(2,1)S(1)}, bf16[16,32,128]{2,1,0:T(8,128)(2,1)S(1)}, u32[]{:S(2)}, u32[]{:S(2)}) collective-permute-start(bf16[16,32,128]{2,1,0:T(8,128)(2,1)S(1)} %all_to_all.10.mine_ref), channel_id=1, source_target_pairs={{0,1},{1,0},{2,3},{3,2},{4,5},{5,4},{6,7},{7,6},{8,9},{9,8},{10,11... | collective-permute-start | bytes 393224 | tf_op jit(solution)/shard_map/ppermute | solution.py:380
  52.7 1.0 %collective-permute-done.5.other_ref = bf16[16,32,128]{2,1,0:T(8,128)(2,1)S(1)} collective-permute-done((bf16[16,32,128]{2,1,0:T(8,128)(2,1)S(1)}, bf16[16,32,128]{2,1,0:T(8,128)(2,1)S(1)}, u32[]{:S(2)}, u32[]{:S(2)}) %collective-permute-start.5) | collective-permute-done | bytes 131104 | tf_op jit(solution)/shard_map/ppermute | solution.py:380
  53.7 1.6 %shard_map.87 = f32[4,32,1024]{2,1,0:T(8,128)} custom-call(s32[32]{0:T(128)S(1)} %copy-done, f32[128,1024]{1,0:T(8,128)S(1)} %get-tuple-element.10.after_ref.sum_ref, bf16[16,32,128]{2,1,0:T(8,128)(2,1)S(1)} %all_to_all.10.mine_ref, bf16[16,32,128]{2,1,0:T(8,128)(2,1)S(1)} %collective-permute-done.5.other_ref, bf16[512,1024]{1,0:T(8,128)(2,1)S(1)} %get-tuple-element.12.w_ref), custom_call_target="tpu_custom_call" | custom-call | tf_op jit(solution)/shard_map/pallas_call | solution.py:381
Async XLA Ops:
  1.8 18.7 %copy-start = (s32[32]{0:T(128)S(1)}, s32[32]{0:T(128)}, u32[]{:S(2)}) copy-start(s32[32]{0:T(128)} %points_ref.5) | copy-start | bytes 388
  1.8 18.7 %copy-start.1 = (s32[8,4]{0,1:T(4,128)S(1)}, s32[8,4]{0,1:T(4,128)}, u32[]{:S(2)}) copy-start(s32[8,4]{0,1:T(4,128)} %param.10) | copy-start | bytes 388
  1.8 6.6 %collective-permute-start.4 = (bf16[128,1024]{1,0:T(8,128)(2,1)S(1)}, bf16[128,1024]{1,0:T(8,128)(2,1)S(1)}, u32[]{:S(2)}, u32[]{:S(2)}) collective-permute-start(bf16[128,1024]{1,0:T(8,128)(2,1)S(1)} %get-tuple-element.9.own_ref), channel_id=1, source_target_pairs={{0,1},{1,0},{2,3},{3,2},{4,5},{5,4},{6,7},{7,6},{8,9},{9,8},{10,11... | collective-permute-start | bytes 786440 | tf_op jit(solution)/shard_map/ppermute | solution.py:338
  5.1 15.3 %collective-permute-start.3 = (bf16[128,1024]{1,0:T(8,128)(2,1)S(1)}, bf16[128,1024]{1,0:T(8,128)(2,1)S(1)}, u32[]{:S(2)}, u32[]{:S(2)}) collective-permute-start(bf16[128,1024]{1,0:T(8,128)(2,1)S(1)} %get-tuple-element.9.own_ref), channel_id=1, source_target_pairs={{0,192},{32,224},{64,0},{96,32},{128,64},{160,96},{192,128},{224,1... | collective-permute-start | bytes 786440 | tf_op jit(solution)/shard_map/ppermute | solution.py:340
  5.9 14.5 %collective-permute-start.2 = (bf16[128,1024]{1,0:T(8,128)(2,1)S(1)}, bf16[128,1024]{1,0:T(8,128)(2,1)S(1)}, u32[]{:S(2)}, u32[]{:S(2)}) collective-permute-start(bf16[128,1024]{1,0:T(8,128)(2,1)S(1)} %get-tuple-element.9.own_ref), channel_id=1, source_target_pairs={{0,224},{32,0},{64,32},{96,64},{128,96},{160,128},{192,160},{224,1... | collective-permute-start | bytes 786440 | tf_op jit(solution)/shard_map/ppermute | solution.py:340
  7.5 13.0 %collective-permute-start.1 = (bf16[128,1024]{1,0:T(8,128)(2,1)S(1)}, bf16[128,1024]{1,0:T(8,128)(2,1)S(1)}, u32[]{:S(2)}, u32[]{:S(2)}) collective-permute-start(bf16[128,1024]{1,0:T(8,128)(2,1)S(1)} %get-tuple-element.9.own_ref), channel_id=1, source_target_pairs={{0,32},{32,64},{64,96},{96,128},{128,160},{160,192},{192,224},{224... | collective-permute-start | bytes 786440 | tf_op jit(solution)/shard_map/ppermute | solution.py:340
  7.5 13.0 %collective-permute-start = (bf16[128,1024]{1,0:T(8,128)(2,1)S(1)}, bf16[128,1024]{1,0:T(8,128)(2,1)S(1)}, u32[]{:S(2)}, u32[]{:S(2)}) collective-permute-start(bf16[128,1024]{1,0:T(8,128)(2,1)S(1)} %get-tuple-element.9.own_ref), channel_id=1, source_target_pairs={{0,64},{32,96},{64,128},{96,160},{128,192},{160,224},{192,0},{224,... | collective-permute-start | bytes 786440 | tf_op jit(solution)/shard_map/ppermute | solution.py:340
  9.8 23.0 %all-to-all-start = ((bf16[16,96,128]{2,1,0:T(8,128)(2,1)}), bf16[16,96,128]{2,1,0:T(8,128)(2,1)S(1)}, u32[]{:S(2)}, u32[]{:S(2)}) async-start(bf16[16,96,128]{2,1,0:T(8,128)(2,1)} %shard_map.85), calls=%async_computation | async-start | bytes 786432 | tf_op jit(solution)/shard_map/all_to_all | solution.py:352
  49.8 3.9 %collective-permute-start.5 = (bf16[16,32,128]{2,1,0:T(8,128)(2,1)S(1)}, bf16[16,32,128]{2,1,0:T(8,128)(2,1)S(1)}, u32[]{:S(2)}, u32[]{:S(2)}) collective-permute-start(bf16[16,32,128]{2,1,0:T(8,128)(2,1)S(1)} %all_to_all.10.mine_ref), channel_id=1, source_target_pairs={{0,1},{1,0},{2,3},{3,2},{4,5},{5,4},{6,7},{7,6},{8,9},{9,8},{10,11... | collective-permute-start | bytes 393224 | tf_op jit(solution)/shard_map/ppermute | solution.py:380

commit v5 on v4

--- a/solution.py
+++ b/solution.py
@@ -16,6 +16,7 @@
 PAIR = 2 * HEAD_DIM
 SCALE = HEAD_DIM**-0.5
 OFFSETS = (-2, -1, 1, 2)
+AXIAL_FLOPS = 20_000_000_000
 BAND_FLOPS = 20_000_000_000
 BAND_OUT_FLOPS = 20_000_000_000
 
@@ -113,57 +114,67 @@
         copy.wait()
 
 
-def axial_kernel(lon_count, points_ref, in_ref, after_ref, out_ref):
-    lon = lax.axis_index("lon")
-    core = lax.rem(lon, 2)
-    chip = lon // 2
-    chips, third, _ = in_ref.shape
+def packed_part(ref, index):
+    chips, third, _ = ref.shape
     slots = third // 3
-    heads = AXIAL_HEADS // 2
-    tokens = chips * slots
-    points = points_ref[lax.axis_index("lat") * (chips // heads) + chip // heads]
-    slot = lax.broadcasted_iota(jnp.int32, (slots, PAIR), 0)
-
-    def bias_of(which):
-        return jnp.concatenate(
-            [
-                jnp.where(slot < live_count(points, 2 * place + which, lon_count), 0.0, DEAD)
-                for place in range(chips)
-            ],
-            axis=0,
-        )
-
+    return ref[:, index * slots : (index + 1) * slots, :].reshape(chips * slots, PAIR)
+
+
+def attend(for_own, for_peer, key_own, key_peer, values, out_ref):
+    scores = jnp.concatenate([dot_t(for_own, key_own), dot_t(for_peer, key_peer)], axis=1)
+    weights = jnp.exp(scores - jnp.max(scores, axis=-1, keepdims=True))
+    total = jnp.sum(weights, axis=-1, keepdims=True)
+    mixed = dot(weights.astype(jnp.bfloat16), values) / total
+    out_ref[...] = mixed.astype(jnp.bfloat16).reshape(out_ref.shape)
+
+
+def lane_masks(tokens):
     lane = lax.broadcasted_iota(jnp.int32, (tokens, PAIR), 1)
-    low = lane < HEAD_DIM
-    first_lane = (lane == 0).astype(jnp.float32)
-    high_lane = (lane == HEAD_DIM).astype(jnp.float32)
-
-    def part(index):
-        return in_ref[:, index * slots : (index + 1) * slots, :].reshape(tokens, PAIR)
-
     bf16 = jnp.bfloat16
-    query = part(0).astype(jnp.float32)
-    key = part(1).astype(jnp.float32)
-    value = part(2)
-    key_own = jnp.where(low, key, high_lane * bias_of(core)).astype(bf16)
-    key_peer = jnp.where(low, first_lane * bias_of(1 - core), key).astype(bf16)
-    rolled = half_roll(query)
-    value_rolled = half_roll(value.astype(jnp.float32)).astype(bf16)
-    plain = jnp.concatenate([value, value_rolled], axis=0)
-    crossed = jnp.concatenate([value_rolled, value], axis=0)
-    blocks = (
-        (jnp.where(low, query, high_lane), jnp.where(low, first_lane, rolled), plain),
-        (jnp.where(low, rolled, high_lane), jnp.where(low, first_lane, query), crossed),
-    )
-    outs = []
-    for for_own, for_peer, values in blocks:
-        scores = jnp.concatenate(
-            [dot_t(for_own.astype(bf16), key_own), dot_t(for_peer.astype(bf16), key_peer)], axis=1
-        )
-        weights = jnp.exp(scores - jnp.max(scores, axis=-1, keepdims=True))
-        total = jnp.sum(weights, axis=-1, keepdims=True)
-        outs.append(dot(weights.astype(bf16), values) / total)
-    out_ref[...] = jnp.where(low, outs[0], outs[1]).astype(bf16).reshape(chips, slots, PAIR)
+    return lane < HEAD_DIM, (lane == 0).astype(bf16), (lane == HEAD_DIM).astype(bf16)
+
+
+def axial_peer_kernel(
+    in_ref, bias_own_ref, bias_peer_ref, out_ref, key_own_ref, key_peer_ref, values_ref, rolled_ref
+):
+    tokens = bias_own_ref.shape[0]
+    low, low_one, high_one = lane_masks(tokens)
+    query, key, value = (packed_part(in_ref, index) for index in range(3))
+    key_own_ref[...] = jnp.where(low, key, bias_own_ref[...])
+    key_peer_ref[...] = jnp.where(low, bias_peer_ref[...], key)
+    query_rolled, value_rolled = half_roll(query), half_roll(value)
+    values_ref[:tokens] = value
+    values_ref[tokens:] = value_rolled
+    rolled_ref[...] = query_rolled
+    attend(
+        jnp.where(low, query_rolled, high_one),
+        jnp.where(low, low_one, query),
+        key_own_ref[...],
+        key_peer_ref[...],
+        jnp.concatenate([value_rolled, value], axis=0),
+        out_ref,
+    )
+
+
+def axial_own_kernel(in_ref, key_own_ref, key_peer_ref, values_ref, rolled_ref, out_ref):
+    low, low_one, high_one = lane_masks(rolled_ref.shape[0])
+    attend(
+        jnp.where(low, packed_part(in_ref, 0), high_one),
+        jnp.where(low, low_one, rolled_ref[...]),
+        key_own_ref[...],
+        key_peer_ref[...],
+        values_ref[...],
+        out_ref,
+    )
+
+
+def join_kernel(low_ref, high_ref, out_ref):
+    items, slots, _ = out_ref.shape
+    low = low_half((items * slots, PAIR))
+    joined = jnp.where(
+        low, low_ref[...].reshape(items * slots, PAIR), high_ref[...].reshape(items * slots, PAIR)
+    )
+    out_ref[...] = joined.reshape(out_ref.shape)
 
 
 def band_kernel(
@@ -231,8 +242,13 @@
         out_ref[:, span] = jnp.where(low_q, mixed[:tokens], mixed[tokens:]).astype(bf16)
 
 
-def band_out_kernel(fields_hbm, band_ref, w_hbm, out_ref, axial_w_ref, fields_ref, w_ref, sems):
-    core = lax.rem(lax.axis_index("lon"), 2)
+def band_out_kernel(
+    lon_count, points_ref, fields_hbm, band_ref, w_hbm, out_ref, axial_w_ref, bias_own_ref, bias_peer_ref,
+    fields_ref, w_ref, sems,
+):
+    lon = lax.axis_index("lon")
+    core = lax.rem(lon, 2)
+    chip = lon // 2
     rows, slots, width = fields_ref.shape
     depth = w_ref.shape[0]
     heads = AXIAL_HEADS // 2
@@ -253,6 +269,15 @@
             )
     for copy in first + rest:
         copy.start()
+    points = points_ref[lax.axis_index("lat") * rows + chip // heads]
+    slot = lax.broadcasted_iota(jnp.int32, (slots, PAIR), 0)
+    lane = lax.broadcasted_iota(jnp.int32, (slots, PAIR), 1)
+    for place in range(lon_count // 2):
+        part = pl.ds(place * slots, slots)
+        dead_own = slot >= live_count(points, 2 * place + core, lon_count)
+        dead_peer = slot >= live_count(points, 2 * place + 1 - core, lon_count)
+        bias_own_ref[part, :] = jnp.where(dead_own & (lane == HEAD_DIM), DEAD, 0.0).astype(jnp.bfloat16)
+        bias_peer_ref[part, :] = jnp.where(dead_peer & (lane == 0), DEAD, 0.0).astype(jnp.bfloat16)
     for copy in first:
         copy.wait()
     out_ref[...] = fields_ref[...].reshape(rows * slots, width) + dot(band_ref[...], w_ref[...])
@@ -260,21 +285,14 @@
         copy.wait()
 
 
-def finish_kernel(lon_count, points_ref, sum_ref, mine_ref, other_ref, w_ref, out_hbm, out_ref, sems):
+def finish_kernel(lon_count, points_ref, sum_ref, mixed_ref, w_ref, out_hbm, out_ref, sems):
     lon = lax.axis_index("lon")
     lat = lax.axis_index("lat")
     rows, slots, width = out_ref.shape
     heads = AXIAL_HEADS // 2
-    low = low_half((slots, PAIR))
     mixed = jnp.concatenate(
         [
-            jnp.concatenate(
-                [
-                    jnp.where(low, mine_ref[row * heads + head], other_ref[row * heads + head])
-                    for head in range(heads)
-                ],
-                axis=1,
-            )
+            jnp.concatenate([mixed_ref[row * heads + head] for head in range(heads)], axis=1)
             for row in range(rows)
         ],
         axis=0,
@@ -360,31 +378,37 @@
         ],
         BAND_FLOPS,
     )(row_points, band_mask.T, normed, *near, *in_hbm(w_query, w_key, w_value))
-    summed, axial_w = call(
-        band_out_kernel,
-        [((tokens, width), f32), ((axial_width, width), bf16)],
-        [HBM, VMEM, HBM],
+    wide = ((chips * slots, PAIR), bf16)
+    summed, axial_w, bias_own, bias_peer = call(
+        functools.partial(band_out_kernel, lon_count),
+        [((tokens, width), f32), ((axial_width, width), bf16), wide, wide],
+        [SMEM, HBM, VMEM, HBM],
         [
             pltpu.VMEM((rows, slots, width), f32),
             pltpu.VMEM((band_width, width), bf16),
             pltpu.SemaphoreType.DMA((2 + AXIAL_HEADS,)),
         ],
         BAND_OUT_FLOPS,
-    )(*in_hbm(fields), band, *in_hbm(w_out))
-    (axial,) = call(
-        functools.partial(axial_kernel, lon_count),
-        [((chips, slots, PAIR), bf16)],
-        [SMEM, VMEM, ANY],
-    )(row_points, row_head, summed)
-    mine = lax.all_to_all(axial, "lon", 0, 0, axis_index_groups=groups, tiled=True)
-    other = lax.ppermute(mine, "lon", swap)
+    )(row_points, *in_hbm(fields), band, *in_hbm(w_out))
+    item = ((chips, slots, PAIR), bf16)
+    away, key_own, key_peer, values, rolled = call(
+        axial_peer_kernel,
+        [item, wide, wide, ((2 * chips * slots, PAIR), bf16), wide],
+        [VMEM] * 3,
+    )(row_head, bias_own, bias_peer)
+    arrived = lax.ppermute(away, "lon", swap)
+    (home,) = call(axial_own_kernel, [item], [VMEM] * 5, flops=AXIAL_FLOPS)(
+        row_head, key_own, key_peer, values, rolled
+    )
+    (joined,) = call(join_kernel, [item], [VMEM] * 2)(home, arrived)
+    mixed = lax.all_to_all(joined, "lon", 0, 0, axis_index_groups=groups, tiled=True)
     (out,) = call(
         functools.partial(finish_kernel, lon_count),
         [((rows, slots, width), f32)],
-        [SMEM] + [VMEM] * 4,
+        [SMEM] + [VMEM] * 3,
         [pltpu.VMEM((rows, slots, width), f32), pltpu.SemaphoreType.DMA((4,))],
         out=ANY,
-    )(row_points, summed, mine, other, axial_w)
+    )(row_points, summed, mixed, axial_w)
     return out
 
 

time: 55.5 us -> 54.6 us (0.984); the launches traced: 55.3 us -> 53.6 us
  waiting for transfers between devices: 5.99 us -> 4.47 us
  Pallas kernels: 14.5 us -> 15.6 us
  blocking collectives: 14.5 us -> 13.4 us
    all_to_all x1, blocking collectives: 14.5 us -> 13.4 us  [on_device(): lax.all_to_all(joined, 'lon', 0, 0, axis_index_groups=groups, tiled=True)]
    pallas_call x2 -> x4, Pallas kernels: 4.29 us -> 5.32 us  [the longest x1 2.32 us: on_device(): call(functools.partial(band_out_kernel, lon_count), [((tokens, width), f3...]
    ppermute x1, waiting for transfers between devices: 0.99 us -> 0.01 us  [on_device(): arrived = lax.ppermute(away, 'lon', swap)]
  transfers between devices with their start and end apart: 7 -> 7, of which waited for: 2 -> 1; matrix products, arithmetic and copies ran while one was open for 0% -> 0% of each run, Pallas kernels for 16% -> 20%
where the time goes in v5:
time: 54.6 us; the launch traced here: 53.6 us
  starting transfers between devices  20 us (37%)
  Pallas kernels  15.6 us (29%)
  blocking collectives  13.4 us (25%)
  waiting for transfers between devices  4.47 us (8%)
    all_to_all x1, blocking collectives, on_device(): lax.all_to_all(joined, 'lon', 0, 0, axis_index_groups=groups, tiled=True)  13.4 us
    all_to_all x1, starting transfers between devices, on_device(): lax.all_to_all(packed, 'lon', 0, 0, axis_index_groups=groups, tiled=True)  10.6 us
    pallas_call x1, Pallas kernels, on_device(): call(functools.partial(band_kernel, lat_count, lon_count), [((tokens, ban...  5.51 us
    all_to_all x1, waiting for transfers between devices, on_device(): lax.all_to_all(packed, 'lon', 0, 0, axis_index_groups=groups, tiled=True)  4.46 us
    ppermute x1, starting transfers between devices, on_device(): peer = lax.ppermute(normed, 'lon', swap)  3.33 us
    ppermute x4, starting transfers between devices, on_device(): lax.ppermute(normed, 'lat', [(place, (place - offset) % lat_count) for pl...  3.24 us
    ppermute x1, starting transfers between devices, on_device(): arrived = lax.ppermute(away, 'lon', swap)  2.77 us
    pallas_call x1, Pallas kernels, on_device(): call(functools.partial(band_out_kernel, lon_count), [((tokens, width), f3...  2.32 us
  transfers between devices with their start and end apart: 7, of which 1 were waited for; matrix products, arithmetic and copies ran while one was open for 0% of the time, Pallas kernels for 20%

profile of v5, /device:TPU:1, one launch (start us, length us, event | category | flops | bytes accessed | tf_op | source)
XLA Modules:
  0.0 53.6 jit_solution(16652949274242766190)
XLA Ops:
  0.0 1.8 %shard_map.82 = (bf16[128,1024]{1,0:T(8,128)(2,1)S(1)}, bf16[3,1024,256]{2,1,0:T(8,128)(2,1)S(1)}) custom-call(f32[4,32,1024]{2,1,0:T(8,128)} %fields_hbm.3, f32[1,1024]{1,0:T(1,128)} %bitcast.3, bf16[1024,1024]{1,0:T(8,128)(2,1)} %wq_hbm.3, bf16[1024,1024]{1,0:T(8,128)(2,1)} %wk_hbm.3, bf16[1024,1024]{1,0:T(8,128)(2,1)} %wv_hbm.3), custom_call_target="tpu_custom_call" | custom-call | tf_op jit(solution)/shard_map/pallas_call | solution.py:346
  1.8 0.0 copy-start
  1.8 0.0 copy-start.1
  1.8 3.3 %collective-permute-start.4 = (bf16[128,1024]{1,0:T(8,128)(2,1)S(1)}, bf16[128,1024]{1,0:T(8,128)(2,1)S(1)}, u32[]{:S(2)}, u32[]{:S(2)}) collective-permute-start(bf16[128,1024]{1,0:T(8,128)(2,1)S(1)} %get-tuple-element.16.own_ref), channel_id=1, source_target_pairs={{0,1},{1,0},{2,3},{3,2},{4,5},{5,4},{6,7},{7,6},{8,9},{9,8},{10,11... | collective-permute-start | bytes 786440 | tf_op jit(solution)/shard_map/ppermute | solution.py:356
  5.1 0.8 %collective-permute-start.3 = (bf16[128,1024]{1,0:T(8,128)(2,1)S(1)}, bf16[128,1024]{1,0:T(8,128)(2,1)S(1)}, u32[]{:S(2)}, u32[]{:S(2)}) collective-permute-start(bf16[128,1024]{1,0:T(8,128)(2,1)S(1)} %get-tuple-element.16.own_ref), channel_id=1, source_target_pairs={{0,192},{32,224},{64,0},{96,32},{128,64},{160,96},{192,128},{224,1... | collective-permute-start | bytes 786440 | tf_op jit(solution)/shard_map/ppermute | solution.py:358
  5.9 1.6 %collective-permute-start.2 = (bf16[128,1024]{1,0:T(8,128)(2,1)S(1)}, bf16[128,1024]{1,0:T(8,128)(2,1)S(1)}, u32[]{:S(2)}, u32[]{:S(2)}) collective-permute-start(bf16[128,1024]{1,0:T(8,128)(2,1)S(1)} %get-tuple-element.16.own_ref), channel_id=1, source_target_pairs={{0,224},{32,0},{64,32},{96,64},{128,96},{160,128},{192,160},{224,1... | collective-permute-start | bytes 786440 | tf_op jit(solution)/shard_map/ppermute | solution.py:358
  7.5 0.0 collective-permute-start.1
  7.5 0.9 %collective-permute-start = (bf16[128,1024]{1,0:T(8,128)(2,1)S(1)}, bf16[128,1024]{1,0:T(8,128)(2,1)S(1)}, u32[]{:S(2)}, u32[]{:S(2)}) collective-permute-start(bf16[128,1024]{1,0:T(8,128)(2,1)S(1)} %get-tuple-element.16.own_ref), channel_id=1, source_target_pairs={{0,64},{32,96},{64,128},{96,160},{128,192},{160,224},{192,0},{224,... | collective-permute-start | bytes 786440 | tf_op jit(solution)/shard_map/ppermute | solution.py:358
  8.4 0.0 collective-permute-done.4.peer_ref
  8.4 1.4 %shard_map.85 = bf16[16,96,128]{2,1,0:T(8,128)(2,1)} custom-call(bf16[128,1024]{1,0:T(8,128)(2,1)S(1)} %get-tuple-element.16.own_ref, bf16[128,1024]{1,0:T(8,128)(2,1)S(1)} %collective-permute-done.4.peer_ref, bf16[3,1024,256]{2,1,0:T(8,128)(2,1)S(1)} %get-tuple-element.18.weights_ref), custom_call_target="tpu_custom_call" | custom-call | tf_op jit(solution)/shard_map/pallas_call | solution.py:363
  9.8 10.6 %all-to-all-start = ((bf16[16,96,128]{2,1,0:T(8,128)(2,1)}), bf16[16,96,128]{2,1,0:T(8,128)(2,1)S(1)}, u32[]{:S(2)}, u32[]{:S(2)}) async-start(bf16[16,96,128]{2,1,0:T(8,128)(2,1)} %shard_map.85), calls=%async_computation | async-start | bytes 786432 | tf_op jit(solution)/shard_map/all_to_all | solution.py:370
  20.4 0.0 collective-permute-done.3.p2_ref
  20.4 0.0 collective-permute-done.2.p1_ref
  20.4 0.0 collective-permute-done.1.m1_ref
  20.4 0.0 collective-permute-done.m2_ref
  20.4 0.0 copy-done
  20.5 0.0 copy-done.1
  20.5 5.5 %shard_map.83.band_ref = bf16[128,512]{1,0:T(8,128)(2,1)S(1)} custom-call(s32[32]{0:T(128)S(1)} %copy-done, s32[4,8]{1,0:T(4,128)S(1)} %bitcast.2, bf16[128,1024]{1,0:T(8,128)(2,1)S(1)} %get-tuple-element.16.own_ref, bf16[128,1024]{1,0:T(8,128)(2,1)S(1)} %collective-permute-done.m2_ref, bf16[128,1024]{1,0:T(8,128)(2,1)S(1)} %collective-permute-done.1.m1_ref, ...), custom_call_target="tpu_custom_call" | custom-call | flops 20000000000 | tf_op jit(solution)/shard_map/pallas_call | solution.py:371
  26.0 2.3 %shard_map.84 = (f32[128,1024]{1,0:T(8,128)S(1)}, bf16[512,1024]{1,0:T(8,128)(2,1)S(1)}, bf16[512,128]{1,0:T(8,128)(2,1)S(1)}, bf16[512,128]{1,0:T(8,128)(2,1)S(1)}) custom-call(s32[32]{0:T(128)S(1)} %copy-done, f32[4,32,1024]{2,1,0:T(8,128)} %fields_hbm.3, bf16[128,512]{1,0:T(8,128)(2,1)S(1)} %shard_map.83.band_ref, bf16[1024,1024]{1,0:T(8,128)(2,1)} %w_hbm.1), custom_call_target="tpu_custom_call" | custom-call | flops 20000000000 | tf_op jit(solution)/shard_map/pallas_call | solution.py:382
  28.3 4.5 %all-to-all-done.in_ref = bf16[16,96,128]{2,1,0:T(8,128)(2,1)S(1)} async-done(((bf16[16,96,128]{2,1,0:T(8,128)(2,1)}), bf16[16,96,128]{2,1,0:T(8,128)(2,1)S(1)}, u32[]{:S(2)}, u32[]{:S(2)}) %all-to-all-start) | async-done | bytes 393248 | tf_op jit(solution)/shard_map/all_to_all | solution.py:370
  32.8 1.5 %shard_map.86 = (bf16[16,32,128]{2,1,0:T(8,128)(2,1)S(1)}, bf16[512,128]{1,0:T(8,128)(2,1)S(1)}, bf16[512,128]{1,0:T(8,128)(2,1)S(1)}, bf16[1024,128]{1,0:T(8,128)(2,1)S(1)}, bf16[512,128]{1,0:T(8,128)(2,1)S(1)}) custom-call(bf16[16,96,128]{2,1,0:T(8,128)(2,1)S(1)} %all-to-all-done.in_ref, bf16[512,128]{1,0:T(8,128)(2,1)S(1)} %get-tuple-element.19.bias_own_ref, ...), custom_call_target="tpu_custom_call" | custom-call | tf_op jit(solution)/shard_map/pallas_call | solution.py:394
  34.3 2.8 %collective-permute-start.5 = (bf16[16,32,128]{2,1,0:T(8,128)(2,1)S(1)}, bf16[16,32,128]{2,1,0:T(8,128)(2,1)S(1)}, u32[]{:S(2)}, u32[]{:S(2)}) collective-permute-start(bf16[16,32,128]{2,1,0:T(8,128)(2,1)S(1)} %get-tuple-element.25), channel_id=1, source_target_pairs={{0,1},{1,0},{2,3},{3,2},{4,5},{5,4},{6,7},{7,6},{8,9},{9,8},{10,11... | collective-permute-start | bytes 393224 | tf_op jit(solution)/shard_map/ppermute | solution.py:399
  37.1 1.4 %shard_map.87.low_ref = bf16[16,32,128]{2,1,0:T(8,128)(2,1)S(1)} custom-call(bf16[16,96,128]{2,1,0:T(8,128)(2,1)S(1)} %all-to-all-done.in_ref, bf16[512,128]{1,0:T(8,128)(2,1)S(1)} %get-tuple-element.21.key_own_ref, bf16[512,128]{1,0:T(8,128)(2,1)S(1)} %get-tuple-element.22.key_peer_ref, bf16[1024,128]{1,0:T(8,128)(2,1)S(1)} %get-tuple-element.23.values_ref, ...), custom_call_target="tpu_custom_call" | custom-call | flops 20000000000 | tf_op jit(solution)/shard_map/pallas_call | solution.py:400
  38.5 0.0 collective-permute-done.5.high_ref
  38.6 13.4 %all_to_all.10.mixed_ref = bf16[16,32,128]{2,1,0:T(8,128)(2,1)S(1)} all-to-all(bf16[16,32,128]{2,1,0:T(8,128)(2,1)S(1)} %shard_map.88), channel_id=1, replica_groups={{0,2,4,6,8,10,12,14,16,18,20,22,24,26,28,30},{1,3,5,7,9,11,13,15,17,19,..., dimensions={0} | all-to-all | bytes 262144 | tf_op jit(solution)/shard_map/all_to_all | solution.py:404
  52.0 1.6 %shard_map.89 = f32[4,32,1024]{2,1,0:T(8,128)} custom-call(s32[32]{0:T(128)S(1)} %copy-done, f32[128,1024]{1,0:T(8,128)S(1)} %get-tuple-element.17.sum_ref, bf16[16,32,128]{2,1,0:T(8,128)(2,1)S(1)} %all_to_all.10.mixed_ref, bf16[512,1024]{1,0:T(8,128)(2,1)S(1)} %get-tuple-element.26.w_ref), custom_call_target="tpu_custom_call" | custom-call | tf_op jit(solution)/shard_map/pallas_call | solution.py:405
  (1 shorter events, 0.0 us)
Async XLA Ops:
  1.8 18.7 %copy-start = (s32[32]{0:T(128)S(1)}, s32[32]{0:T(128)}, u32[]{:S(2)}) copy-start(s32[32]{0:T(128)} %points_ref.5) | copy-start | bytes 388
  1.8 18.7 %copy-start.1 = (s32[8,4]{0,1:T(4,128)S(1)}, s32[8,4]{0,1:T(4,128)}, u32[]{:S(2)}) copy-start(s32[8,4]{0,1:T(4,128)} %param.10) | copy-start | bytes 388
  1.8 6.6 %collective-permute-start.4 = (bf16[128,1024]{1,0:T(8,128)(2,1)S(1)}, bf16[128,1024]{1,0:T(8,128)(2,1)S(1)}, u32[]{:S(2)}, u32[]{:S(2)}) collective-permute-start(bf16[128,1024]{1,0:T(8,128)(2,1)S(1)} %get-tuple-element.16.own_ref), channel_id=1, source_target_pairs={{0,1},{1,0},{2,3},{3,2},{4,5},{5,4},{6,7},{7,6},{8,9},{9,8},{10,11... | collective-permute-start | bytes 786440 | tf_op jit(solution)/shard_map/ppermute | solution.py:356
  5.1 15.3 %collective-permute-start.3 = (bf16[128,1024]{1,0:T(8,128)(2,1)S(1)}, bf16[128,1024]{1,0:T(8,128)(2,1)S(1)}, u32[]{:S(2)}, u32[]{:S(2)}) collective-permute-start(bf16[128,1024]{1,0:T(8,128)(2,1)S(1)} %get-tuple-element.16.own_ref), channel_id=1, source_target_pairs={{0,192},{32,224},{64,0},{96,32},{128,64},{160,96},{192,128},{224,1... | collective-permute-start | bytes 786440 | tf_op jit(solution)/shard_map/ppermute | solution.py:358
  5.9 14.5 %collective-permute-start.2 = (bf16[128,1024]{1,0:T(8,128)(2,1)S(1)}, bf16[128,1024]{1,0:T(8,128)(2,1)S(1)}, u32[]{:S(2)}, u32[]{:S(2)}) collective-permute-start(bf16[128,1024]{1,0:T(8,128)(2,1)S(1)} %get-tuple-element.16.own_ref), channel_id=1, source_target_pairs={{0,224},{32,0},{64,32},{96,64},{128,96},{160,128},{192,160},{224,1... | collective-permute-start | bytes 786440 | tf_op jit(solution)/shard_map/ppermute | solution.py:358
  7.5 13.0 %collective-permute-start.1 = (bf16[128,1024]{1,0:T(8,128)(2,1)S(1)}, bf16[128,1024]{1,0:T(8,128)(2,1)S(1)}, u32[]{:S(2)}, u32[]{:S(2)}) collective-permute-start(bf16[128,1024]{1,0:T(8,128)(2,1)S(1)} %get-tuple-element.16.own_ref), channel_id=1, source_target_pairs={{0,32},{32,64},{64,96},{96,128},{128,160},{160,192},{192,224},{224... | collective-permute-start | bytes 786440 | tf_op jit(solution)/shard_map/ppermute | solution.py:358
  7.5 13.0 %collective-permute-start = (bf16[128,1024]{1,0:T(8,128)(2,1)S(1)}, bf16[128,1024]{1,0:T(8,128)(2,1)S(1)}, u32[]{:S(2)}, u32[]{:S(2)}) collective-permute-start(bf16[128,1024]{1,0:T(8,128)(2,1)S(1)} %get-tuple-element.16.own_ref), channel_id=1, source_target_pairs={{0,64},{32,96},{64,128},{96,160},{128,192},{160,224},{192,0},{224,... | collective-permute-start | bytes 786440 | tf_op jit(solution)/shard_map/ppermute | solution.py:358
  9.8 23.0 %all-to-all-start = ((bf16[16,96,128]{2,1,0:T(8,128)(2,1)}), bf16[16,96,128]{2,1,0:T(8,128)(2,1)S(1)}, u32[]{:S(2)}, u32[]{:S(2)}) async-start(bf16[16,96,128]{2,1,0:T(8,128)(2,1)} %shard_map.85), calls=%async_computation | async-start | bytes 786432 | tf_op jit(solution)/shard_map/all_to_all | solution.py:370
  34.3 4.2 %collective-permute-start.5 = (bf16[16,32,128]{2,1,0:T(8,128)(2,1)S(1)}, bf16[16,32,128]{2,1,0:T(8,128)(2,1)S(1)}, u32[]{:S(2)}, u32[]{:S(2)}) collective-permute-start(bf16[16,32,128]{2,1,0:T(8,128)(2,1)S(1)} %get-tuple-element.25), channel_id=1, source_target_pairs={{0,1},{1,0},{2,3},{3,2},{4,5},{5,4},{6,7},{7,6},{8,9},{9,8},{10,11... | collective-permute-start | bytes 393224 | tf_op jit(solution)/shard_map/ppermute | solution.py:399

commit v6 on v5

--- a/solution.py
+++ b/solution.py
@@ -40,6 +40,16 @@
 
 def low_half(shape):
     return lax.broadcasted_iota(jnp.int32, shape, 1) < HEAD_DIM
+
+
+def chip_order(chips):
+    half = chips // 2
+    return [side * half + (z + half // 2) % half for side in range(2) for z in range(half)]
+
+
+def place_of(chip, chips):
+    half = chips // 2
+    return chip // half * half + lax.rem(lax.rem(chip, half) + half // 2, half)
 
 
 def live_count(points, tile, tiles):
@@ -269,13 +279,14 @@
             )
     for copy in first + rest:
         copy.start()
-    points = points_ref[lax.axis_index("lat") * rows + chip // heads]
+    order = chip_order(lon_count // 2)
+    points = points_ref[lax.axis_index("lat") * rows + place_of(chip, len(order)) // heads]
     slot = lax.broadcasted_iota(jnp.int32, (slots, PAIR), 0)
     lane = lax.broadcasted_iota(jnp.int32, (slots, PAIR), 1)
-    for place in range(lon_count // 2):
+    for place, source in enumerate(order):
         part = pl.ds(place * slots, slots)
-        dead_own = slot >= live_count(points, 2 * place + core, lon_count)
-        dead_peer = slot >= live_count(points, 2 * place + 1 - core, lon_count)
+        dead_own = slot >= live_count(points, 2 * source + core, lon_count)
+        dead_peer = slot >= live_count(points, 2 * source + 1 - core, lon_count)
         bias_own_ref[part, :] = jnp.where(dead_own & (lane == HEAD_DIM), DEAD, 0.0).astype(jnp.bfloat16)
         bias_peer_ref[part, :] = jnp.where(dead_peer & (lane == 0), DEAD, 0.0).astype(jnp.bfloat16)
     for copy in first:
@@ -337,7 +348,7 @@
     axial_width = AXIAL_HEADS * HEAD_DIM
     band_width = (HEADS - AXIAL_HEADS) * HEAD_DIM
     bf16, f32 = jnp.bfloat16, jnp.float32
-    groups = [[2 * chip + core for chip in range(chips)] for core in range(2)]
+    groups = [[2 * chip + core for chip in chip_order(chips)] for core in range(2)]
     swap = [(place, place + 1 - 2 * (place % 2)) for place in range(lon_count)]
 
     def in_hbm(*arrays):

time: 54.6 us -> 52.6 us (0.963)
  waiting for transfers between devices: 4.47 us -> 2.36 us
  starting transfers between devices: 20 us -> 20.8 us
    all_to_all x1, waiting for transfers between devices: 4.46 us -> 2.35 us  [on_device(): lax.all_to_all(packed, 'lon', 0, 0, axis_index_groups=groups, tiled=True)]
    all_to_all x1, starting transfers between devices: 10.6 us -> 12.2 us  [on_device(): lax.all_to_all(packed, 'lon', 0, 0, axis_index_groups=groups, tiled=True)]
    ppermute x1, starting transfers between devices: 2.77 us -> 2.02 us  [on_device(): arrived = lax.ppermute(away, 'lon', swap)]
  transfers between devices with their start and end apart: 7 -> 7, of which waited for: 1 -> 1; matrix products, arithmetic and copies ran while one was open for 0% -> 0% of each run, Pallas kernels for 20% -> 21%
where the time goes in v6:
time: 52.6 us; the launch traced here: 51.8 us
  starting transfers between devices  20.8 us (40%)
  Pallas kernels  15.6 us (30%)
  blocking collectives  12.9 us (25%)
  waiting for transfers between devices  2.36 us (4%)
    all_to_all x1, blocking collectives, on_device(): lax.all_to_all(joined, 'lon', 0, 0, axis_index_groups=groups, tiled=True)  12.9 us
    all_to_all x1, starting transfers between devices, on_device(): lax.all_to_all(packed, 'lon', 0, 0, axis_index_groups=groups, tiled=True)  12.2 us
    pallas_call x1, Pallas kernels, on_device(): call(functools.partial(band_kernel, lat_count, lon_count), [((tokens, ban...  5.52 us
    ppermute x1, starting transfers between devices, on_device(): peer = lax.ppermute(normed, 'lon', swap)  3.33 us
    ppermute x4, starting transfers between devices, on_device(): lax.ppermute(normed, 'lat', [(place, (place - offset) % lat_count) for pl...  3.24 us
    all_to_all x1, waiting for transfers between devices, on_device(): lax.all_to_all(packed, 'lon', 0, 0, axis_index_groups=groups, tiled=True)  2.35 us
    pallas_call x1, Pallas kernels, on_device(): call(functools.partial(band_out_kernel, lon_count), [((tokens, width), f3...  2.32 us
    ppermute x1, starting transfers between devices, on_device(): arrived = lax.ppermute(away, 'lon', swap)  2.02 us
  transfers between devices with their start and end apart: 7, of which 1 were waited for; matrix products, arithmetic and copies ran while one was open for 0% of the time, Pallas kernels for 21%

profile of v6, /device:TPU:1, one launch (start us, length us, event | category | flops | bytes accessed | tf_op | source)
XLA Modules:
  0.0 51.8 jit_solution(282975591503097165)
XLA Ops:
  0.0 1.8 %shard_map.82 = (bf16[128,1024]{1,0:T(8,128)(2,1)S(1)}, bf16[3,1024,256]{2,1,0:T(8,128)(2,1)S(1)}) custom-call(f32[4,32,1024]{2,1,0:T(8,128)} %fields_hbm.3, f32[1,1024]{1,0:T(1,128)} %bitcast.3, bf16[1024,1024]{1,0:T(8,128)(2,1)} %wq_hbm.3, bf16[1024,1024]{1,0:T(8,128)(2,1)} %wk_hbm.3, bf16[1024,1024]{1,0:T(8,128)(2,1)} %wv_hbm.3), custom_call_target="tpu_custom_call" | custom-call | tf_op jit(solution)/shard_map/pallas_call | solution.py:357
  1.8 0.0 copy-start
  1.8 0.0 copy-start.1
  1.8 3.3 %collective-permute-start.4 = (bf16[128,1024]{1,0:T(8,128)(2,1)S(1)}, bf16[128,1024]{1,0:T(8,128)(2,1)S(1)}, u32[]{:S(2)}, u32[]{:S(2)}) collective-permute-start(bf16[128,1024]{1,0:T(8,128)(2,1)S(1)} %get-tuple-element.16.own_ref), channel_id=1, source_target_pairs={{0,1},{1,0},{2,3},{3,2},{4,5},{5,4},{6,7},{7,6},{8,9},{9,8},{10,11... | collective-permute-start | bytes 786440 | tf_op jit(solution)/shard_map/ppermute | solution.py:367
  5.1 0.8 %collective-permute-start.3 = (bf16[128,1024]{1,0:T(8,128)(2,1)S(1)}, bf16[128,1024]{1,0:T(8,128)(2,1)S(1)}, u32[]{:S(2)}, u32[]{:S(2)}) collective-permute-start(bf16[128,1024]{1,0:T(8,128)(2,1)S(1)} %get-tuple-element.16.own_ref), channel_id=1, source_target_pairs={{0,192},{32,224},{64,0},{96,32},{128,64},{160,96},{192,128},{224,1... | collective-permute-start | bytes 786440 | tf_op jit(solution)/shard_map/ppermute | solution.py:369
  5.9 1.6 %collective-permute-start.2 = (bf16[128,1024]{1,0:T(8,128)(2,1)S(1)}, bf16[128,1024]{1,0:T(8,128)(2,1)S(1)}, u32[]{:S(2)}, u32[]{:S(2)}) collective-permute-start(bf16[128,1024]{1,0:T(8,128)(2,1)S(1)} %get-tuple-element.16.own_ref), channel_id=1, source_target_pairs={{0,224},{32,0},{64,32},{96,64},{128,96},{160,128},{192,160},{224,1... | collective-permute-start | bytes 786440 | tf_op jit(solution)/shard_map/ppermute | solution.py:369
  7.5 0.0 collective-permute-start.1
  7.5 0.9 %collective-permute-start = (bf16[128,1024]{1,0:T(8,128)(2,1)S(1)}, bf16[128,1024]{1,0:T(8,128)(2,1)S(1)}, u32[]{:S(2)}, u32[]{:S(2)}) collective-permute-start(bf16[128,1024]{1,0:T(8,128)(2,1)S(1)} %get-tuple-element.16.own_ref), channel_id=1, source_target_pairs={{0,64},{32,96},{64,128},{96,160},{128,192},{160,224},{192,0},{224,... | collective-permute-start | bytes 786440 | tf_op jit(solution)/shard_map/ppermute | solution.py:369
  8.4 0.0 collective-permute-done.4.peer_ref
  8.4 1.4 %shard_map.85 = bf16[16,96,128]{2,1,0:T(8,128)(2,1)} custom-call(bf16[128,1024]{1,0:T(8,128)(2,1)S(1)} %get-tuple-element.16.own_ref, bf16[128,1024]{1,0:T(8,128)(2,1)S(1)} %collective-permute-done.4.peer_ref, bf16[3,1024,256]{2,1,0:T(8,128)(2,1)S(1)} %get-tuple-element.18.weights_ref), custom_call_target="tpu_custom_call" | custom-call | tf_op jit(solution)/shard_map/pallas_call | solution.py:374
  9.8 12.2 %all-to-all-start = ((bf16[16,96,128]{2,1,0:T(8,128)(2,1)}), bf16[16,96,128]{2,1,0:T(8,128)(2,1)S(1)}, u32[]{:S(2)}, u32[]{:S(2)}) async-start(bf16[16,96,128]{2,1,0:T(8,128)(2,1)} %shard_map.85), calls=%async_computation | async-start | bytes 786432 | tf_op jit(solution)/shard_map/all_to_all | solution.py:381
  22.0 0.0 collective-permute-done.3.p2_ref
  22.0 0.0 collective-permute-done.2.p1_ref
  22.0 0.0 collective-permute-done.1.m1_ref
  22.0 0.0 collective-permute-done.m2_ref
  22.0 0.0 copy-done
  22.0 0.0 copy-done.1
  22.0 5.5 %shard_map.83.band_ref = bf16[128,512]{1,0:T(8,128)(2,1)S(1)} custom-call(s32[32]{0:T(128)S(1)} %copy-done, s32[4,8]{1,0:T(4,128)S(1)} %bitcast.2, bf16[128,1024]{1,0:T(8,128)(2,1)S(1)} %get-tuple-element.16.own_ref, bf16[128,1024]{1,0:T(8,128)(2,1)S(1)} %collective-permute-done.m2_ref, bf16[128,1024]{1,0:T(8,128)(2,1)S(1)} %collective-permute-done.1.m1_ref, ...), custom_call_target="tpu_custom_call" | custom-call | flops 20000000000 | tf_op jit(solution)/shard_map/pallas_call | solution.py:382
  27.5 2.3 %shard_map.84 = (f32[128,1024]{1,0:T(8,128)S(1)}, bf16[512,1024]{1,0:T(8,128)(2,1)S(1)}, bf16[512,128]{1,0:T(8,128)(2,1)S(1)}, bf16[512,128]{1,0:T(8,128)(2,1)S(1)}) custom-call(s32[32]{0:T(128)S(1)} %copy-done, f32[4,32,1024]{2,1,0:T(8,128)} %fields_hbm.3, bf16[128,512]{1,0:T(8,128)(2,1)S(1)} %shard_map.83.band_ref, bf16[1024,1024]{1,0:T(8,128)(2,1)} %w_hbm.1), custom_call_target="tpu_custom_call" | custom-call | flops 20000000000 | tf_op jit(solution)/shard_map/pallas_call | solution.py:393
  29.9 2.3 %all-to-all-done.in_ref = bf16[16,96,128]{2,1,0:T(8,128)(2,1)S(1)} async-done(((bf16[16,96,128]{2,1,0:T(8,128)(2,1)}), bf16[16,96,128]{2,1,0:T(8,128)(2,1)S(1)}, u32[]{:S(2)}, u32[]{:S(2)}) %all-to-all-start) | async-done | bytes 393248 | tf_op jit(solution)/shard_map/all_to_all | solution.py:381
  32.2 1.5 %shard_map.86 = (bf16[16,32,128]{2,1,0:T(8,128)(2,1)S(1)}, bf16[512,128]{1,0:T(8,128)(2,1)S(1)}, bf16[512,128]{1,0:T(8,128)(2,1)S(1)}, bf16[1024,128]{1,0:T(8,128)(2,1)S(1)}, bf16[512,128]{1,0:T(8,128)(2,1)S(1)}) custom-call(bf16[16,96,128]{2,1,0:T(8,128)(2,1)S(1)} %all-to-all-done.in_ref, bf16[512,128]{1,0:T(8,128)(2,1)S(1)} %get-tuple-element.19.bias_own_ref, ...), custom_call_target="tpu_custom_call" | custom-call | tf_op jit(solution)/shard_map/pallas_call | solution.py:405
  33.7 2.0 %collective-permute-start.5 = (bf16[16,32,128]{2,1,0:T(8,128)(2,1)S(1)}, bf16[16,32,128]{2,1,0:T(8,128)(2,1)S(1)}, u32[]{:S(2)}, u32[]{:S(2)}) collective-permute-start(bf16[16,32,128]{2,1,0:T(8,128)(2,1)S(1)} %get-tuple-element.25), channel_id=1, source_target_pairs={{0,1},{1,0},{2,3},{3,2},{4,5},{5,4},{6,7},{7,6},{8,9},{9,8},{10,11... | collective-permute-start | bytes 393224 | tf_op jit(solution)/shard_map/ppermute | solution.py:410
  35.8 1.5 %shard_map.87.low_ref = bf16[16,32,128]{2,1,0:T(8,128)(2,1)S(1)} custom-call(bf16[16,96,128]{2,1,0:T(8,128)(2,1)S(1)} %all-to-all-done.in_ref, bf16[512,128]{1,0:T(8,128)(2,1)S(1)} %get-tuple-element.21.key_own_ref, bf16[512,128]{1,0:T(8,128)(2,1)S(1)} %get-tuple-element.22.key_peer_ref, bf16[1024,128]{1,0:T(8,128)(2,1)S(1)} %get-tuple-element.23.values_ref, ...), custom_call_target="tpu_custom_call" | custom-call | flops 20000000000 | tf_op jit(solution)/shard_map/pallas_call | solution.py:411
  37.2 0.0 collective-permute-done.5.high_ref
  37.3 12.9 %all_to_all.10.mixed_ref = bf16[16,32,128]{2,1,0:T(8,128)(2,1)S(1)} all-to-all(bf16[16,32,128]{2,1,0:T(8,128)(2,1)S(1)} %shard_map.88), channel_id=1, replica_groups={{8,10,12,14,0,2,4,6,24,26,28,30,16,18,20,22},{9,11,13,15,1,3,5,7,25,27,..., dimensions={0} | all-to-all | bytes 262144 | tf_op jit(solution)/shard_map/all_to_all | solution.py:415
  50.2 1.6 %shard_map.89 = f32[4,32,1024]{2,1,0:T(8,128)} custom-call(s32[32]{0:T(128)S(1)} %copy-done, f32[128,1024]{1,0:T(8,128)S(1)} %get-tuple-element.17.sum_ref, bf16[16,32,128]{2,1,0:T(8,128)(2,1)S(1)} %all_to_all.10.mixed_ref, bf16[512,1024]{1,0:T(8,128)(2,1)S(1)} %get-tuple-element.26.w_ref), custom_call_target="tpu_custom_call" | custom-call | tf_op jit(solution)/shard_map/pallas_call | solution.py:416
  (1 shorter events, 0.0 us)
Async XLA Ops:
  1.8 20.2 %copy-start = (s32[32]{0:T(128)S(1)}, s32[32]{0:T(128)}, u32[]{:S(2)}) copy-start(s32[32]{0:T(128)} %points_ref.5) | copy-start | bytes 388
  1.8 20.2 %copy-start.1 = (s32[8,4]{0,1:T(4,128)S(1)}, s32[8,4]{0,1:T(4,128)}, u32[]{:S(2)}) copy-start(s32[8,4]{0,1:T(4,128)} %param.10) | copy-start | bytes 388
  1.8 6.6 %collective-permute-start.4 = (bf16[128,1024]{1,0:T(8,128)(2,1)S(1)}, bf16[128,1024]{1,0:T(8,128)(2,1)S(1)}, u32[]{:S(2)}, u32[]{:S(2)}) collective-permute-start(bf16[128,1024]{1,0:T(8,128)(2,1)S(1)} %get-tuple-element.16.own_ref), channel_id=1, source_target_pairs={{0,1},{1,0},{2,3},{3,2},{4,5},{5,4},{6,7},{7,6},{8,9},{9,8},{10,11... | collective-permute-start | bytes 786440 | tf_op jit(solution)/shard_map/ppermute | solution.py:367
  5.1 16.8 %collective-permute-start.3 = (bf16[128,1024]{1,0:T(8,128)(2,1)S(1)}, bf16[128,1024]{1,0:T(8,128)(2,1)S(1)}, u32[]{:S(2)}, u32[]{:S(2)}) collective-permute-start(bf16[128,1024]{1,0:T(8,128)(2,1)S(1)} %get-tuple-element.16.own_ref), channel_id=1, source_target_pairs={{0,192},{32,224},{64,0},{96,32},{128,64},{160,96},{192,128},{224,1... | collective-permute-start | bytes 786440 | tf_op jit(solution)/shard_map/ppermute | solution.py:369
  5.9 16.1 %collective-permute-start.2 = (bf16[128,1024]{1,0:T(8,128)(2,1)S(1)}, bf16[128,1024]{1,0:T(8,128)(2,1)S(1)}, u32[]{:S(2)}, u32[]{:S(2)}) collective-permute-start(bf16[128,1024]{1,0:T(8,128)(2,1)S(1)} %get-tuple-element.16.own_ref), channel_id=1, source_target_pairs={{0,224},{32,0},{64,32},{96,64},{128,96},{160,128},{192,160},{224,1... | collective-permute-start | bytes 786440 | tf_op jit(solution)/shard_map/ppermute | solution.py:369
  7.5 14.5 %collective-permute-start.1 = (bf16[128,1024]{1,0:T(8,128)(2,1)S(1)}, bf16[128,1024]{1,0:T(8,128)(2,1)S(1)}, u32[]{:S(2)}, u32[]{:S(2)}) collective-permute-start(bf16[128,1024]{1,0:T(8,128)(2,1)S(1)} %get-tuple-element.16.own_ref), channel_id=1, source_target_pairs={{0,32},{32,64},{64,96},{96,128},{128,160},{160,192},{192,224},{224... | collective-permute-start | bytes 786440 | tf_op jit(solution)/shard_map/ppermute | solution.py:369
  7.5 14.5 %collective-permute-start = (bf16[128,1024]{1,0:T(8,128)(2,1)S(1)}, bf16[128,1024]{1,0:T(8,128)(2,1)S(1)}, u32[]{:S(2)}, u32[]{:S(2)}) collective-permute-start(bf16[128,1024]{1,0:T(8,128)(2,1)S(1)} %get-tuple-element.16.own_ref), channel_id=1, source_target_pairs={{0,64},{32,96},{64,128},{96,160},{128,192},{160,224},{192,0},{224,... | collective-permute-start | bytes 786440 | tf_op jit(solution)/shard_map/ppermute | solution.py:369
  9.8 22.5 %all-to-all-start = ((bf16[16,96,128]{2,1,0:T(8,128)(2,1)}), bf16[16,96,128]{2,1,0:T(8,128)(2,1)S(1)}, u32[]{:S(2)}, u32[]{:S(2)}) async-start(bf16[16,96,128]{2,1,0:T(8,128)(2,1)} %shard_map.85), calls=%async_computation | async-start | bytes 786432 | tf_op jit(solution)/shard_map/all_to_all | solution.py:381
  33.7 3.5 %collective-permute-start.5 = (bf16[16,32,128]{2,1,0:T(8,128)(2,1)S(1)}, bf16[16,32,128]{2,1,0:T(8,128)(2,1)S(1)}, u32[]{:S(2)}, u32[]{:S(2)}) collective-permute-start(bf16[16,32,128]{2,1,0:T(8,128)(2,1)S(1)} %get-tuple-element.25), channel_id=1, source_target_pairs={{0,1},{1,0},{2,3},{3,2},{4,5},{5,4},{6,7},{7,6},{8,9},{9,8},{10,11... | collective-permute-start | bytes 393224 | tf_op jit(solution)/shard_map/ppermute | solution.py:410

commit v7 on v6

--- a/solution.py
+++ b/solution.py
@@ -18,7 +18,6 @@
 OFFSETS = (-2, -1, 1, 2)
 AXIAL_FLOPS = 20_000_000_000
 BAND_FLOPS = 20_000_000_000
-BAND_OUT_FLOPS = 20_000_000_000
 
 VMEM = pl.BlockSpec(memory_space=pltpu.VMEM)
 SMEM = pl.BlockSpec(memory_space=pltpu.SMEM)
@@ -189,7 +188,9 @@
 
 def band_kernel(
     lat_count, lon_count, points_ref, mask_ref, own_ref, m2_ref, m1_ref, p1_ref, p2_ref,
-    wq_hbm, wk_hbm, wv_hbm, out_ref, weights_ref, sems,
+    wq_hbm, wk_hbm, wv_hbm, fields_hbm, w_hbm,
+    out_ref, axial_w_ref, bias_own_ref, bias_peer_ref,
+    weights_ref, fields_ref, w_ref, band_ref, sems,
 ):
     first = AXIAL_HEADS * HEAD_DIM
     columns = pl.ds(first, weights_ref.shape[2])
@@ -197,10 +198,26 @@
         pltpu.make_async_copy(hbm.at[:, columns], weights_ref.at[place], sems.at[place])
         for place, hbm in enumerate((wk_hbm, wv_hbm, wq_hbm))
     ]
-    for copy in copies:
-        copy.start()
+    late = [
+        pltpu.make_async_copy(w_hbm.at[pl.ds(first, w_ref.shape[0])], w_ref, sems.at[3]),
+        pltpu.make_async_copy(fields_hbm, fields_ref, sems.at[4]),
+    ]
     lat = lax.axis_index("lat")
     lon = lax.axis_index("lon")
+    core = lax.rem(lon, 2)
+    heads = AXIAL_HEADS // 2
+    for head in range(heads):
+        for side in range(2):
+            source = (jnp.where(side == 0, core, 1 - core) * heads + head) * HEAD_DIM
+            late.append(
+                pltpu.make_async_copy(
+                    w_hbm.at[pl.ds(pl.multiple_of(source, HEAD_DIM), HEAD_DIM)],
+                    axial_w_ref.at[pl.ds(head * PAIR + side * HEAD_DIM, HEAD_DIM)],
+                    sems.at[5 + head * 2 + side],
+                )
+            )
+    for copy in copies + late:
+        copy.start()
     tokens = own_ref.shape[0]
     slots = 32
     rows = tokens // slots
@@ -249,50 +266,21 @@
         weights = jnp.exp(scores - jnp.max(scores, axis=-1, keepdims=True))
         total = jnp.sum(weights, axis=-1, keepdims=True)
         mixed = dot(weights.astype(bf16), v) / total
-        out_ref[:, span] = jnp.where(low_q, mixed[:tokens], mixed[tokens:]).astype(bf16)
-
-
-def band_out_kernel(
-    lon_count, points_ref, fields_hbm, band_ref, w_hbm, out_ref, axial_w_ref, bias_own_ref, bias_peer_ref,
-    fields_ref, w_ref, sems,
-):
-    lon = lax.axis_index("lon")
-    core = lax.rem(lon, 2)
-    chip = lon // 2
-    rows, slots, width = fields_ref.shape
-    depth = w_ref.shape[0]
-    heads = AXIAL_HEADS // 2
-    first = [
-        pltpu.make_async_copy(w_hbm.at[pl.ds(depth, depth)], w_ref, sems.at[0]),
-        pltpu.make_async_copy(fields_hbm, fields_ref, sems.at[1]),
-    ]
-    rest = []
-    for head in range(heads):
-        for side in range(2):
-            source = (jnp.where(side == 0, core, 1 - core) * heads + head) * HEAD_DIM
-            rest.append(
-                pltpu.make_async_copy(
-                    w_hbm.at[pl.ds(pl.multiple_of(source, HEAD_DIM), HEAD_DIM)],
-                    axial_w_ref.at[pl.ds(head * PAIR + side * HEAD_DIM, HEAD_DIM)],
-                    sems.at[2 + head * 2 + side],
-                )
-            )
-    for copy in first + rest:
-        copy.start()
+        band_ref[:, span] = jnp.where(low_q, mixed[:tokens], mixed[tokens:]).astype(bf16)
     order = chip_order(lon_count // 2)
-    points = points_ref[lax.axis_index("lat") * rows + place_of(chip, len(order)) // heads]
-    slot = lax.broadcasted_iota(jnp.int32, (slots, PAIR), 0)
+    points = points_ref[lat * rows + place_of(lon // 2, len(order)) // heads]
     lane = lax.broadcasted_iota(jnp.int32, (slots, PAIR), 1)
     for place, source in enumerate(order):
         part = pl.ds(place * slots, slots)
         dead_own = slot >= live_count(points, 2 * source + core, lon_count)
         dead_peer = slot >= live_count(points, 2 * source + 1 - core, lon_count)
-        bias_own_ref[part, :] = jnp.where(dead_own & (lane == HEAD_DIM), DEAD, 0.0).astype(jnp.bfloat16)
-        bias_peer_ref[part, :] = jnp.where(dead_peer & (lane == 0), DEAD, 0.0).astype(jnp.bfloat16)
-    for copy in first:
+        bias_own_ref[part, :] = jnp.where(dead_own & (lane == HEAD_DIM), DEAD, 0.0).astype(bf16)
+        bias_peer_ref[part, :] = jnp.where(dead_peer & (lane == 0), DEAD, 0.0).astype(bf16)
+    for copy in late[:2]:
         copy.wait()
-    out_ref[...] = fields_ref[...].reshape(rows * slots, width) + dot(band_ref[...], w_ref[...])
-    for copy in rest:
+    width = fields_ref.shape[2]
+    out_ref[...] = fields_ref[...].reshape(tokens, width) + dot(band_ref[...], w_ref[...])
+    for copy in late[2:]:
         copy.wait()
 
 
@@ -379,28 +367,20 @@
         out=ANY,
     )(normed, peer, weights)
     row_head = lax.all_to_all(packed, "lon", 0, 0, axis_index_groups=groups, tiled=True)
-    (band,) = call(
+    wide = ((chips * slots, PAIR), bf16)
+    summed, axial_w, bias_own, bias_peer = call(
         functools.partial(band_kernel, lat_count, lon_count),
-        [((tokens, band_width), bf16)],
-        [SMEM, SMEM] + [VMEM] * 5 + [HBM] * 3,
+        [((tokens, width), f32), ((axial_width, width), bf16), wide, wide],
+        [SMEM, SMEM] + [VMEM] * 5 + [HBM] * 5,
         [
             pltpu.VMEM((3, width, band_width), bf16),
-            pltpu.SemaphoreType.DMA((3,)),
+            pltpu.VMEM((rows, slots, width), f32),
+            pltpu.VMEM((band_width, width), bf16),
+            pltpu.VMEM((tokens, band_width), bf16),
+            pltpu.SemaphoreType.DMA((5 + AXIAL_HEADS,)),
         ],
         BAND_FLOPS,
-    )(row_points, band_mask.T, normed, *near, *in_hbm(w_query, w_key, w_value))
-    wide = ((chips * slots, PAIR), bf16)
-    summed, axial_w, bias_own, bias_peer = call(
-        functools.partial(band_out_kernel, lon_count),
-        [((tokens, width), f32), ((axial_width, width), bf16), wide, wide],
-        [SMEM, HBM, VMEM, HBM],
-        [
-            pltpu.VMEM((rows, slots, width), f32),
-            pltpu.VMEM((band_width, width), bf16),
-            pltpu.SemaphoreType.DMA((2 + AXIAL_HEADS,)),
-        ],
-        BAND_OUT_FLOPS,
-    )(row_points, *in_hbm(fields), band, *in_hbm(w_out))
+    )(row_points, band_mask.T, normed, *near, *in_hbm(w_query, w_key, w_value, fields, w_out))
     item = ((chips, slots, PAIR), bf16)
     away, key_own, key_peer, values, rolled = call(
         axial_peer_kernel,

time: 52.6 us -> 52 us (0.989); the launches traced: 51.8 us -> 51.8 us
  Pallas kernels: 15.6 us -> 13.7 us
  waiting for transfers between devices: 2.36 us -> 4.24 us
    all_to_all x1, waiting for transfers between devices: 2.35 us -> 4.23 us  [on_device(): lax.all_to_all(packed, 'lon', 0, 0, axis_index_groups=groups, tiled=True)]
    pallas_call x2 -> x1, Pallas kernels: 7.84 us -> 5.97 us  [on_device(): call(functools.partial(band_kernel, lat_count, lon_count), [((tokens, wid...]
  transfers between devices with their start and end apart: 7 -> 7, of which waited for: 1 -> 1; matrix products, arithmetic and copies ran while one was open for 0% -> 0% of each run, Pallas kernels for 21% -> 17%
where the time goes in v7:
time: 52 us; the launch traced here: 51.8 us
  starting transfers between devices  20.8 us (40%)
  Pallas kernels  13.7 us (26%)
  blocking collectives  12.9 us (25%)
  waiting for transfers between devices  4.24 us (8%)
    all_to_all x1, blocking collectives, on_device(): lax.all_to_all(joined, 'lon', 0, 0, axis_index_groups=groups, tiled=True)  12.9 us
    all_to_all x1, starting transfers between devices, on_device(): lax.all_to_all(packed, 'lon', 0, 0, axis_index_groups=groups, tiled=True)  12.2 us
    pallas_call x1, Pallas kernels, on_device(): call(functools.partial(band_kernel, lat_count, lon_count), [((tokens, wid...  5.97 us
    all_to_all x1, waiting for transfers between devices, on_device(): lax.all_to_all(packed, 'lon', 0, 0, axis_index_groups=groups, tiled=True)  4.23 us
    ppermute x1, starting transfers between devices, on_device(): peer = lax.ppermute(normed, 'lon', swap)  3.33 us
    ppermute x4, starting transfers between devices, on_device(): lax.ppermute(normed, 'lat', [(place, (place - offset) % lat_count) for pl...  3.24 us
    ppermute x1, starting transfers between devices, on_device(): arrived = lax.ppermute(away, 'lon', swap)  2.02 us
    pallas_call x1, Pallas kernels, on_device(): call(norm_kernel, [((tokens, width), bf16), ((3, width, axial_width // 2)...  1.77 us
  transfers between devices with their start and end apart: 7, of which 1 were waited for; matrix products, arithmetic and copies ran while one was open for 0% of the time, Pallas kernels for 17%

profile of v7, /device:TPU:1, one launch (start us, length us, event | category | flops | bytes accessed | tf_op | source)
XLA Modules:
  0.0 51.8 jit_solution(18259236074968637816)
XLA Ops:
  0.0 1.8 %shard_map.82 = (bf16[128,1024]{1,0:T(8,128)(2,1)S(1)}, bf16[3,1024,256]{2,1,0:T(8,128)(2,1)S(1)}) custom-call(f32[4,32,1024]{2,1,0:T(8,128)} %fields_hbm.3, f32[1,1024]{1,0:T(1,128)} %bitcast.3, bf16[1024,1024]{1,0:T(8,128)(2,1)} %wq_hbm.3, bf16[1024,1024]{1,0:T(8,128)(2,1)} %wk_hbm.3, bf16[1024,1024]{1,0:T(8,128)(2,1)} %wv_hbm.3), custom_call_target="tpu_custom_call" | custom-call | tf_op jit(solution)/shard_map/pallas_call | solution.py:345
  1.8 0.0 copy-start
  1.8 0.0 copy-start.1
  1.8 3.3 %collective-permute-start.4 = (bf16[128,1024]{1,0:T(8,128)(2,1)S(1)}, bf16[128,1024]{1,0:T(8,128)(2,1)S(1)}, u32[]{:S(2)}, u32[]{:S(2)}) collective-permute-start(bf16[128,1024]{1,0:T(8,128)(2,1)S(1)} %get-tuple-element.16.own_ref), channel_id=1, source_target_pairs={{0,1},{1,0},{2,3},{3,2},{4,5},{5,4},{6,7},{7,6},{8,9},{9,8},{10,11... | collective-permute-start | bytes 786440 | tf_op jit(solution)/shard_map/ppermute | solution.py:355
  5.1 0.8 %collective-permute-start.3 = (bf16[128,1024]{1,0:T(8,128)(2,1)S(1)}, bf16[128,1024]{1,0:T(8,128)(2,1)S(1)}, u32[]{:S(2)}, u32[]{:S(2)}) collective-permute-start(bf16[128,1024]{1,0:T(8,128)(2,1)S(1)} %get-tuple-element.16.own_ref), channel_id=1, source_target_pairs={{0,192},{32,224},{64,0},{96,32},{128,64},{160,96},{192,128},{224,1... | collective-permute-start | bytes 786440 | tf_op jit(solution)/shard_map/ppermute | solution.py:357
  5.9 1.6 %collective-permute-start.2 = (bf16[128,1024]{1,0:T(8,128)(2,1)S(1)}, bf16[128,1024]{1,0:T(8,128)(2,1)S(1)}, u32[]{:S(2)}, u32[]{:S(2)}) collective-permute-start(bf16[128,1024]{1,0:T(8,128)(2,1)S(1)} %get-tuple-element.16.own_ref), channel_id=1, source_target_pairs={{0,224},{32,0},{64,32},{96,64},{128,96},{160,128},{192,160},{224,1... | collective-permute-start | bytes 786440 | tf_op jit(solution)/shard_map/ppermute | solution.py:357
  7.5 0.0 collective-permute-start.1
  7.5 0.9 %collective-permute-start = (bf16[128,1024]{1,0:T(8,128)(2,1)S(1)}, bf16[128,1024]{1,0:T(8,128)(2,1)S(1)}, u32[]{:S(2)}, u32[]{:S(2)}) collective-permute-start(bf16[128,1024]{1,0:T(8,128)(2,1)S(1)} %get-tuple-element.16.own_ref), channel_id=1, source_target_pairs={{0,64},{32,96},{64,128},{96,160},{128,192},{160,224},{192,0},{224,... | collective-permute-start | bytes 786440 | tf_op jit(solution)/shard_map/ppermute | solution.py:357
  8.4 0.0 collective-permute-done.4.peer_ref
  8.4 1.4 %shard_map.84 = bf16[16,96,128]{2,1,0:T(8,128)(2,1)} custom-call(bf16[128,1024]{1,0:T(8,128)(2,1)S(1)} %get-tuple-element.16.own_ref, bf16[128,1024]{1,0:T(8,128)(2,1)S(1)} %collective-permute-done.4.peer_ref, bf16[3,1024,256]{2,1,0:T(8,128)(2,1)S(1)} %get-tuple-element.18.weights_ref), custom_call_target="tpu_custom_call" | custom-call | tf_op jit(solution)/shard_map/pallas_call | solution.py:362
  9.8 12.2 %all-to-all-start = ((bf16[16,96,128]{2,1,0:T(8,128)(2,1)}), bf16[16,96,128]{2,1,0:T(8,128)(2,1)S(1)}, u32[]{:S(2)}, u32[]{:S(2)}) async-start(bf16[16,96,128]{2,1,0:T(8,128)(2,1)} %shard_map.84), calls=%async_computation | async-start | bytes 786432 | tf_op jit(solution)/shard_map/all_to_all | solution.py:369
  22.0 0.0 collective-permute-done.3.p2_ref
  22.0 0.0 collective-permute-done.2.p1_ref
  22.0 0.0 collective-permute-done.1.m1_ref
  22.0 0.0 collective-permute-done.m2_ref
  22.0 0.0 copy-done
  22.0 0.0 copy-done.1
  22.0 6.0 %shard_map.83 = (f32[128,1024]{1,0:T(8,128)S(1)}, bf16[512,1024]{1,0:T(8,128)(2,1)S(1)}, bf16[512,128]{1,0:T(8,128)(2,1)S(1)}, bf16[512,128]{1,0:T(8,128)(2,1)S(1)}) custom-call(s32[32]{0:T(128)S(1)} %copy-done, s32[4,8]{1,0:T(4,128)S(1)} %bitcast.2, bf16[128,1024]{1,0:T(8,128)(2,1)S(1)} %get-tuple-element.16.own_ref, ...), custom_call_target="tpu_custom_call" | custom-call | flops 20000000000 | tf_op jit(solution)/shard_map/pallas_call | solution.py:371
  28.0 4.2 %all-to-all-done.in_ref = bf16[16,96,128]{2,1,0:T(8,128)(2,1)S(1)} async-done(((bf16[16,96,128]{2,1,0:T(8,128)(2,1)}), bf16[16,96,128]{2,1,0:T(8,128)(2,1)S(1)}, u32[]{:S(2)}, u32[]{:S(2)}) %all-to-all-start) | async-done | bytes 393248 | tf_op jit(solution)/shard_map/all_to_all | solution.py:369
  32.2 1.5 %shard_map.85 = (bf16[16,32,128]{2,1,0:T(8,128)(2,1)S(1)}, bf16[512,128]{1,0:T(8,128)(2,1)S(1)}, bf16[512,128]{1,0:T(8,128)(2,1)S(1)}, bf16[1024,128]{1,0:T(8,128)(2,1)S(1)}, bf16[512,128]{1,0:T(8,128)(2,1)S(1)}) custom-call(bf16[16,96,128]{2,1,0:T(8,128)(2,1)S(1)} %all-to-all-done.in_ref, bf16[512,128]{1,0:T(8,128)(2,1)S(1)} %get-tuple-element.19.bias_own_ref, ...), custom_call_target="tpu_custom_call" | custom-call | tf_op jit(solution)/shard_map/pallas_call | solution.py:385
  33.7 2.0 %collective-permute-start.5 = (bf16[16,32,128]{2,1,0:T(8,128)(2,1)S(1)}, bf16[16,32,128]{2,1,0:T(8,128)(2,1)S(1)}, u32[]{:S(2)}, u32[]{:S(2)}) collective-permute-start(bf16[16,32,128]{2,1,0:T(8,128)(2,1)S(1)} %get-tuple-element.25), channel_id=1, source_target_pairs={{0,1},{1,0},{2,3},{3,2},{4,5},{5,4},{6,7},{7,6},{8,9},{9,8},{10,11... | collective-permute-start | bytes 393224 | tf_op jit(solution)/shard_map/ppermute | solution.py:390
  35.8 1.5 %shard_map.86.low_ref = bf16[16,32,128]{2,1,0:T(8,128)(2,1)S(1)} custom-call(bf16[16,96,128]{2,1,0:T(8,128)(2,1)S(1)} %all-to-all-done.in_ref, bf16[512,128]{1,0:T(8,128)(2,1)S(1)} %get-tuple-element.21.key_own_ref, bf16[512,128]{1,0:T(8,128)(2,1)S(1)} %get-tuple-element.22.key_peer_ref, bf16[1024,128]{1,0:T(8,128)(2,1)S(1)} %get-tuple-element.23.values_ref, ...), custom_call_target="tpu_custom_call" | custom-call | flops 20000000000 | tf_op jit(solution)/shard_map/pallas_call | solution.py:391
  37.2 0.0 collective-permute-done.5.high_ref
  37.3 12.9 %all_to_all.10.mixed_ref = bf16[16,32,128]{2,1,0:T(8,128)(2,1)S(1)} all-to-all(bf16[16,32,128]{2,1,0:T(8,128)(2,1)S(1)} %shard_map.87), channel_id=1, replica_groups={{8,10,12,14,0,2,4,6,24,26,28,30,16,18,20,22},{9,11,13,15,1,3,5,7,25,27,..., dimensions={0} | all-to-all | bytes 262144 | tf_op jit(solution)/shard_map/all_to_all | solution.py:395
  50.2 1.6 %shard_map.88 = f32[4,32,1024]{2,1,0:T(8,128)} custom-call(s32[32]{0:T(128)S(1)} %copy-done, f32[128,1024]{1,0:T(8,128)S(1)} %get-tuple-element.17.sum_ref, bf16[16,32,128]{2,1,0:T(8,128)(2,1)S(1)} %all_to_all.10.mixed_ref, bf16[512,1024]{1,0:T(8,128)(2,1)S(1)} %get-tuple-element.26.w_ref), custom_call_target="tpu_custom_call" | custom-call | tf_op jit(solution)/shard_map/pallas_call | solution.py:396
  (1 shorter events, 0.0 us)
Async XLA Ops:
  1.8 20.2 %copy-start = (s32[32]{0:T(128)S(1)}, s32[32]{0:T(128)}, u32[]{:S(2)}) copy-start(s32[32]{0:T(128)} %points_ref.3) | copy-start | bytes 388
  1.8 20.2 %copy-start.1 = (s32[8,4]{0,1:T(4,128)S(1)}, s32[8,4]{0,1:T(4,128)}, u32[]{:S(2)}) copy-start(s32[8,4]{0,1:T(4,128)} %param.10) | copy-start | bytes 388
  1.8 6.6 %collective-permute-start.4 = (bf16[128,1024]{1,0:T(8,128)(2,1)S(1)}, bf16[128,1024]{1,0:T(8,128)(2,1)S(1)}, u32[]{:S(2)}, u32[]{:S(2)}) collective-permute-start(bf16[128,1024]{1,0:T(8,128)(2,1)S(1)} %get-tuple-element.16.own_ref), channel_id=1, source_target_pairs={{0,1},{1,0},{2,3},{3,2},{4,5},{5,4},{6,7},{7,6},{8,9},{9,8},{10,11... | collective-permute-start | bytes 786440 | tf_op jit(solution)/shard_map/ppermute | solution.py:355
  5.1 16.8 %collective-permute-start.3 = (bf16[128,1024]{1,0:T(8,128)(2,1)S(1)}, bf16[128,1024]{1,0:T(8,128)(2,1)S(1)}, u32[]{:S(2)}, u32[]{:S(2)}) collective-permute-start(bf16[128,1024]{1,0:T(8,128)(2,1)S(1)} %get-tuple-element.16.own_ref), channel_id=1, source_target_pairs={{0,192},{32,224},{64,0},{96,32},{128,64},{160,96},{192,128},{224,1... | collective-permute-start | bytes 786440 | tf_op jit(solution)/shard_map/ppermute | solution.py:357
  5.9 16.1 %collective-permute-start.2 = (bf16[128,1024]{1,0:T(8,128)(2,1)S(1)}, bf16[128,1024]{1,0:T(8,128)(2,1)S(1)}, u32[]{:S(2)}, u32[]{:S(2)}) collective-permute-start(bf16[128,1024]{1,0:T(8,128)(2,1)S(1)} %get-tuple-element.16.own_ref), channel_id=1, source_target_pairs={{0,224},{32,0},{64,32},{96,64},{128,96},{160,128},{192,160},{224,1... | collective-permute-start | bytes 786440 | tf_op jit(solution)/shard_map/ppermute | solution.py:357
  7.5 14.5 %collective-permute-start.1 = (bf16[128,1024]{1,0:T(8,128)(2,1)S(1)}, bf16[128,1024]{1,0:T(8,128)(2,1)S(1)}, u32[]{:S(2)}, u32[]{:S(2)}) collective-permute-start(bf16[128,1024]{1,0:T(8,128)(2,1)S(1)} %get-tuple-element.16.own_ref), channel_id=1, source_target_pairs={{0,32},{32,64},{64,96},{96,128},{128,160},{160,192},{192,224},{224... | collective-permute-start | bytes 786440 | tf_op jit(solution)/shard_map/ppermute | solution.py:357
  7.5 14.5 %collective-permute-start = (bf16[128,1024]{1,0:T(8,128)(2,1)S(1)}, bf16[128,1024]{1,0:T(8,128)(2,1)S(1)}, u32[]{:S(2)}, u32[]{:S(2)}) collective-permute-start(bf16[128,1024]{1,0:T(8,128)(2,1)S(1)} %get-tuple-element.16.own_ref), channel_id=1, source_target_pairs={{0,64},{32,96},{64,128},{96,160},{128,192},{160,224},{192,0},{224,... | collective-permute-start | bytes 786440 | tf_op jit(solution)/shard_map/ppermute | solution.py:357
  9.8 22.5 %all-to-all-start = ((bf16[16,96,128]{2,1,0:T(8,128)(2,1)}), bf16[16,96,128]{2,1,0:T(8,128)(2,1)S(1)}, u32[]{:S(2)}, u32[]{:S(2)}) async-start(bf16[16,96,128]{2,1,0:T(8,128)(2,1)} %shard_map.84), calls=%async_computation | async-start | bytes 786432 | tf_op jit(solution)/shard_map/all_to_all | solution.py:369
  33.7 3.5 %collective-permute-start.5 = (bf16[16,32,128]{2,1,0:T(8,128)(2,1)S(1)}, bf16[16,32,128]{2,1,0:T(8,128)(2,1)S(1)}, u32[]{:S(2)}, u32[]{:S(2)}) collective-permute-start(bf16[16,32,128]{2,1,0:T(8,128)(2,1)S(1)} %get-tuple-element.25), channel_id=1, source_target_pairs={{0,1},{1,0},{2,3},{3,2},{4,5},{5,4},{6,7},{7,6},{8,9},{9,8},{10,11... | collective-permute-start | bytes 393224 | tf_op jit(solution)/shard_map/ppermute | solution.py:390

commit v8 on v7

--- a/solution.py
+++ b/solution.py
@@ -43,12 +43,12 @@
 
 def chip_order(chips):
     half = chips // 2
-    return [side * half + (z + half // 2) % half for side in range(2) for z in range(half)]
+    return [side * half + (z + half // 2) % half for side in (1, 0) for z in range(half)]
 
 
 def place_of(chip, chips):
     half = chips // 2
-    return chip // half * half + lax.rem(lax.rem(chip, half) + half // 2, half)
+    return (1 - chip // half) * half + lax.rem(lax.rem(chip, half) + half // 2, half)
 
 
 def live_count(points, tile, tiles):

time: 52 us -> 51.1 us (0.983)
  waiting for transfers between devices: 4.24 us -> 3.5 us
    ppermute x1, starting transfers between devices: 2.02 us -> 1.13 us  [on_device(): arrived = lax.ppermute(away, 'lon', swap)]
    all_to_all x1, waiting for transfers between devices: 4.23 us -> 3.48 us  [on_device(): lax.all_to_all(packed, 'lon', 0, 0, axis_index_groups=groups, tiled=True)]
where the time goes in v8:
time: 51.1 us; the launch traced here: 50.9 us
  starting transfers between devices  20.4 us (40%)
  Pallas kernels  13.7 us (27%)
  blocking collectives  13.1 us (26%)
  waiting for transfers between devices  3.5 us (7%)
    all_to_all x1, blocking collectives, on_device(): lax.all_to_all(joined, 'lon', 0, 0, axis_index_groups=groups, tiled=True)  13.1 us
    all_to_all x1, starting transfers between devices, on_device(): lax.all_to_all(packed, 'lon', 0, 0, axis_index_groups=groups, tiled=True)  12.7 us
    pallas_call x1, Pallas kernels, on_device(): call(functools.partial(band_kernel, lat_count, lon_count), [((tokens, wid...  5.97 us
    all_to_all x1, waiting for transfers between devices, on_device(): lax.all_to_all(packed, 'lon', 0, 0, axis_index_groups=groups, tiled=True)  3.48 us
    ppermute x1, starting transfers between devices, on_device(): peer = lax.ppermute(normed, 'lon', swap)  3.33 us
    ppermute x4, starting transfers between devices, on_device(): lax.ppermute(normed, 'lat', [(place, (place - offset) % lat_count) for pl...  3.24 us
    pallas_call x1, Pallas kernels, on_device(): call(norm_kernel, [((tokens, width), bf16), ((3, width, axial_width // 2)...  1.77 us
    pallas_call x1, Pallas kernels, on_device(): call(functools.partial(finish_kernel, lon_count), [((rows, slots, width),...  1.61 us
  transfers between devices with their start and end apart: 7, of which 1 were waited for; matrix products, arithmetic and copies ran while one was open for 0% of the time, Pallas kernels for 17%

profile of v8, /device:TPU:1, one launch (start us, length us, event | category | flops | bytes accessed | tf_op | source)
XLA Modules:
  0.0 50.9 jit_solution(5382641561887234036)
XLA Ops:
  0.0 1.8 %shard_map.82 = (bf16[128,1024]{1,0:T(8,128)(2,1)S(1)}, bf16[3,1024,256]{2,1,0:T(8,128)(2,1)S(1)}) custom-call(f32[4,32,1024]{2,1,0:T(8,128)} %fields_hbm.3, f32[1,1024]{1,0:T(1,128)} %bitcast.3, bf16[1024,1024]{1,0:T(8,128)(2,1)} %wq_hbm.3, bf16[1024,1024]{1,0:T(8,128)(2,1)} %wk_hbm.3, bf16[1024,1024]{1,0:T(8,128)(2,1)} %wv_hbm.3), custom_call_target="tpu_custom_call" | custom-call | tf_op jit(solution)/shard_map/pallas_call | solution.py:345
  1.8 0.0 copy-start
  1.8 0.0 copy-start.1
  1.8 3.3 %collective-permute-start.4 = (bf16[128,1024]{1,0:T(8,128)(2,1)S(1)}, bf16[128,1024]{1,0:T(8,128)(2,1)S(1)}, u32[]{:S(2)}, u32[]{:S(2)}) collective-permute-start(bf16[128,1024]{1,0:T(8,128)(2,1)S(1)} %get-tuple-element.16.own_ref), channel_id=1, source_target_pairs={{0,1},{1,0},{2,3},{3,2},{4,5},{5,4},{6,7},{7,6},{8,9},{9,8},{10,11... | collective-permute-start | bytes 786440 | tf_op jit(solution)/shard_map/ppermute | solution.py:355
  5.1 0.8 %collective-permute-start.3 = (bf16[128,1024]{1,0:T(8,128)(2,1)S(1)}, bf16[128,1024]{1,0:T(8,128)(2,1)S(1)}, u32[]{:S(2)}, u32[]{:S(2)}) collective-permute-start(bf16[128,1024]{1,0:T(8,128)(2,1)S(1)} %get-tuple-element.16.own_ref), channel_id=1, source_target_pairs={{0,192},{32,224},{64,0},{96,32},{128,64},{160,96},{192,128},{224,1... | collective-permute-start | bytes 786440 | tf_op jit(solution)/shard_map/ppermute | solution.py:357
  5.9 1.6 %collective-permute-start.2 = (bf16[128,1024]{1,0:T(8,128)(2,1)S(1)}, bf16[128,1024]{1,0:T(8,128)(2,1)S(1)}, u32[]{:S(2)}, u32[]{:S(2)}) collective-permute-start(bf16[128,1024]{1,0:T(8,128)(2,1)S(1)} %get-tuple-element.16.own_ref), channel_id=1, source_target_pairs={{0,224},{32,0},{64,32},{96,64},{128,96},{160,128},{192,160},{224,1... | collective-permute-start | bytes 786440 | tf_op jit(solution)/shard_map/ppermute | solution.py:357
  7.5 0.0 collective-permute-start.1
  7.5 0.9 %collective-permute-start = (bf16[128,1024]{1,0:T(8,128)(2,1)S(1)}, bf16[128,1024]{1,0:T(8,128)(2,1)S(1)}, u32[]{:S(2)}, u32[]{:S(2)}) collective-permute-start(bf16[128,1024]{1,0:T(8,128)(2,1)S(1)} %get-tuple-element.16.own_ref), channel_id=1, source_target_pairs={{0,64},{32,96},{64,128},{96,160},{128,192},{160,224},{192,0},{224,... | collective-permute-start | bytes 786440 | tf_op jit(solution)/shard_map/ppermute | solution.py:357
  8.4 0.0 collective-permute-done.4.peer_ref
  8.4 1.4 %shard_map.84 = bf16[16,96,128]{2,1,0:T(8,128)(2,1)} custom-call(bf16[128,1024]{1,0:T(8,128)(2,1)S(1)} %get-tuple-element.16.own_ref, bf16[128,1024]{1,0:T(8,128)(2,1)S(1)} %collective-permute-done.4.peer_ref, bf16[3,1024,256]{2,1,0:T(8,128)(2,1)S(1)} %get-tuple-element.18.weights_ref), custom_call_target="tpu_custom_call" | custom-call | tf_op jit(solution)/shard_map/pallas_call | solution.py:362
  9.8 12.7 %all-to-all-start = ((bf16[16,96,128]{2,1,0:T(8,128)(2,1)}), bf16[16,96,128]{2,1,0:T(8,128)(2,1)S(1)}, u32[]{:S(2)}, u32[]{:S(2)}) async-start(bf16[16,96,128]{2,1,0:T(8,128)(2,1)} %shard_map.84), calls=%async_computation | async-start | bytes 786432 | tf_op jit(solution)/shard_map/all_to_all | solution.py:369
  22.4 0.0 collective-permute-done.3.p2_ref
  22.4 0.0 collective-permute-done.2.p1_ref
  22.5 0.0 collective-permute-done.1.m1_ref
  22.5 0.0 collective-permute-done.m2_ref
  22.5 0.0 copy-done
  22.5 0.0 copy-done.1
  22.5 6.0 %shard_map.83 = (f32[128,1024]{1,0:T(8,128)S(1)}, bf16[512,1024]{1,0:T(8,128)(2,1)S(1)}, bf16[512,128]{1,0:T(8,128)(2,1)S(1)}, bf16[512,128]{1,0:T(8,128)(2,1)S(1)}) custom-call(s32[32]{0:T(128)S(1)} %copy-done, s32[4,8]{1,0:T(4,128)S(1)} %bitcast.2, bf16[128,1024]{1,0:T(8,128)(2,1)S(1)} %get-tuple-element.16.own_ref, ...), custom_call_target="tpu_custom_call" | custom-call | flops 20000000000 | tf_op jit(solution)/shard_map/pallas_call | solution.py:371
  28.5 3.5 %all-to-all-done.in_ref = bf16[16,96,128]{2,1,0:T(8,128)(2,1)S(1)} async-done(((bf16[16,96,128]{2,1,0:T(8,128)(2,1)}), bf16[16,96,128]{2,1,0:T(8,128)(2,1)S(1)}, u32[]{:S(2)}, u32[]{:S(2)}) %all-to-all-start) | async-done | bytes 393248 | tf_op jit(solution)/shard_map/all_to_all | solution.py:369
  31.9 1.5 %shard_map.85 = (bf16[16,32,128]{2,1,0:T(8,128)(2,1)S(1)}, bf16[512,128]{1,0:T(8,128)(2,1)S(1)}, bf16[512,128]{1,0:T(8,128)(2,1)S(1)}, bf16[1024,128]{1,0:T(8,128)(2,1)S(1)}, bf16[512,128]{1,0:T(8,128)(2,1)S(1)}) custom-call(bf16[16,96,128]{2,1,0:T(8,128)(2,1)S(1)} %all-to-all-done.in_ref, bf16[512,128]{1,0:T(8,128)(2,1)S(1)} %get-tuple-element.19.bias_own_ref, ...), custom_call_target="tpu_custom_call" | custom-call | tf_op jit(solution)/shard_map/pallas_call | solution.py:385
  33.5 1.1 %collective-permute-start.5 = (bf16[16,32,128]{2,1,0:T(8,128)(2,1)S(1)}, bf16[16,32,128]{2,1,0:T(8,128)(2,1)S(1)}, u32[]{:S(2)}, u32[]{:S(2)}) collective-permute-start(bf16[16,32,128]{2,1,0:T(8,128)(2,1)S(1)} %get-tuple-element.25), channel_id=1, source_target_pairs={{0,1},{1,0},{2,3},{3,2},{4,5},{5,4},{6,7},{7,6},{8,9},{9,8},{10,11... | collective-permute-start | bytes 393224 | tf_op jit(solution)/shard_map/ppermute | solution.py:390
  34.6 1.5 %shard_map.86.low_ref = bf16[16,32,128]{2,1,0:T(8,128)(2,1)S(1)} custom-call(bf16[16,96,128]{2,1,0:T(8,128)(2,1)S(1)} %all-to-all-done.in_ref, bf16[512,128]{1,0:T(8,128)(2,1)S(1)} %get-tuple-element.21.key_own_ref, bf16[512,128]{1,0:T(8,128)(2,1)S(1)} %get-tuple-element.22.key_peer_ref, bf16[1024,128]{1,0:T(8,128)(2,1)S(1)} %get-tuple-element.23.values_ref, ...), custom_call_target="tpu_custom_call" | custom-call | flops 20000000000 | tf_op jit(solution)/shard_map/pallas_call | solution.py:391
  36.1 0.0 collective-permute-done.5.high_ref
  36.1 13.1 %all_to_all.10.mixed_ref = bf16[16,32,128]{2,1,0:T(8,128)(2,1)S(1)} all-to-all(bf16[16,32,128]{2,1,0:T(8,128)(2,1)S(1)} %shard_map.87), channel_id=1, replica_groups={{24,26,28,30,16,18,20,22,8,10,12,14,0,2,4,6},{25,27,29,31,17,19,21,23,9..., dimensions={0} | all-to-all | bytes 262144 | tf_op jit(solution)/shard_map/all_to_all | solution.py:395
  49.2 1.6 %shard_map.88 = f32[4,32,1024]{2,1,0:T(8,128)} custom-call(s32[32]{0:T(128)S(1)} %copy-done, f32[128,1024]{1,0:T(8,128)S(1)} %get-tuple-element.17.sum_ref, bf16[16,32,128]{2,1,0:T(8,128)(2,1)S(1)} %all_to_all.10.mixed_ref, bf16[512,1024]{1,0:T(8,128)(2,1)S(1)} %get-tuple-element.26.w_ref), custom_call_target="tpu_custom_call" | custom-call | tf_op jit(solution)/shard_map/pallas_call | solution.py:396
  (1 shorter events, 0.0 us)
Async XLA Ops:
  1.8 20.7 %copy-start = (s32[32]{0:T(128)S(1)}, s32[32]{0:T(128)}, u32[]{:S(2)}) copy-start(s32[32]{0:T(128)} %points_ref.3) | copy-start | bytes 388
  1.8 20.7 %copy-start.1 = (s32[8,4]{0,1:T(4,128)S(1)}, s32[8,4]{0,1:T(4,128)}, u32[]{:S(2)}) copy-start(s32[8,4]{0,1:T(4,128)} %param.10) | copy-start | bytes 388
  1.8 6.6 %collective-permute-start.4 = (bf16[128,1024]{1,0:T(8,128)(2,1)S(1)}, bf16[128,1024]{1,0:T(8,128)(2,1)S(1)}, u32[]{:S(2)}, u32[]{:S(2)}) collective-permute-start(bf16[128,1024]{1,0:T(8,128)(2,1)S(1)} %get-tuple-element.16.own_ref), channel_id=1, source_target_pairs={{0,1},{1,0},{2,3},{3,2},{4,5},{5,4},{6,7},{7,6},{8,9},{9,8},{10,11... | collective-permute-start | bytes 786440 | tf_op jit(solution)/shard_map/ppermute | solution.py:355
  5.1 17.3 %collective-permute-start.3 = (bf16[128,1024]{1,0:T(8,128)(2,1)S(1)}, bf16[128,1024]{1,0:T(8,128)(2,1)S(1)}, u32[]{:S(2)}, u32[]{:S(2)}) collective-permute-start(bf16[128,1024]{1,0:T(8,128)(2,1)S(1)} %get-tuple-element.16.own_ref), channel_id=1, source_target_pairs={{0,192},{32,224},{64,0},{96,32},{128,64},{160,96},{192,128},{224,1... | collective-permute-start | bytes 786440 | tf_op jit(solution)/shard_map/ppermute | solution.py:357
  5.9 16.6 %collective-permute-start.2 = (bf16[128,1024]{1,0:T(8,128)(2,1)S(1)}, bf16[128,1024]{1,0:T(8,128)(2,1)S(1)}, u32[]{:S(2)}, u32[]{:S(2)}) collective-permute-start(bf16[128,1024]{1,0:T(8,128)(2,1)S(1)} %get-tuple-element.16.own_ref), channel_id=1, source_target_pairs={{0,224},{32,0},{64,32},{96,64},{128,96},{160,128},{192,160},{224,1... | collective-permute-start | bytes 786440 | tf_op jit(solution)/shard_map/ppermute | solution.py:357
  7.5 15.0 %collective-permute-start.1 = (bf16[128,1024]{1,0:T(8,128)(2,1)S(1)}, bf16[128,1024]{1,0:T(8,128)(2,1)S(1)}, u32[]{:S(2)}, u32[]{:S(2)}) collective-permute-start(bf16[128,1024]{1,0:T(8,128)(2,1)S(1)} %get-tuple-element.16.own_ref), channel_id=1, source_target_pairs={{0,32},{32,64},{64,96},{96,128},{128,160},{160,192},{192,224},{224... | collective-permute-start | bytes 786440 | tf_op jit(solution)/shard_map/ppermute | solution.py:357
  7.5 15.0 %collective-permute-start = (bf16[128,1024]{1,0:T(8,128)(2,1)S(1)}, bf16[128,1024]{1,0:T(8,128)(2,1)S(1)}, u32[]{:S(2)}, u32[]{:S(2)}) collective-permute-start(bf16[128,1024]{1,0:T(8,128)(2,1)S(1)} %get-tuple-element.16.own_ref), channel_id=1, source_target_pairs={{0,64},{32,96},{64,128},{96,160},{128,192},{160,224},{192,0},{224,... | collective-permute-start | bytes 786440 | tf_op jit(solution)/shard_map/ppermute | solution.py:357
  9.8 22.2 %all-to-all-start = ((bf16[16,96,128]{2,1,0:T(8,128)(2,1)}), bf16[16,96,128]{2,1,0:T(8,128)(2,1)S(1)}, u32[]{:S(2)}, u32[]{:S(2)}) async-start(bf16[16,96,128]{2,1,0:T(8,128)(2,1)} %shard_map.84), calls=%async_computation | async-start | bytes 786432 | tf_op jit(solution)/shard_map/all_to_all | solution.py:369
  33.5 2.6 %collective-permute-start.5 = (bf16[16,32,128]{2,1,0:T(8,128)(2,1)S(1)}, bf16[16,32,128]{2,1,0:T(8,128)(2,1)S(1)}, u32[]{:S(2)}, u32[]{:S(2)}) collective-permute-start(bf16[16,32,128]{2,1,0:T(8,128)(2,1)S(1)} %get-tuple-element.25), channel_id=1, source_target_pairs={{0,1},{1,0},{2,3},{3,2},{4,5},{5,4},{6,7},{7,6},{8,9},{9,8},{10,11... | collective-permute-start | bytes 393224 | tf_op jit(solution)/shard_map/ppermute | solution.py:390

commit v9 on v8

--- a/solution.py
+++ b/solution.py
@@ -15,7 +15,7 @@
 DEAD = -1e30
 PAIR = 2 * HEAD_DIM
 SCALE = HEAD_DIM**-0.5
-OFFSETS = (-2, -1, 1, 2)
+OFFSETS = (-1, 1, -2, 2)
 AXIAL_FLOPS = 20_000_000_000
 BAND_FLOPS = 20_000_000_000
 
@@ -187,7 +187,7 @@
 
 
 def band_kernel(
-    lat_count, lon_count, points_ref, mask_ref, own_ref, m2_ref, m1_ref, p1_ref, p2_ref,
+    lat_count, lon_count, points_ref, mask_ref, own_ref, below_ref, above_ref, below2_ref, above2_ref,
     wq_hbm, wk_hbm, wv_hbm, fields_hbm, w_hbm,
     out_ref, axial_w_ref, bias_own_ref, bias_peer_ref,
     weights_ref, fields_ref, w_ref, band_ref, sems,
@@ -223,7 +223,7 @@
     rows = tokens // slots
     bf16 = jnp.bfloat16
     own = own_ref[...]
-    everything = jnp.concatenate([own, m2_ref[...], m1_ref[...], p1_ref[...], p2_ref[...]], axis=0)
+    everything = jnp.concatenate([own, below_ref[...], above_ref[...], below2_ref[...], above2_ref[...]], axis=0)
     keys = everything.shape[0]
     slot = lax.broadcasted_iota(jnp.int32, (slots, PAIR), 0)
     blocks = []

time: 51.1 us -> 52.3 us (1.023)
  starting transfers between devices: 20.4 us -> 21.6 us
    ppermute x4, starting transfers between devices: 3.24 us -> 4.45 us  [on_device(): lax.ppermute(normed, 'lat', [(place, (place - offset) % lat_count) for pl...]
where the time goes in v9:
time: 52.3 us; the launch traced here: 52.1 us
  starting transfers between devices  21.6 us (41%)
  Pallas kernels  13.7 us (26%)
  blocking collectives  13.2 us (25%)
  waiting for transfers between devices  3.5 us (7%)
    all_to_all x1, blocking collectives, on_device(): lax.all_to_all(joined, 'lon', 0, 0, axis_index_groups=groups, tiled=True)  13.2 us
    all_to_all x1, starting transfers between devices, on_device(): lax.all_to_all(packed, 'lon', 0, 0, axis_index_groups=groups, tiled=True)  12.7 us
    pallas_call x1, Pallas kernels, on_device(): call(functools.partial(band_kernel, lat_count, lon_count), [((tokens, wid...  5.96 us
    ppermute x4, starting transfers between devices, on_device(): lax.ppermute(normed, 'lat', [(place, (place - offset) % lat_count) for pl...  4.45 us
    all_to_all x1, waiting for transfers between devices, on_device(): lax.all_to_all(packed, 'lon', 0, 0, axis_index_groups=groups, tiled=True)  3.49 us
    ppermute x1, starting transfers between devices, on_device(): peer = lax.ppermute(normed, 'lon', swap)  3.33 us
    pallas_call x1, Pallas kernels, on_device(): call(norm_kernel, [((tokens, width), bf16), ((3, width, axial_width // 2)...  1.77 us
    pallas_call x1, Pallas kernels, on_device(): call(functools.partial(finish_kernel, lon_count), [((rows, slots, width),...  1.61 us
  transfers between devices with their start and end apart: 7, of which 1 were waited for; matrix products, arithmetic and copies ran while one was open for 0% of the time, Pallas kernels for 17%

profile of v9, /device:TPU:1, one launch (start us, length us, event | category | flops | bytes accessed | tf_op | source)
XLA Modules:
  0.0 52.1 jit_solution(17752768851430237251)
XLA Ops:
  0.0 1.8 %shard_map.82 = (bf16[128,1024]{1,0:T(8,128)(2,1)S(1)}, bf16[3,1024,256]{2,1,0:T(8,128)(2,1)S(1)}) custom-call(f32[4,32,1024]{2,1,0:T(8,128)} %fields_hbm.3, f32[1,1024]{1,0:T(1,128)} %bitcast.3, bf16[1024,1024]{1,0:T(8,128)(2,1)} %wq_hbm.3, bf16[1024,1024]{1,0:T(8,128)(2,1)} %wk_hbm.3, bf16[1024,1024]{1,0:T(8,128)(2,1)} %wv_hbm.3), custom_call_target="tpu_custom_call" | custom-call | tf_op jit(solution)/shard_map/pallas_call | solution.py:345
  1.8 0.0 copy-start
  1.8 0.0 copy-start.1
  1.8 3.3 %collective-permute-start.4 = (bf16[128,1024]{1,0:T(8,128)(2,1)S(1)}, bf16[128,1024]{1,0:T(8,128)(2,1)S(1)}, u32[]{:S(2)}, u32[]{:S(2)}) collective-permute-start(bf16[128,1024]{1,0:T(8,128)(2,1)S(1)} %get-tuple-element.16.own_ref), channel_id=1, source_target_pairs={{0,1},{1,0},{2,3},{3,2},{4,5},{5,4},{6,7},{7,6},{8,9},{9,8},{10,11... | collective-permute-start | bytes 786440 | tf_op jit(solution)/shard_map/ppermute | solution.py:355
  5.1 0.8 %collective-permute-start.3 = (bf16[128,1024]{1,0:T(8,128)(2,1)S(1)}, bf16[128,1024]{1,0:T(8,128)(2,1)S(1)}, u32[]{:S(2)}, u32[]{:S(2)}) collective-permute-start(bf16[128,1024]{1,0:T(8,128)(2,1)S(1)} %get-tuple-element.16.own_ref), channel_id=1, source_target_pairs={{0,192},{32,224},{64,0},{96,32},{128,64},{160,96},{192,128},{224,1... | collective-permute-start | bytes 786440 | tf_op jit(solution)/shard_map/ppermute | solution.py:357
  5.9 0.7 %collective-permute-start.2 = (bf16[128,1024]{1,0:T(8,128)(2,1)S(1)}, bf16[128,1024]{1,0:T(8,128)(2,1)S(1)}, u32[]{:S(2)}, u32[]{:S(2)}) collective-permute-start(bf16[128,1024]{1,0:T(8,128)(2,1)S(1)} %get-tuple-element.16.own_ref), channel_id=1, source_target_pairs={{0,64},{32,96},{64,128},{96,160},{128,192},{160,224},{192,0},{224,... | collective-permute-start | bytes 786440 | tf_op jit(solution)/shard_map/ppermute | solution.py:357
  6.6 3.0 %collective-permute-start.1 = (bf16[128,1024]{1,0:T(8,128)(2,1)S(1)}, bf16[128,1024]{1,0:T(8,128)(2,1)S(1)}, u32[]{:S(2)}, u32[]{:S(2)}) collective-permute-start(bf16[128,1024]{1,0:T(8,128)(2,1)S(1)} %get-tuple-element.16.own_ref), channel_id=1, source_target_pairs={{0,224},{32,0},{64,32},{96,64},{128,96},{160,128},{192,160},{224,1... | collective-permute-start | bytes 786440 | tf_op jit(solution)/shard_map/ppermute | solution.py:357
  9.6 0.0 collective-permute-start
  9.6 0.0 collective-permute-done.4.peer_ref
  9.6 1.4 %shard_map.84 = bf16[16,96,128]{2,1,0:T(8,128)(2,1)} custom-call(bf16[128,1024]{1,0:T(8,128)(2,1)S(1)} %get-tuple-element.16.own_ref, bf16[128,1024]{1,0:T(8,128)(2,1)S(1)} %collective-permute-done.4.peer_ref, bf16[3,1024,256]{2,1,0:T(8,128)(2,1)S(1)} %get-tuple-element.18.weights_ref), custom_call_target="tpu_custom_call" | custom-call | tf_op jit(solution)/shard_map/pallas_call | solution.py:362
  11.0 12.7 %all-to-all-start = ((bf16[16,96,128]{2,1,0:T(8,128)(2,1)}), bf16[16,96,128]{2,1,0:T(8,128)(2,1)S(1)}, u32[]{:S(2)}, u32[]{:S(2)}) async-start(bf16[16,96,128]{2,1,0:T(8,128)(2,1)} %shard_map.84), calls=%async_computation | async-start | bytes 786432 | tf_op jit(solution)/shard_map/all_to_all | solution.py:369
  23.6 0.0 collective-permute-done.3.above2_ref
  23.7 0.0 collective-permute-done.2.below2_ref
  23.7 0.0 collective-permute-done.1.above_ref
  23.7 0.0 collective-permute-done.below_ref
  23.7 0.0 copy-done
  23.7 0.0 copy-done.1
  23.7 6.0 %shard_map.83 = (f32[128,1024]{1,0:T(8,128)S(1)}, bf16[512,1024]{1,0:T(8,128)(2,1)S(1)}, bf16[512,128]{1,0:T(8,128)(2,1)S(1)}, bf16[512,128]{1,0:T(8,128)(2,1)S(1)}) custom-call(s32[32]{0:T(128)S(1)} %copy-done, s32[4,8]{1,0:T(4,128)S(1)} %bitcast.2, bf16[128,1024]{1,0:T(8,128)(2,1)S(1)} %get-tuple-element.16.own_ref, ...), custom_call_target="tpu_custom_call" | custom-call | flops 20000000000 | tf_op jit(solution)/shard_map/pallas_call | solution.py:371
  29.7 3.5 %all-to-all-done.in_ref = bf16[16,96,128]{2,1,0:T(8,128)(2,1)S(1)} async-done(((bf16[16,96,128]{2,1,0:T(8,128)(2,1)}), bf16[16,96,128]{2,1,0:T(8,128)(2,1)S(1)}, u32[]{:S(2)}, u32[]{:S(2)}) %all-to-all-start) | async-done | bytes 393248 | tf_op jit(solution)/shard_map/all_to_all | solution.py:369
  33.2 1.5 %shard_map.85 = (bf16[16,32,128]{2,1,0:T(8,128)(2,1)S(1)}, bf16[512,128]{1,0:T(8,128)(2,1)S(1)}, bf16[512,128]{1,0:T(8,128)(2,1)S(1)}, bf16[1024,128]{1,0:T(8,128)(2,1)S(1)}, bf16[512,128]{1,0:T(8,128)(2,1)S(1)}) custom-call(bf16[16,96,128]{2,1,0:T(8,128)(2,1)S(1)} %all-to-all-done.in_ref, bf16[512,128]{1,0:T(8,128)(2,1)S(1)} %get-tuple-element.19.bias_own_ref, ...), custom_call_target="tpu_custom_call" | custom-call | tf_op jit(solution)/shard_map/pallas_call | solution.py:385
  34.7 1.1 %collective-permute-start.5 = (bf16[16,32,128]{2,1,0:T(8,128)(2,1)S(1)}, bf16[16,32,128]{2,1,0:T(8,128)(2,1)S(1)}, u32[]{:S(2)}, u32[]{:S(2)}) collective-permute-start(bf16[16,32,128]{2,1,0:T(8,128)(2,1)S(1)} %get-tuple-element.25), channel_id=1, source_target_pairs={{0,1},{1,0},{2,3},{3,2},{4,5},{5,4},{6,7},{7,6},{8,9},{9,8},{10,11... | collective-permute-start | bytes 393224 | tf_op jit(solution)/shard_map/ppermute | solution.py:390
  35.8 1.5 %shard_map.86.low_ref = bf16[16,32,128]{2,1,0:T(8,128)(2,1)S(1)} custom-call(bf16[16,96,128]{2,1,0:T(8,128)(2,1)S(1)} %all-to-all-done.in_ref, bf16[512,128]{1,0:T(8,128)(2,1)S(1)} %get-tuple-element.21.key_own_ref, bf16[512,128]{1,0:T(8,128)(2,1)S(1)} %get-tuple-element.22.key_peer_ref, bf16[1024,128]{1,0:T(8,128)(2,1)S(1)} %get-tuple-element.23.values_ref, ...), custom_call_target="tpu_custom_call" | custom-call | flops 20000000000 | tf_op jit(solution)/shard_map/pallas_call | solution.py:391
  37.3 0.0 collective-permute-done.5.high_ref
  37.3 13.2 %all_to_all.10.mixed_ref = bf16[16,32,128]{2,1,0:T(8,128)(2,1)S(1)} all-to-all(bf16[16,32,128]{2,1,0:T(8,128)(2,1)S(1)} %shard_map.87), channel_id=1, replica_groups={{24,26,28,30,16,18,20,22,8,10,12,14,0,2,4,6},{25,27,29,31,17,19,21,23,9..., dimensions={0} | all-to-all | bytes 262144 | tf_op jit(solution)/shard_map/all_to_all | solution.py:395
  50.5 1.6 %shard_map.88 = f32[4,32,1024]{2,1,0:T(8,128)} custom-call(s32[32]{0:T(128)S(1)} %copy-done, f32[128,1024]{1,0:T(8,128)S(1)} %get-tuple-element.17.sum_ref, bf16[16,32,128]{2,1,0:T(8,128)(2,1)S(1)} %all_to_all.10.mixed_ref, bf16[512,1024]{1,0:T(8,128)(2,1)S(1)} %get-tuple-element.26.w_ref), custom_call_target="tpu_custom_call" | custom-call | tf_op jit(solution)/shard_map/pallas_call | solution.py:396
  (1 shorter events, 0.0 us)
Async XLA Ops:
  1.8 21.9 %copy-start = (s32[32]{0:T(128)S(1)}, s32[32]{0:T(128)}, u32[]{:S(2)}) copy-start(s32[32]{0:T(128)} %points_ref.3) | copy-start | bytes 388
  1.8 21.9 %copy-start.1 = (s32[8,4]{0,1:T(4,128)S(1)}, s32[8,4]{0,1:T(4,128)}, u32[]{:S(2)}) copy-start(s32[8,4]{0,1:T(4,128)} %param.10) | copy-start | bytes 388
  1.8 7.8 %collective-permute-start.4 = (bf16[128,1024]{1,0:T(8,128)(2,1)S(1)}, bf16[128,1024]{1,0:T(8,128)(2,1)S(1)}, u32[]{:S(2)}, u32[]{:S(2)}) collective-permute-start(bf16[128,1024]{1,0:T(8,128)(2,1)S(1)} %get-tuple-element.16.own_ref), channel_id=1, source_target_pairs={{0,1},{1,0},{2,3},{3,2},{4,5},{5,4},{6,7},{7,6},{8,9},{9,8},{10,11... | collective-permute-start | bytes 786440 | tf_op jit(solution)/shard_map/ppermute | solution.py:355
  5.1 18.5 %collective-permute-start.3 = (bf16[128,1024]{1,0:T(8,128)(2,1)S(1)}, bf16[128,1024]{1,0:T(8,128)(2,1)S(1)}, u32[]{:S(2)}, u32[]{:S(2)}) collective-permute-start(bf16[128,1024]{1,0:T(8,128)(2,1)S(1)} %get-tuple-element.16.own_ref), channel_id=1, source_target_pairs={{0,192},{32,224},{64,0},{96,32},{128,64},{160,96},{192,128},{224,1... | collective-permute-start | bytes 786440 | tf_op jit(solution)/shard_map/ppermute | solution.py:357
  5.9 17.8 %collective-permute-start.2 = (bf16[128,1024]{1,0:T(8,128)(2,1)S(1)}, bf16[128,1024]{1,0:T(8,128)(2,1)S(1)}, u32[]{:S(2)}, u32[]{:S(2)}) collective-permute-start(bf16[128,1024]{1,0:T(8,128)(2,1)S(1)} %get-tuple-element.16.own_ref), channel_id=1, source_target_pairs={{0,64},{32,96},{64,128},{96,160},{128,192},{160,224},{192,0},{224,... | collective-permute-start | bytes 786440 | tf_op jit(solution)/shard_map/ppermute | solution.py:357
  6.6 17.0 %collective-permute-start.1 = (bf16[128,1024]{1,0:T(8,128)(2,1)S(1)}, bf16[128,1024]{1,0:T(8,128)(2,1)S(1)}, u32[]{:S(2)}, u32[]{:S(2)}) collective-permute-start(bf16[128,1024]{1,0:T(8,128)(2,1)S(1)} %get-tuple-element.16.own_ref), channel_id=1, source_target_pairs={{0,224},{32,0},{64,32},{96,64},{128,96},{160,128},{192,160},{224,1... | collective-permute-start | bytes 786440 | tf_op jit(solution)/shard_map/ppermute | solution.py:357
  9.6 14.1 %collective-permute-start = (bf16[128,1024]{1,0:T(8,128)(2,1)S(1)}, bf16[128,1024]{1,0:T(8,128)(2,1)S(1)}, u32[]{:S(2)}, u32[]{:S(2)}) collective-permute-start(bf16[128,1024]{1,0:T(8,128)(2,1)S(1)} %get-tuple-element.16.own_ref), channel_id=1, source_target_pairs={{0,32},{32,64},{64,96},{96,128},{128,160},{160,192},{192,224},{224... | collective-permute-start | bytes 786440 | tf_op jit(solution)/shard_map/ppermute | solution.py:357
  11.0 22.2 %all-to-all-start = ((bf16[16,96,128]{2,1,0:T(8,128)(2,1)}), bf16[16,96,128]{2,1,0:T(8,128)(2,1)S(1)}, u32[]{:S(2)}, u32[]{:S(2)}) async-start(bf16[16,96,128]{2,1,0:T(8,128)(2,1)} %shard_map.84), calls=%async_computation | async-start | bytes 786432 | tf_op jit(solution)/shard_map/all_to_all | solution.py:369
  34.7 2.6 %collective-permute-start.5 = (bf16[16,32,128]{2,1,0:T(8,128)(2,1)S(1)}, bf16[16,32,128]{2,1,0:T(8,128)(2,1)S(1)}, u32[]{:S(2)}, u32[]{:S(2)}) collective-permute-start(bf16[16,32,128]{2,1,0:T(8,128)(2,1)S(1)} %get-tuple-element.25), channel_id=1, source_target_pairs={{0,1},{1,0},{2,3},{3,2},{4,5},{5,4},{6,7},{7,6},{8,9},{9,8},{10,11... | collective-permute-start | bytes 393224 | tf_op jit(solution)/shard_map/ppermute | solution.py:390

commit v10 on v9

--- a/solution.py
+++ b/solution.py
@@ -15,7 +15,7 @@
 DEAD = -1e30
 PAIR = 2 * HEAD_DIM
 SCALE = HEAD_DIM**-0.5
-OFFSETS = (-1, 1, -2, 2)
+OFFSETS = (-1, -2, 2, 1)
 AXIAL_FLOPS = 20_000_000_000
 BAND_FLOPS = 20_000_000_000
 
@@ -187,7 +187,7 @@
 
 
 def band_kernel(
-    lat_count, lon_count, points_ref, mask_ref, own_ref, below_ref, above_ref, below2_ref, above2_ref,
+    lat_count, lon_count, points_ref, mask_ref, own_ref, below_ref, below2_ref, above2_ref, above_ref,
     wq_hbm, wk_hbm, wv_hbm, fields_hbm, w_hbm,
     out_ref, axial_w_ref, bias_own_ref, bias_peer_ref,
     weights_ref, fields_ref, w_ref, band_ref, sems,
@@ -223,7 +223,7 @@
     rows = tokens // slots
     bf16 = jnp.bfloat16
     own = own_ref[...]
-    everything = jnp.concatenate([own, below_ref[...], above_ref[...], below2_ref[...], above2_ref[...]], axis=0)
+    everything = jnp.concatenate([own, below_ref[...], below2_ref[...], above2_ref[...], above_ref[...]], axis=0)
     keys = everything.shape[0]
     slot = lax.broadcasted_iota(jnp.int32, (slots, PAIR), 0)
     blocks = []

time: 52.3 us -> 52.1 us (level)
  starting transfers between devices: 21.6 us -> 20.4 us
  blocking collectives: 13.2 us -> 14.2 us
    ppermute x4, starting transfers between devices: 4.45 us -> 3.24 us  [on_device(): lax.ppermute(normed, 'lat', [(place, (place - offset) % lat_count) for pl...]
    all_to_all x1, blocking collectives: 13.2 us -> 14.2 us  [on_device(): lax.all_to_all(joined, 'lon', 0, 0, axis_index_groups=groups, tiled=True)]
where the time goes in v10:
time: 52.1 us; the launch traced here: 51.9 us
  starting transfers between devices  20.4 us (39%)
  blocking collectives  14.2 us (27%)
  Pallas kernels  13.7 us (26%)
  waiting for transfers between devices  3.5 us (7%)
    all_to_all x1, blocking collectives, on_device(): lax.all_to_all(joined, 'lon', 0, 0, axis_index_groups=groups, tiled=True)  14.2 us
    all_to_all x1, starting transfers between devices, on_device(): lax.all_to_all(packed, 'lon', 0, 0, axis_index_groups=groups, tiled=True)  12.7 us
    pallas_call x1, Pallas kernels, on_device(): call(functools.partial(band_kernel, lat_count, lon_count), [((tokens, wid...  5.96 us
    all_to_all x1, waiting for transfers between devices, on_device(): lax.all_to_all(packed, 'lon', 0, 0, axis_index_groups=groups, tiled=True)  3.49 us
    ppermute x1, starting transfers between devices, on_device(): peer = lax.ppermute(normed, 'lon', swap)  3.33 us
    ppermute x4, starting transfers between devices, on_device(): lax.ppermute(normed, 'lat', [(place, (place - offset) % lat_count) for pl...  3.24 us
    pallas_call x1, Pallas kernels, on_device(): call(norm_kernel, [((tokens, width), bf16), ((3, width, axial_width // 2)...  1.77 us
    pallas_call x1, Pallas kernels, on_device(): call(functools.partial(finish_kernel, lon_count), [((rows, slots, width),...  1.6 us
  transfers between devices with their start and end apart: 7, of which 1 were waited for; matrix products, arithmetic and copies ran while one was open for 0% of the time, Pallas kernels for 17%

profile of v10, /device:TPU:1, one launch (start us, length us, event | category | flops | bytes accessed | tf_op | source)
XLA Modules:
  0.0 51.9 jit_solution(8527893773005956599)
XLA Ops:
  0.0 1.8 %shard_map.82 = (bf16[128,1024]{1,0:T(8,128)(2,1)S(1)}, bf16[3,1024,256]{2,1,0:T(8,128)(2,1)S(1)}) custom-call(f32[4,32,1024]{2,1,0:T(8,128)} %fields_hbm.3, f32[1,1024]{1,0:T(1,128)} %bitcast.3, bf16[1024,1024]{1,0:T(8,128)(2,1)} %wq_hbm.3, bf16[1024,1024]{1,0:T(8,128)(2,1)} %wk_hbm.3, bf16[1024,1024]{1,0:T(8,128)(2,1)} %wv_hbm.3), custom_call_target="tpu_custom_call" | custom-call | tf_op jit(solution)/shard_map/pallas_call | solution.py:345
  1.8 0.0 copy-start
  1.8 0.0 copy-start.1
  1.8 3.3 %collective-permute-start.4 = (bf16[128,1024]{1,0:T(8,128)(2,1)S(1)}, bf16[128,1024]{1,0:T(8,128)(2,1)S(1)}, u32[]{:S(2)}, u32[]{:S(2)}) collective-permute-start(bf16[128,1024]{1,0:T(8,128)(2,1)S(1)} %get-tuple-element.16.own_ref), channel_id=1, source_target_pairs={{0,1},{1,0},{2,3},{3,2},{4,5},{5,4},{6,7},{7,6},{8,9},{9,8},{10,11... | collective-permute-start | bytes 786440 | tf_op jit(solution)/shard_map/ppermute | solution.py:355
  5.1 1.8 %collective-permute-start.3 = (bf16[128,1024]{1,0:T(8,128)(2,1)S(1)}, bf16[128,1024]{1,0:T(8,128)(2,1)S(1)}, u32[]{:S(2)}, u32[]{:S(2)}) collective-permute-start(bf16[128,1024]{1,0:T(8,128)(2,1)S(1)} %get-tuple-element.16.own_ref), channel_id=1, source_target_pairs={{0,224},{32,0},{64,32},{96,64},{128,96},{160,128},{192,160},{224,1... | collective-permute-start | bytes 786440 | tf_op jit(solution)/shard_map/ppermute | solution.py:357
  6.9 0.5 %collective-permute-start.2 = (bf16[128,1024]{1,0:T(8,128)(2,1)S(1)}, bf16[128,1024]{1,0:T(8,128)(2,1)S(1)}, u32[]{:S(2)}, u32[]{:S(2)}) collective-permute-start(bf16[128,1024]{1,0:T(8,128)(2,1)S(1)} %get-tuple-element.16.own_ref), channel_id=1, source_target_pairs={{0,192},{32,224},{64,0},{96,32},{128,64},{160,96},{192,128},{224,1... | collective-permute-start | bytes 786440 | tf_op jit(solution)/shard_map/ppermute | solution.py:357
  7.5 0.9 %collective-permute-start.1 = (bf16[128,1024]{1,0:T(8,128)(2,1)S(1)}, bf16[128,1024]{1,0:T(8,128)(2,1)S(1)}, u32[]{:S(2)}, u32[]{:S(2)}) collective-permute-start(bf16[128,1024]{1,0:T(8,128)(2,1)S(1)} %get-tuple-element.16.own_ref), channel_id=1, source_target_pairs={{0,64},{32,96},{64,128},{96,160},{128,192},{160,224},{192,0},{224,... | collective-permute-start | bytes 786440 | tf_op jit(solution)/shard_map/ppermute | solution.py:357
  8.4 0.0 collective-permute-start
  8.4 0.0 collective-permute-done.4.peer_ref
  8.4 1.4 %shard_map.84 = bf16[16,96,128]{2,1,0:T(8,128)(2,1)} custom-call(bf16[128,1024]{1,0:T(8,128)(2,1)S(1)} %get-tuple-element.16.own_ref, bf16[128,1024]{1,0:T(8,128)(2,1)S(1)} %collective-permute-done.4.peer_ref, bf16[3,1024,256]{2,1,0:T(8,128)(2,1)S(1)} %get-tuple-element.18.weights_ref), custom_call_target="tpu_custom_call" | custom-call | tf_op jit(solution)/shard_map/pallas_call | solution.py:362
  9.8 12.7 %all-to-all-start = ((bf16[16,96,128]{2,1,0:T(8,128)(2,1)}), bf16[16,96,128]{2,1,0:T(8,128)(2,1)S(1)}, u32[]{:S(2)}, u32[]{:S(2)}) async-start(bf16[16,96,128]{2,1,0:T(8,128)(2,1)} %shard_map.84), calls=%async_computation | async-start | bytes 786432 | tf_op jit(solution)/shard_map/all_to_all | solution.py:369
  22.4 0.0 collective-permute-done.3.above_ref
  22.4 0.0 collective-permute-done.2.above2_ref
  22.5 0.0 collective-permute-done.1.below2_ref
  22.5 0.0 collective-permute-done.below_ref
  22.5 0.0 copy-done
  22.5 0.0 copy-done.1
  22.5 6.0 %shard_map.83 = (f32[128,1024]{1,0:T(8,128)S(1)}, bf16[512,1024]{1,0:T(8,128)(2,1)S(1)}, bf16[512,128]{1,0:T(8,128)(2,1)S(1)}, bf16[512,128]{1,0:T(8,128)(2,1)S(1)}) custom-call(s32[32]{0:T(128)S(1)} %copy-done, s32[4,8]{1,0:T(4,128)S(1)} %bitcast.2, bf16[128,1024]{1,0:T(8,128)(2,1)S(1)} %get-tuple-element.16.own_ref, ...), custom_call_target="tpu_custom_call" | custom-call | flops 20000000000 | tf_op jit(solution)/shard_map/pallas_call | solution.py:371
  28.5 3.5 %all-to-all-done.in_ref = bf16[16,96,128]{2,1,0:T(8,128)(2,1)S(1)} async-done(((bf16[16,96,128]{2,1,0:T(8,128)(2,1)}), bf16[16,96,128]{2,1,0:T(8,128)(2,1)S(1)}, u32[]{:S(2)}, u32[]{:S(2)}) %all-to-all-start) | async-done | bytes 393248 | tf_op jit(solution)/shard_map/all_to_all | solution.py:369
  31.9 1.5 %shard_map.85 = (bf16[16,32,128]{2,1,0:T(8,128)(2,1)S(1)}, bf16[512,128]{1,0:T(8,128)(2,1)S(1)}, bf16[512,128]{1,0:T(8,128)(2,1)S(1)}, bf16[1024,128]{1,0:T(8,128)(2,1)S(1)}, bf16[512,128]{1,0:T(8,128)(2,1)S(1)}) custom-call(bf16[16,96,128]{2,1,0:T(8,128)(2,1)S(1)} %all-to-all-done.in_ref, bf16[512,128]{1,0:T(8,128)(2,1)S(1)} %get-tuple-element.19.bias_own_ref, ...), custom_call_target="tpu_custom_call" | custom-call | tf_op jit(solution)/shard_map/pallas_call | solution.py:385
  33.5 1.1 %collective-permute-start.5 = (bf16[16,32,128]{2,1,0:T(8,128)(2,1)S(1)}, bf16[16,32,128]{2,1,0:T(8,128)(2,1)S(1)}, u32[]{:S(2)}, u32[]{:S(2)}) collective-permute-start(bf16[16,32,128]{2,1,0:T(8,128)(2,1)S(1)} %get-tuple-element.25), channel_id=1, source_target_pairs={{0,1},{1,0},{2,3},{3,2},{4,5},{5,4},{6,7},{7,6},{8,9},{9,8},{10,11... | collective-permute-start | bytes 393224 | tf_op jit(solution)/shard_map/ppermute | solution.py:390
  34.6 1.5 %shard_map.86.low_ref = bf16[16,32,128]{2,1,0:T(8,128)(2,1)S(1)} custom-call(bf16[16,96,128]{2,1,0:T(8,128)(2,1)S(1)} %all-to-all-done.in_ref, bf16[512,128]{1,0:T(8,128)(2,1)S(1)} %get-tuple-element.21.key_own_ref, bf16[512,128]{1,0:T(8,128)(2,1)S(1)} %get-tuple-element.22.key_peer_ref, bf16[1024,128]{1,0:T(8,128)(2,1)S(1)} %get-tuple-element.23.values_ref, ...), custom_call_target="tpu_custom_call" | custom-call | flops 20000000000 | tf_op jit(solution)/shard_map/pallas_call | solution.py:391
  36.1 0.0 collective-permute-done.5.high_ref
  36.1 14.2 %all_to_all.10.mixed_ref = bf16[16,32,128]{2,1,0:T(8,128)(2,1)S(1)} all-to-all(bf16[16,32,128]{2,1,0:T(8,128)(2,1)S(1)} %shard_map.87), channel_id=1, replica_groups={{24,26,28,30,16,18,20,22,8,10,12,14,0,2,4,6},{25,27,29,31,17,19,21,23,9..., dimensions={0} | all-to-all | bytes 262144 | tf_op jit(solution)/shard_map/all_to_all | solution.py:395
  50.3 1.6 %shard_map.88 = f32[4,32,1024]{2,1,0:T(8,128)} custom-call(s32[32]{0:T(128)S(1)} %copy-done, f32[128,1024]{1,0:T(8,128)S(1)} %get-tuple-element.17.sum_ref, bf16[16,32,128]{2,1,0:T(8,128)(2,1)S(1)} %all_to_all.10.mixed_ref, bf16[512,1024]{1,0:T(8,128)(2,1)S(1)} %get-tuple-element.26.w_ref), custom_call_target="tpu_custom_call" | custom-call | tf_op jit(solution)/shard_map/pallas_call | solution.py:396
  (1 shorter events, 0.0 us)
Async XLA Ops:
  1.8 20.7 %copy-start = (s32[32]{0:T(128)S(1)}, s32[32]{0:T(128)}, u32[]{:S(2)}) copy-start(s32[32]{0:T(128)} %points_ref.3) | copy-start | bytes 388
  1.8 20.7 %copy-start.1 = (s32[8,4]{0,1:T(4,128)S(1)}, s32[8,4]{0,1:T(4,128)}, u32[]{:S(2)}) copy-start(s32[8,4]{0,1:T(4,128)} %param.10) | copy-start | bytes 388
  1.8 6.6 %collective-permute-start.4 = (bf16[128,1024]{1,0:T(8,128)(2,1)S(1)}, bf16[128,1024]{1,0:T(8,128)(2,1)S(1)}, u32[]{:S(2)}, u32[]{:S(2)}) collective-permute-start(bf16[128,1024]{1,0:T(8,128)(2,1)S(1)} %get-tuple-element.16.own_ref), channel_id=1, source_target_pairs={{0,1},{1,0},{2,3},{3,2},{4,5},{5,4},{6,7},{7,6},{8,9},{9,8},{10,11... | collective-permute-start | bytes 786440 | tf_op jit(solution)/shard_map/ppermute | solution.py:355
  5.1 17.3 %collective-permute-start.3 = (bf16[128,1024]{1,0:T(8,128)(2,1)S(1)}, bf16[128,1024]{1,0:T(8,128)(2,1)S(1)}, u32[]{:S(2)}, u32[]{:S(2)}) collective-permute-start(bf16[128,1024]{1,0:T(8,128)(2,1)S(1)} %get-tuple-element.16.own_ref), channel_id=1, source_target_pairs={{0,224},{32,0},{64,32},{96,64},{128,96},{160,128},{192,160},{224,1... | collective-permute-start | bytes 786440 | tf_op jit(solution)/shard_map/ppermute | solution.py:357
  6.9 15.5 %collective-permute-start.2 = (bf16[128,1024]{1,0:T(8,128)(2,1)S(1)}, bf16[128,1024]{1,0:T(8,128)(2,1)S(1)}, u32[]{:S(2)}, u32[]{:S(2)}) collective-permute-start(bf16[128,1024]{1,0:T(8,128)(2,1)S(1)} %get-tuple-element.16.own_ref), channel_id=1, source_target_pairs={{0,192},{32,224},{64,0},{96,32},{128,64},{160,96},{192,128},{224,1... | collective-permute-start | bytes 786440 | tf_op jit(solution)/shard_map/ppermute | solution.py:357
  7.5 15.0 %collective-permute-start.1 = (bf16[128,1024]{1,0:T(8,128)(2,1)S(1)}, bf16[128,1024]{1,0:T(8,128)(2,1)S(1)}, u32[]{:S(2)}, u32[]{:S(2)}) collective-permute-start(bf16[128,1024]{1,0:T(8,128)(2,1)S(1)} %get-tuple-element.16.own_ref), channel_id=1, source_target_pairs={{0,64},{32,96},{64,128},{96,160},{128,192},{160,224},{192,0},{224,... | collective-permute-start | bytes 786440 | tf_op jit(solution)/shard_map/ppermute | solution.py:357
  8.4 14.1 %collective-permute-start = (bf16[128,1024]{1,0:T(8,128)(2,1)S(1)}, bf16[128,1024]{1,0:T(8,128)(2,1)S(1)}, u32[]{:S(2)}, u32[]{:S(2)}) collective-permute-start(bf16[128,1024]{1,0:T(8,128)(2,1)S(1)} %get-tuple-element.16.own_ref), channel_id=1, source_target_pairs={{0,32},{32,64},{64,96},{96,128},{128,160},{160,192},{192,224},{224... | collective-permute-start | bytes 786440 | tf_op jit(solution)/shard_map/ppermute | solution.py:357
  9.8 22.2 %all-to-all-start = ((bf16[16,96,128]{2,1,0:T(8,128)(2,1)}), bf16[16,96,128]{2,1,0:T(8,128)(2,1)S(1)}, u32[]{:S(2)}, u32[]{:S(2)}) async-start(bf16[16,96,128]{2,1,0:T(8,128)(2,1)} %shard_map.84), calls=%async_computation | async-start | bytes 786432 | tf_op jit(solution)/shard_map/all_to_all | solution.py:369
  33.5 2.6 %collective-permute-start.5 = (bf16[16,32,128]{2,1,0:T(8,128)(2,1)S(1)}, bf16[16,32,128]{2,1,0:T(8,128)(2,1)S(1)}, u32[]{:S(2)}, u32[]{:S(2)}) collective-permute-start(bf16[16,32,128]{2,1,0:T(8,128)(2,1)S(1)} %get-tuple-element.25), channel_id=1, source_target_pairs={{0,1},{1,0},{2,3},{3,2},{4,5},{5,4},{6,7},{7,6},{8,9},{9,8},{10,11... | collective-permute-start | bytes 393224 | tf_op jit(solution)/shard_map/ppermute | solution.py:390
